TPU v7x, 32 devices: a whole 2x2x4 slice. The times are simulated.
32 devices in a mesh: grp: 4 (over z), slab: 8 (over y, x, core).
Axes of the slice: x: 2, y: 2, z: 4, core: 2. Of those that a mesh axis runs over, the one named last changes fastest.
Arguments:
- snapshots: bfloat16 [4, 128, 32, 8, 128], P('grp', None, 'slab'), may hold values from -24 to 24
- base_flow: float32 [32, 8, 128], P('slab'), may hold values from 0.1 to 0.6
Outputs:
- direct_modes: bfloat16 [128, 32, 8, 128], P('grp', 'slab')
- adjoint_modes: bfloat16 [128, 32, 8, 128], P('grp', 'slab')
All inputs are finite; a program needn't handle non-finite values.
Results may differ from a plain program's by a relative error of at most 0.015.
Values may be sent and summed in bfloat16 or wider, within the bound.
No kernel may reach another device: no remote copies, remote signals or barrier semaphores. Data moves between devices by JAX's collectives and lax.ppermute only.
A program may use at most 64 MiB of HBM per device.

v0:
```python
import math

import jax
import jax.numpy as jnp
from jax import lax
from jax.sharding import PartitionSpec as P

SNAP = 128
SECTIONS = 4


diffuse_x = 0.35
diffuse_side = 0.05
keep_center = 0.1
damping = 0.5


def with_halo(cells, sides, width):
    for axis, dim in sides:
        count = lax.axis_size(axis)
        head = lax.slice_in_dim(cells, 0, width, axis=dim)
        tail = lax.slice_in_dim(cells, cells.shape[dim] - width, cells.shape[dim], axis=dim)
        cells = jnp.concatenate(
            [
                lax.ppermute(tail, axis, [(i, (i + 1) % count) for i in range(count)]),
                cells,
                lax.ppermute(head, axis, [((i + 1) % count, i) for i in range(count)]),
            ],
            axis=dim,
        )
    return cells


def spread(value, axis, source):
    kept = jnp.where(lax.axis_index(axis) == source, value, 0).astype(value.dtype)
    return lax.psum(kept, axis)


def advance_section(extended, plus_coef, minus_coef):
    center = extended[:, 1:-1].astype(jnp.float32)
    ahead_cells = extended[:, 2:].astype(jnp.float32)
    behind = extended[:, :-2].astype(jnp.float32)
    side_sum = jnp.roll(center, 1, axis=2) + jnp.roll(center, -1, axis=2)
    side_sum = side_sum + jnp.roll(center, 1, axis=3) + jnp.roll(center, -1, axis=3)
    updated = (
        keep_center * center
        + plus_coef * ahead_cells
        + minus_coef * behind
        + diffuse_side * side_sum
    )
    return updated.astype(jnp.bfloat16)


def blockwise(sweep_block, extended):
    block_size = math.gcd(extended.shape[0], 64)
    blocks = extended.reshape((extended.shape[0] // block_size, block_size) + extended.shape[1:])
    result = lax.map(sweep_block, blocks)
    return result.reshape((extended.shape[0],) + result.shape[2:])


def per_device(snapshots, base_flow):
    snapshot_field = snapshots[0]
    groups = lax.axis_size("grp")
    group_index = lax.axis_index("grp")
    adjoint = group_index == groups - 1
    cell_rows = snapshot_field.shape[1]
    flow_ext = with_halo(base_flow, (("slab", 0),), SECTIONS)
    plus_coef = jnp.where(adjoint, diffuse_x + 0.5 * flow_ext[2:], diffuse_x - 0.5 * flow_ext[1:-1])
    minus_coef = jnp.where(
        adjoint, diffuse_x - 0.5 * flow_ext[:-2], diffuse_x + 0.5 * flow_ext[1:-1]
    )
    plus_inner = plus_coef[SECTIONS - 1 : SECTIONS - 1 + cell_rows]
    minus_inner = minus_coef[SECTIONS - 1 : SECTIONS - 1 + cell_rows]

    def single_section(snap_block):
        return advance_section(snap_block, plus_inner, minus_inner)

    for section_index in range(SECTIONS):
        extended = with_halo(snapshot_field, (("slab", 1),), 1)
        snapshot_field = blockwise(single_section, extended)
    adjoint_field = spread(snapshot_field, "grp", groups - 1)
    direct_flat = snapshot_field.reshape(SNAP, -1)
    adjoint_flat = adjoint_field.reshape(SNAP, -1)
    partial_value = lax.dot_general(
        adjoint_flat, direct_flat, (((1,), (1,)), ((), ())), preferred_element_type=jnp.float32
    )
    partial_value = jnp.where(adjoint, jnp.float32(0.0), partial_value)
    cell_count = (
        cell_rows * lax.axis_size("slab") * snapshot_field.shape[2] * snapshot_field.shape[3]
    )
    norm_scale = 1.0 / math.sqrt(cell_count)
    coupling = lax.psum(partial_value, "slab") * norm_scale
    own_gram = jnp.dot(coupling, coupling.T, precision=lax.Precision.HIGHEST)
    gram_matrix = lax.psum(own_gram.astype(jnp.bfloat16), "grp").astype(jnp.float32)
    energy = jnp.trace(gram_matrix) / SNAP
    system = gram_matrix / energy + damping * jnp.eye(SNAP, dtype=jnp.float32)
    factor = jnp.linalg.cholesky(system)
    inverse = jax.scipy.linalg.cho_solve((factor, True), jnp.eye(SNAP, dtype=jnp.float32))
    weights = (
        jnp.dot(inverse, coupling, precision=lax.Precision.HIGHEST) / jnp.sqrt(energy)
    ).astype(jnp.bfloat16)
    mode_share = SNAP // groups
    row_block = lax.slice_in_dim(weights, 0, mode_share * lax.axis_size("grp"), axis=0)
    summed_modes = lax.psum_scatter(
        jnp.dot(row_block, direct_flat, preferred_element_type=jnp.float32).astype(jnp.bfloat16),
        "grp",
        scatter_dimension=0,
        tiled=True,
    )
    direct_modes = summed_modes.reshape((mode_share,) + snapshot_field.shape[1:])
    inverse_rows = lax.dynamic_slice_in_dim(
        inverse.astype(jnp.bfloat16), group_index * mode_share, mode_share, 0
    )
    adjoint_modes = jnp.dot(inverse_rows, adjoint_flat, preferred_element_type=jnp.float32)
    adjoint_modes = adjoint_modes.astype(jnp.bfloat16).reshape(
        (mode_share,) + snapshot_field.shape[1:]
    )
    return (direct_modes, adjoint_modes)


def solution(mesh):
    return jax.shard_map(
        per_device,
        mesh=mesh,
        in_specs=(P("grp", None, "slab", None, None), P("slab", None, None)),
        out_specs=(P("grp", "slab", None, None), P("grp", "slab", None, None)),
        check_vma=False,
    )
```

profile of v0, /device:TPU:0, one launch (start us, length us, event | category | flops | bytes accessed | tf_op | source)
XLA Modules:
  0.0 261.6 jit_solution(14811955001155633427)
XLA Ops:
  7.7 2.9 %collective-permute-start.3 = (f32[4,8,128]{2,1,0:T(8,128)}, f32[4,8,128]{2,1,0:T(8,128)S(1)}, u32[]{:S(2)}, u32[]{:S(2)}) collective-permute-start(f32[4,8,128]{2,1,0:T(8,128)} %param.11), channel_id=1, source_target_pairs={{1,0},{2,1},{3,2},{4,3},{5,4},{6,5},{7,6},{0,7},{9,8},{10,9},{11,1... | collective-permute-start | bytes 49160 | tf_op jit(solution)/shard_map/ppermute | solution.py:27
  13.2 5.8 %collective-permute-done.1 = bf16[128,1,8,128]{3,2,1,0:T(8,128)(2,1)S(1)} collective-permute-done((bf16[128,1,8,128]{3,2,1,0:T(8,128)(2,1)S(1)}, bf16[128,1,8,128]{3,2,1,0:T(8,128)(2,1)S(1)}, u32[]{:S(2)}, u32[]{:S(2)}) %collective-permute-start.1) | collective-permute-done | bytes 262176 | tf_op jit(solution)/shard_map/ppermute | solution.py:27
  19.1 2.1 collective-permute-done
  21.6 5.8 %while.40 = (s32[]{:T(128)}, bf16[2,64,4,8,128]{4,3,2,1,0:T(8,128)(2,1)S(1)}, bf16[2,64,6,8,128]{4,3,2,1,0:T(8,128)(2,1)S(1)}, f32[4,8,128]{2,1,0:T(8,128)S(1)}, f32[4,8,128]{2,1,0:T(8,128)S(1)}, /*index=5*/s32[]{:T(128)}) while((s32[]{:T(128)}, bf16[2,64,4,8,128]{4,3,2,1,0:T(8,128)(2,1)S(1)}, bf16[2,64,6,8,128]{4,3,2,1,0:T(8,128)(2,1)S(1)}, ...), condition=%wide.region_1.2_spmd, body=%wide.region_0.1_spmd.sunk | while | flops 4980738 | bytes 20217932 | solution.py:57
  25.9 1.5 bitcast_dynamic-update-slice_fusion.8
  27.5 2.6 %collective-permute-start.5 = (bf16[128,1,8,128]{3,2,0,1:T(8,128)(2,1)S(1)}, bf16[128,1,8,128]{3,2,0,1:T(8,128)(2,1)S(1)}, u32[]{:S(2)}, u32[]{:S(2)}) collective-permute-start(bf16[128,1,8,128]{3,2,0,1:T(8,128)(2,1)S(1)} %get-tuple-element.191), channel_id=1, source_target_pairs={{1,0},{2,1},{3,2},{4,3},{5,4},{6,5},{7,6},{0,7},{9,8},{10,9},{11,1... | collective-permute-start | bytes 786440 | tf_op jit(solution)/shard_map/ppermute | solution.py:27
  30.1 6.1 %collective-permute-done.4 = bf16[128,1,8,128]{3,2,0,1:T(8,128)(2,1)S(1)} collective-permute-done((bf16[128,1,8,128]{3,2,0,1:T(8,128)(2,1)S(1)}, bf16[128,1,8,128]{3,2,0,1:T(8,128)(2,1)S(1)}, u32[]{:S(2)}, u32[]{:S(2)}) %collective-permute-start.4) | collective-permute-done | bytes 262176 | tf_op jit(solution)/shard_map/ppermute | solution.py:25
  36.6 5.8 %while.41 = (s32[]{:T(128)}, bf16[2,64,4,8,128]{4,3,2,1,0:T(8,128)(2,1)S(1)}, bf16[2,64,6,8,128]{4,3,2,1,0:T(8,128)(2,1)S(1)}, f32[4,8,128]{2,1,0:T(8,128)S(1)}, f32[4,8,128]{2,1,0:T(8,128)S(1)}, /*index=5*/s32[]{:T(128)}) while((s32[]{:T(128)}, bf16[2,64,4,8,128]{4,3,2,1,0:T(8,128)(2,1)S(1)}, bf16[2,64,6,8,128]{4,3,2,1,0:T(8,128)(2,1)S(1)}, ...), condition=%wide.region_3.4_spmd, body=%wide.region_2.3_spmd.sunk | while | flops 4980738 | bytes 20217932 | solution.py:57
  37.9 1.5 bitcast_dynamic-update-slice_fusion.9
  42.4 2.6 %collective-permute-start.7 = (bf16[128,1,8,128]{3,2,0,1:T(8,128)(2,1)S(1)}, bf16[128,1,8,128]{3,2,0,1:T(8,128)(2,1)S(1)}, u32[]{:S(2)}, u32[]{:S(2)}) collective-permute-start(bf16[128,1,8,128]{3,2,0,1:T(8,128)(2,1)S(1)} %get-tuple-element.189), channel_id=1, source_target_pairs={{1,0},{2,1},{3,2},{4,3},{5,4},{6,5},{7,6},{0,7},{9,8},{10,9},{11,1... | collective-permute-start | bytes 786440 | tf_op jit(solution)/shard_map/ppermute | solution.py:27
  45.1 6.8 %collective-permute-done.6 = bf16[128,1,8,128]{3,2,0,1:T(8,128)(2,1)S(1)} collective-permute-done((bf16[128,1,8,128]{3,2,0,1:T(8,128)(2,1)S(1)}, bf16[128,1,8,128]{3,2,0,1:T(8,128)(2,1)S(1)}, u32[]{:S(2)}, u32[]{:S(2)}) %collective-permute-start.6) | collective-permute-done | bytes 262176 | tf_op jit(solution)/shard_map/ppermute | solution.py:25
  52.3 5.8 %while.42 = (s32[]{:T(128)}, bf16[2,64,4,8,128]{4,3,2,1,0:T(8,128)(2,1)S(1)}, bf16[2,64,6,8,128]{4,3,2,1,0:T(8,128)(2,1)S(1)}, f32[4,8,128]{2,1,0:T(8,128)S(1)}, f32[4,8,128]{2,1,0:T(8,128)S(1)}, /*index=5*/s32[]{:T(128)}) while((s32[]{:T(128)}, bf16[2,64,4,8,128]{4,3,2,1,0:T(8,128)(2,1)S(1)}, bf16[2,64,6,8,128]{4,3,2,1,0:T(8,128)(2,1)S(1)}, ...), condition=%wide.region_5.6_spmd, body=%wide.region_4.5_spmd.sunk | while | flops 4980738 | bytes 20217932 | solution.py:57
  58.2 2.6 %collective-permute-start.9 = (bf16[128,1,8,128]{3,2,0,1:T(8,128)(2,1)S(1)}, bf16[128,1,8,128]{3,2,0,1:T(8,128)(2,1)S(1)}, u32[]{:S(2)}, u32[]{:S(2)}) collective-permute-start(bf16[128,1,8,128]{3,2,0,1:T(8,128)(2,1)S(1)} %get-tuple-element.187), channel_id=1, source_target_pairs={{1,0},{2,1},{3,2},{4,3},{5,4},{6,5},{7,6},{0,7},{9,8},{10,9},{11,1... | collective-permute-start | bytes 786440 | tf_op jit(solution)/shard_map/ppermute | solution.py:27
  60.8 6.2 %collective-permute-done.8 = bf16[128,1,8,128]{3,2,0,1:T(8,128)(2,1)S(1)} collective-permute-done((bf16[128,1,8,128]{3,2,0,1:T(8,128)(2,1)S(1)}, bf16[128,1,8,128]{3,2,0,1:T(8,128)(2,1)S(1)}, u32[]{:S(2)}, u32[]{:S(2)}) %collective-permute-start.8) | collective-permute-done | bytes 262176 | tf_op jit(solution)/shard_map/ppermute | solution.py:25
  67.5 5.8 %while.43 = (s32[]{:T(128)}, bf16[2,64,4,8,128]{4,3,2,1,0:T(8,128)(2,1)S(1)}, bf16[2,64,6,8,128]{4,3,2,1,0:T(8,128)(2,1)S(1)}, f32[4,8,128]{2,1,0:T(8,128)S(1)}, f32[4,8,128]{2,1,0:T(8,128)S(1)}, /*index=5*/s32[]{:T(128)}) while((s32[]{:T(128)}, bf16[2,64,4,8,128]{4,3,2,1,0:T(8,128)(2,1)S(1)}, bf16[2,64,6,8,128]{4,3,2,1,0:T(8,128)(2,1)S(1)}, ...), condition=%wide.region_7.8_spmd, body=%wide.region_6.7_spmd.sunk | while | flops 4980738 | bytes 20217932 | solution.py:57
  71.7 1.5 bitcast_dynamic-update-slice_fusion.11
  75.2 51.0 %all-reduce.3.cloned.1.call-done = bf16[128,4096]{1,0:T(8,128)(2,1)} async-done(((bf16[128,4096]{1,0:T(8,128)(2,1)}), bf16[128,4096]{1,0:T(8,128)(2,1)}) %all-reduce.3.cloned.1.call-update) | async-done | bytes 1048592 | tf_op jit(solution)/shard_map/psum | solution.py:36
  126.2 2.3 convolution_select_fusion
  128.6 53.4 %all-reduce.5.cloned.1.call-done = f32[128,128]{1,0:T(8,128)} async-done(((f32[128,128]{1,0:T(8,128)}), f32[128,128]{1,0:T(8,128)}) %all-reduce.5.cloned.1.call-update) | async-done | bytes 65552 | tf_op jit(solution)/shard_map/psum | solution.py:92
  183.1 19.0 %psum.23 = bf16[128,128]{1,0:T(8,128)(2,1)S(1)} all-reduce(bf16[128,128]{1,0:T(8,128)(2,1)S(1)} %convolution_convert_fusion.2), channel_id=1, replica_groups=mesh['grp'=4,'slab'=8] {'grp'}, use_global_device_ids=true, to_apply=%region_10.11 | all-reduce | flops 16384 | bytes 65536 | tf_op jit(solution)/shard_map/psum | solution.py:94
  203.6 11.7 %cholesky.18 = f32[128,128]{1,0:T(8,128)S(1)} custom-call(f32[128,128]{1,0:T(8,128)S(1)} %fusion.29), custom_call_target="Cholesky" | custom-call | tf_op jit(solution)/shard_map/jit(cholesky)/cholesky | solution.py:97
  216.6 9.8 %custom-call.10 = f32[1,128,128]{1,2,0:T(8,128)S(1)} custom-call(f32[1,128,128]{2,1,0:T(8,128)S(1)} %fusion.22), custom_call_target="InvertDiagBlocksLowerTriangular" | custom-call | tf_op jit(solution)/shard_map/jit(_cho_solve)/triangular_solve | solution.py:98
  230.4 22.9 %reduce-scatter.2.cloned.1.call-done = bf16[32,4096]{1,0:T(8,128)(2,1)} async-done(((bf16[128,4096]{1,0:T(8,128)(2,1)}), bf16[32,4096]{1,0:T(8,128)(2,1)}) %reduce-scatter.2.cloned.1.call-update) | async-done | bytes 262160 | tf_op jit(solution)/shard_map/reduce_scatter | solution.py:104
  253.4 1.7 copy.17
  (108 shorter events, 32.2 us)
Async XLA Ops:
  7.2 14.0 %copy-start.1 = (bf16[1,128,4,8,128]{4,3,2,1,0:T(8,128)(2,1)S(1)}, bf16[1,128,4,8,128]{4,3,2,1,0:T(8,128)(2,1)}, u32[]{:S(2)}) copy-start(bf16[1,128,4,8,128]{4,3,2,1,0:T(8,128)(2,1)} %param.10) | copy-start | bytes 3145732
  7.2 119.0 %all-reduce.3.cloned.1.call-start = ((), (), s32[]{:S(2)}) async-start(), calls=%async_computation.1 | async-start | bytes 2097152 | tf_op jit(solution)/shard_map/psum | solution.py:36
  7.2 5.3 %collective-permute-start.2 = (f32[4,8,128]{2,1,0:T(8,128)}, f32[4,8,128]{2,1,0:T(8,128)S(1)}, u32[]{:S(2)}, u32[]{:S(2)}) collective-permute-start(f32[4,8,128]{2,1,0:T(8,128)} %param.11), channel_id=1, source_target_pairs={{0,1},{1,2},{2,3},{3,4},{4,5},{5,6},{6,7},{7,0},{8,9},{9,10},{10,1... | collective-permute-start | bytes 49160 | tf_op jit(solution)/shard_map/ppermute | solution.py:25
  7.7 5.5 %collective-permute-start.3 = (f32[4,8,128]{2,1,0:T(8,128)}, f32[4,8,128]{2,1,0:T(8,128)S(1)}, u32[]{:S(2)}, u32[]{:S(2)}) collective-permute-start(f32[4,8,128]{2,1,0:T(8,128)} %param.11), channel_id=1, source_target_pairs={{1,0},{2,1},{3,2},{4,3},{5,4},{6,5},{7,6},{0,7},{9,8},{10,9},{11,1... | collective-permute-start | bytes 49160 | tf_op jit(solution)/shard_map/ppermute | solution.py:27
  11.7 7.3 %collective-permute-start.1 = (bf16[128,1,8,128]{3,2,1,0:T(8,128)(2,1)S(1)}, bf16[128,1,8,128]{3,2,1,0:T(8,128)(2,1)S(1)}, u32[]{:S(2)}, u32[]{:S(2)}) collective-permute-start(bf16[128,1,8,128]{3,2,1,0:T(8,128)(2,1)S(1)} %get-tuple-element.193), channel_id=1, source_target_pairs={{1,0},{2,1},{3,2},{4,3},{5,4},{6,5},{7,6},{0,7},{9,8},{10,9},{11,1... | collective-permute-start | bytes 786440 | tf_op jit(solution)/shard_map/ppermute | solution.py:27
  12.5 8.7 %collective-permute-start = (bf16[128,1,8,128]{3,2,1,0:T(8,128)(2,1)S(1)}, bf16[128,1,8,128]{3,2,1,0:T(8,128)(2,1)S(1)}, u32[]{:S(2)}, u32[]{:S(2)}) collective-permute-start(bf16[128,1,8,128]{3,2,1,0:T(8,128)(2,1)S(1)} %get-tuple-element.192), channel_id=1, source_target_pairs={{0,1},{1,2},{2,3},{3,4},{4,5},{5,6},{6,7},{7,0},{8,9},{9,10},{10,1... | collective-permute-start | bytes 786440 | tf_op jit(solution)/shard_map/ppermute | solution.py:25
  27.4 8.8 %collective-permute-start.4 = (bf16[128,1,8,128]{3,2,0,1:T(8,128)(2,1)S(1)}, bf16[128,1,8,128]{3,2,0,1:T(8,128)(2,1)S(1)}, u32[]{:S(2)}, u32[]{:S(2)}) collective-permute-start(bf16[128,1,8,128]{3,2,0,1:T(8,128)(2,1)S(1)} %get-tuple-element.190), channel_id=1, source_target_pairs={{0,1},{1,2},{2,3},{3,4},{4,5},{5,6},{6,7},{7,0},{8,9},{9,10},{10,1... | collective-permute-start | bytes 786440 | tf_op jit(solution)/shard_map/ppermute | solution.py:25
  27.5 8.7 %collective-permute-start.5 = (bf16[128,1,8,128]{3,2,0,1:T(8,128)(2,1)S(1)}, bf16[128,1,8,128]{3,2,0,1:T(8,128)(2,1)S(1)}, u32[]{:S(2)}, u32[]{:S(2)}) collective-permute-start(bf16[128,1,8,128]{3,2,0,1:T(8,128)(2,1)S(1)} %get-tuple-element.191), channel_id=1, source_target_pairs={{1,0},{2,1},{3,2},{4,3},{5,4},{6,5},{7,6},{0,7},{9,8},{10,9},{11,1... | collective-permute-start | bytes 786440 | tf_op jit(solution)/shard_map/ppermute | solution.py:27
  42.4 9.5 %collective-permute-start.6 = (bf16[128,1,8,128]{3,2,0,1:T(8,128)(2,1)S(1)}, bf16[128,1,8,128]{3,2,0,1:T(8,128)(2,1)S(1)}, u32[]{:S(2)}, u32[]{:S(2)}) collective-permute-start(bf16[128,1,8,128]{3,2,0,1:T(8,128)(2,1)S(1)} %get-tuple-element.188), channel_id=1, source_target_pairs={{0,1},{1,2},{2,3},{3,4},{4,5},{5,6},{6,7},{7,0},{8,9},{9,10},{10,1... | collective-permute-start | bytes 786440 | tf_op jit(solution)/shard_map/ppermute | solution.py:25
  42.4 9.5 %collective-permute-start.7 = (bf16[128,1,8,128]{3,2,0,1:T(8,128)(2,1)S(1)}, bf16[128,1,8,128]{3,2,0,1:T(8,128)(2,1)S(1)}, u32[]{:S(2)}, u32[]{:S(2)}) collective-permute-start(bf16[128,1,8,128]{3,2,0,1:T(8,128)(2,1)S(1)} %get-tuple-element.189), channel_id=1, source_target_pairs={{1,0},{2,1},{3,2},{4,3},{5,4},{6,5},{7,6},{0,7},{9,8},{10,9},{11,1... | collective-permute-start | bytes 786440 | tf_op jit(solution)/shard_map/ppermute | solution.py:27
  58.1 8.9 %collective-permute-start.8 = (bf16[128,1,8,128]{3,2,0,1:T(8,128)(2,1)S(1)}, bf16[128,1,8,128]{3,2,0,1:T(8,128)(2,1)S(1)}, u32[]{:S(2)}, u32[]{:S(2)}) collective-permute-start(bf16[128,1,8,128]{3,2,0,1:T(8,128)(2,1)S(1)} %get-tuple-element.186), channel_id=1, source_target_pairs={{0,1},{1,2},{2,3},{3,4},{4,5},{5,6},{6,7},{7,0},{8,9},{9,10},{10,1... | collective-permute-start | bytes 786440 | tf_op jit(solution)/shard_map/ppermute | solution.py:25
  58.2 8.9 %collective-permute-start.9 = (bf16[128,1,8,128]{3,2,0,1:T(8,128)(2,1)S(1)}, bf16[128,1,8,128]{3,2,0,1:T(8,128)(2,1)S(1)}, u32[]{:S(2)}, u32[]{:S(2)}) collective-permute-start(bf16[128,1,8,128]{3,2,0,1:T(8,128)(2,1)S(1)} %get-tuple-element.187), channel_id=1, source_target_pairs={{1,0},{2,1},{3,2},{4,3},{5,4},{6,5},{7,6},{0,7},{9,8},{10,9},{11,1... | collective-permute-start | bytes 786440 | tf_op jit(solution)/shard_map/ppermute | solution.py:27
  74.6 107.3 %all-reduce.5.cloned.1.call-start = ((), (), s32[]{:S(2)}) async-start(), calls=%async_computation.2 | async-start | bytes 131072 | tf_op jit(solution)/shard_map/psum | solution.py:92
  128.5 124.9 %reduce-scatter.2.cloned.1.call-start = ((), (), s32[]{:S(2)}) async-start(), calls=%async_computation.3 | async-start | bytes 1310720 | tf_op jit(solution)/shard_map/reduce_scatter | solution.py:104
  228.0 1.4 copy-start
Sparse Core Ops, SparseCore 0:
  74.7 51.4 all-reduce.2
  130.1 51.8 all-reduce.4
  229.5 23.7 reduce-scatter.1
where the time goes:
time: 262 us
  waiting for transfers between devices  154 us (59%)
  other arithmetic  37.5 us (14%)
  blocking collectives  19 us (7%)
  local copies, waits for them, and re-layouts  16.5 us (6%)
  between operations  14.7 us (6%)
  starting transfers between devices  12.4 us (5%)
  matrix products  6.64 us (3%)
    psum x1, waiting for transfers between devices, per_device(): coupling = lax.psum(partial_value, 'slab') * norm_scale  53.4 us
    psum x1, waiting for transfers between devices, spread(): return lax.psum(kept, axis)  51 us
    reduce_scatter x1, waiting for transfers between devices, per_device(): lax.psum_scatter(jnp.dot(row_block, direct_flat, preferred_element_type=j...  22.9 us
    ppermute x5, waiting for transfers between devices, with_halo(): lax.ppermute(tail, axis, [(i, (i + 1) % count) for i in range(count)])  21.3 us
    psum x1, blocking collectives, per_device(): lax.psum(own_gram.astype(jnp.bfloat16), 'grp').astype(jnp.float32)  19 us
    another operation x3, other arithmetic, per_device(): factor = jnp.linalg.cholesky(system)  12.4 us
    dynamic_update_slice x8, other arithmetic, blockwise(): result = lax.map(sweep_block, blocks)  11.9 us
    ppermute x5, starting transfers between devices, with_halo(): lax.ppermute(head, axis, [((i + 1) % count, i) for i in range(count)])  11.6 us
  transfers between devices with their start and end apart: 13, of which 8 were waited for; matrix products, arithmetic and copies ran while one was open for 1% of the time, Pallas kernels for 0%

commit v1 on v0

v1 whole, which is shorter than its diff:
```python
import functools
import math

import jax
import jax.numpy as jnp
from jax import lax
from jax.experimental import pallas as pl
from jax.experimental.pallas import tpu as pltpu
from jax.sharding import PartitionSpec as P

SECTIONS = 4
CHUNKS = 1

diffuse_x = 0.35
diffuse_side = 0.05
damping = 0.5

VMEM_LIMIT = 48 * 1024 * 1024
vmem = pl.BlockSpec(memory_space=pltpu.VMEM)
smem = pl.BlockSpec(memory_space=pltpu.SMEM)
anywhere = pl.BlockSpec(memory_space=pl.ANY)
f32 = jnp.float32
bf16 = jnp.bfloat16


def peer(index, step):
    return index ^ step


def swap(value, axis, step):
    count = lax.axis_size(axis)
    return lax.ppermute(value, axis, [(i, i ^ step) for i in range(count)])


def shift(value, axis, step):
    count = lax.axis_size(axis)
    return lax.ppermute(value, axis, [(i, (i + step) % count) for i in range(count)])


def sections_kernel(groups, rows, where_ref, flow_ref, flow_lo, flow_hi, ring_ref,
                    own_ref, lo_ref, hi_ref, *rest):
    outs = rest[:groups]
    flow_ext, plus, minus, stage, first, second = rest[groups:]
    snaps, _, ny, nz = own_ref.shape
    reach = SECTIONS
    me = where_ref[0]
    adj = (me == groups - 1).astype(jnp.int32)
    sign = jnp.where(me == groups - 1, f32(0.5), f32(-0.5))
    flow_ext[0:reach] = flow_lo[...]
    flow_ext[reach:reach + rows] = flow_ref[...]
    flow_ext[reach + rows:] = flow_hi[...]
    total = rows + 2 * reach
    for e in range(1, total - 1):
        plus[e] = diffuse_x + sign * flow_ext[e + adj]
        minus[e] = diffuse_x - sign * flow_ext[e - adj]

    def turn(source, base, count):
        def body(r, carry):
            block = source[:, pl.ds(r, 1)]
            stage[...] = block.astype(f32).reshape(snaps * ny, nz)
            for y in range(ny):
                first[base + r, y] = stage[pl.ds(y, snaps, stride=ny), :].astype(bf16)
            return carry
        lax.fori_loop(0, count, body, 0)

    turn(lo_ref, 0, reach)
    turn(own_ref, reach, rows)
    turn(hi_ref, reach + rows, reach)
    ring = ring_ref[...]

    def one(src, e, y):
        side = jnp.dot(src[e, y], ring, preferred_element_type=f32)
        side = side + src[e, (y + 1) % ny].astype(f32) + src[e, (y - 1) % ny].astype(f32)
        updated = diffuse_side * side
        updated = updated + plus[e][y:y + 1] * src[e + 1, y].astype(f32)
        updated = updated + minus[e][y:y + 1] * src[e - 1, y].astype(f32)
        return updated.astype(bf16)

    bufs = (first, second)
    for s in range(1, SECTIONS):
        src, dst = bufs[(s - 1) % 2], bufs[s % 2]

        def body(e, carry, src=src, dst=dst):
            for y in range(ny):
                dst[e, y] = one(src, e, y)
            return carry
        lax.fori_loop(s, total - s, body, 0)
    src = bufs[(SECTIONS - 1) % 2]
    share = rows // groups
    for k in range(groups):
        for j in range(share):
            e = reach + peer(me, k) * share + j
            for y in range(ny):
                outs[k][j * ny + y] = one(src, e, y)


def sections(where, flow, flow_lo, flow_hi, ring, own, lo, hi, groups):
    snaps, rows, ny, nz = own.shape
    share = rows // groups
    total = rows + 2 * SECTIONS
    return pl.pallas_call(
        functools.partial(sections_kernel, groups, rows),
        out_shape=[jax.ShapeDtypeStruct((share * ny, snaps, nz), bf16)] * groups,
        in_specs=[smem] + [vmem] * 7,
        out_specs=[vmem] * groups,
        scratch_shapes=[
            pltpu.VMEM((total, ny, nz), f32),
            pltpu.VMEM((total, ny, nz), f32),
            pltpu.VMEM((total, ny, nz), f32),
            pltpu.VMEM((snaps * ny, nz), f32),
            pltpu.VMEM((total, ny, snaps, nz), bf16),
            pltpu.VMEM((total, ny, snaps, nz), bf16),
        ],
        compiler_params=pltpu.CompilerParams(vmem_limit_bytes=VMEM_LIMIT),
        name="sections",
    )(where, flow, flow_lo, flow_hi, ring, own, lo, hi)


def coupling_kernel(groups, chunks, where_ref, *rest):
    blocks = rest[: groups * chunks]
    fields, keep, send, scratch, sem = rest[groups * chunks:]
    me, half = where_ref[0], where_ref[1]
    step = blocks[0].shape[1]
    copies = []
    for k in range(groups):
        for c in range(chunks):
            copies.append(pltpu.make_async_copy(
                blocks[k * chunks + c],
                fields.at[peer(me, k), :, pl.ds(c * step, step)],
                sem.at[k * chunks + c]))
    for copy in copies:
        copy.start()
    for copy in copies:
        copy.wait()
    parts, snaps = fields.shape[1], fields.shape[2]
    width = 2 if parts % 2 == 0 else 1

    def wide(g, y):
        return jnp.concatenate([fields[g, y + i] for i in range(width)], axis=1)

    for g in range(groups - 1):
        acc = None
        for y in range(0, parts, width):
            term = lax.dot_general(wide(groups - 1, y), wide(g, y), (((1,), (1,)), ((), ())),
                                   preferred_element_type=f32)
            acc = term if acc is None else acc + term
        scratch[:, g * snaps:(g + 1) * snaps] = acc
    mid = snaps // 2
    keep[...] = scratch[pl.ds(pl.multiple_of(half * mid, mid), mid), :]
    send[...] = scratch[pl.ds(pl.multiple_of((1 - half) * mid, mid), mid), :].astype(send.dtype)


def coupling(where, blocks, groups, chunks):
    parts, step, nz = blocks[0].shape
    snaps = step * chunks
    wide = (groups - 1) * snaps
    return pl.pallas_call(
        functools.partial(coupling_kernel, groups, chunks),
        out_shape=[
            jax.ShapeDtypeStruct((groups, parts, snaps, nz), bf16),
            jax.ShapeDtypeStruct((snaps // 2, wide), f32),
            jax.ShapeDtypeStruct((snaps // 2, wide), f32),
        ],
        in_specs=[smem] + [anywhere] * (groups * chunks),
        out_specs=[vmem] * 3,
        scratch_shapes=[pltpu.VMEM((snaps, wide), f32),
                        pltpu.SemaphoreType.DMA((groups * chunks,))],
        compiler_params=pltpu.CompilerParams(vmem_limit_bytes=VMEM_LIMIT),
        name="coupling",
    )(where, *blocks)


def invert(system):
    size = system.shape[0]
    panels = [system[8 * i:8 * i + 8] for i in range(size // 8)]
    lane = lax.broadcasted_iota(jnp.int32, (8, size), 1)
    row = lax.broadcasted_iota(jnp.int32, (8, size), 0)

    def spread_lane(panel, j):
        return jnp.broadcast_to(panel[:, j:j + 1], (8, size))

    def spread_row(value, j):
        return jnp.broadcast_to(value[j:j + 1], (8, size))

    def small_inverse(a, b, d):
        det = 1.0 / (a * d - b * b)
        return d * det, -b * det, a * det

    for p in range(size // 8):
        for h in range(2):
            base = 8 * p + 4 * h
            lead = panels[p]
            cols = [spread_lane(lead, base + j) for j in range(4)]
            m = [[spread_row(cols[j], 4 * h + i) for j in range(4)] for i in range(4)]
            a0, a1, a2 = small_inverse(m[0][0], m[0][1], m[1][1])
            b00, b01, b10, b11 = m[0][2], m[0][3], m[1][2], m[1][3]
            x00, x01 = a0 * b00 + a1 * b10, a0 * b01 + a1 * b11
            x10, x11 = a1 * b00 + a2 * b10, a1 * b01 + a2 * b11
            s0 = m[2][2] - (b00 * x00 + b10 * x10)
            s1 = m[2][3] - (b00 * x01 + b10 * x11)
            s2 = m[3][3] - (b01 * x01 + b11 * x11)
            d0, d1, d2 = small_inverse(s0, s1, s2)
            y00, y01 = x00 * d0 + x01 * d1, x00 * d1 + x01 * d2
            y10, y11 = x10 * d0 + x11 * d1, x10 * d1 + x11 * d2
            inv = [
                [a0 + y00 * x00 + y01 * x01, a1 + y00 * x10 + y01 * x11, -y00, -y01],
                [None, a2 + y10 * x10 + y11 * x11, -y10, -y11],
                [None, None, d0, d1],
                [None, None, None, d2],
            ]
            for i in range(4):
                for j in range(i):
                    inv[i][j] = inv[j][i]
            rows4 = [spread_row(lead, 4 * h + i) for i in range(4)]
            for i in range(4):
                for j in range(4):
                    rows4[i] = jnp.where(lane == base + j, f32(1.0 if i == j else 0.0), rows4[i])
            new = [sum(inv[i][j] * rows4[j] for j in range(4)) for i in range(4)]
            block = (lane >= base) & (lane < base + 4)
            for q in range(size // 8):
                target = panels[q]
                kept = jnp.where(block, f32(0.0), target)
                if q == p:
                    factors = cols
                else:
                    factors = [spread_lane(target, base + j) for j in range(4)]
                out = kept - sum(factors[j] * new[j] for j in range(4))
                if q == p:
                    for i in range(4):
                        out = jnp.where(row == 4 * h + i, new[i], out)
                panels[q] = out
    return jnp.concatenate(panels, axis=0)


def modes_kernel(groups, where_ref, mine_ref, other_ref, fields, *rest):
    outs = rest[:groups]
    coupling_ref, stage = rest[groups:]
    me, half = where_ref[0], where_ref[1]
    mid = mine_ref.shape[0]
    snaps = 2 * mid
    parts = fields.shape[1]
    scale = where_ref.shape[0]
    coupling_ref[pl.ds(pl.multiple_of(half * mid, mid), mid), :] = mine_ref[...]
    coupling_ref[pl.ds(pl.multiple_of((1 - half) * mid, mid), mid), :] = other_ref[...]
    coupled = coupling_ref[...]
    gram = lax.dot_general(coupled, coupled, (((1,), (1,)), ((), ())),
                           precision=lax.Precision.HIGHEST, preferred_element_type=f32)
    r = lax.broadcasted_iota(jnp.int32, (snaps, snaps), 0)
    c = lax.broadcasted_iota(jnp.int32, (snaps, snaps), 1)
    diagonal = jnp.where(r == c, gram, 0.0)
    energy = jnp.sum(jnp.sum(diagonal, axis=0, keepdims=True), axis=1, keepdims=True) / snaps
    system = gram / energy + jnp.where(r == c, f32(damping), f32(0.0))
    inverse = invert(system)
    weights = jnp.dot(inverse, coupled, precision=lax.Precision.HIGHEST,
                      preferred_element_type=f32) / jnp.sqrt(energy)
    weights = weights.astype(bf16)
    inverse = inverse.astype(bf16)
    share = snaps // groups
    ny = outs[0].shape[3]
    layers = parts // ny
    for which in range(2):
        for layer in range(layers):
            for y in range(ny):
                at = layer * ny + y
                if which == 0:
                    stacked = jnp.concatenate([fields[g, at] for g in range(groups - 1)], axis=0)
                    value = jnp.dot(weights, stacked, preferred_element_type=f32)
                else:
                    value = jnp.dot(inverse, fields[groups - 1, at], preferred_element_type=f32)
                stage[which, layer, pl.ds(y, snaps, stride=ny), :] = value
    for k in range(groups):
        start = pl.multiple_of(peer(me, k) * (share * ny), share * ny)
        for which in range(2):
            for layer in range(layers):
                value = stage[which, layer, pl.ds(start, share * ny), :]
                outs[k][which, :, layer] = value.reshape(share, ny, value.shape[1]).astype(bf16)


def modes(where, mine, other, fields, groups, ny):
    _, parts, snaps, nz = fields.shape
    layers = parts // ny
    share = snaps // groups
    return pl.pallas_call(
        functools.partial(modes_kernel, groups),
        out_shape=[jax.ShapeDtypeStruct((2, share, layers, ny, nz), bf16)] * groups,
        in_specs=[smem, vmem, vmem, vmem],
        out_specs=[vmem] * groups,
        scratch_shapes=[pltpu.VMEM((snaps, mine.shape[1]), f32),
                        pltpu.VMEM((2, layers, snaps * ny, nz), f32)],
        compiler_params=pltpu.CompilerParams(vmem_limit_bytes=VMEM_LIMIT),
        name="modes",
    )(where, mine, other, fields)


def place_kernel(groups, where_ref, *rest):
    blocks = rest[:groups]
    direct, adjoint, sem = rest[groups:]
    me = where_ref[0]
    layers = blocks[0].shape[2]
    copies = []
    for k in range(groups):
        for which, out in enumerate((direct, adjoint)):
            copies.append(pltpu.make_async_copy(
                blocks[k].at[which],
                out.at[:, pl.ds(peer(me, k) * layers, layers)],
                sem.at[2 * k + which]))
    for copy in copies:
        copy.start()
    for copy in copies:
        copy.wait()


def place(where, blocks, groups):
    _, share, layers, ny, nz = blocks[0].shape
    out = jax.ShapeDtypeStruct((share, layers * groups, ny, nz), bf16)
    return pl.pallas_call(
        functools.partial(place_kernel, groups),
        out_shape=[out, out],
        in_specs=[smem] + [anywhere] * groups,
        out_specs=[anywhere] * 2,
        scratch_shapes=[pltpu.SemaphoreType.DMA((2 * groups,))],
        name="place",
    )(where, *blocks)


def per_device(snapshots, base_flow):
    field = snapshots[0]
    snaps, rows, ny, nz = field.shape
    groups = lax.axis_size("grp")
    slabs = lax.axis_size("slab")
    me = lax.axis_index("grp")
    half = lax.axis_index("slab") % 2
    where = jnp.stack([me, half]).astype(jnp.int32)
    flow_lo = shift(base_flow[rows - SECTIONS:], "slab", 1)
    flow_hi = shift(base_flow[:SECTIONS], "slab", -1)
    at = jnp.arange(nz)
    gap = (at[:, None] - at[None, :]) % nz
    ring = (2 * (gap == 0) + (gap == 1) + (gap == nz - 1)).astype(bf16)
    step = snaps // CHUNKS
    blocks = [[None] * CHUNKS for _ in range(groups)]
    for c in range(CHUNKS):
        own = field[c * step:(c + 1) * step]
        lo = shift(own[:, rows - SECTIONS:], "slab", 1)
        hi = shift(own[:, :SECTIONS], "slab", -1)
        parts = sections(where, base_flow, flow_lo, flow_hi, ring, own, lo, hi, groups)
        blocks[0][c] = parts[0]
        for k in range(1, groups):
            blocks[k][c] = swap(parts[k], "grp", k)
    flat = [blocks[k][c] for k in range(groups) for c in range(CHUNKS)]
    fields, keep, send = coupling(where, flat, groups, CHUNKS)
    total = keep + swap(send, "slab", 1)
    bit = 2
    while bit < slabs:
        steps = [bit]
        if 2 * bit < slabs:
            steps += [2 * bit, 3 * bit]
        sent = total.astype(bf16)
        total = sum((swap(sent, "slab", s).astype(f32) for s in steps), total)
        bit *= 4
    sent = total.astype(bf16)
    total = sum((swap(sent, "grp", s).astype(f32) for s in range(1, groups)), total)
    mine = total * (1.0 / math.sqrt(rows * slabs * ny * nz))
    other = swap(mine, "slab", 1)
    outs = modes(where, mine, other, fields, groups, ny)
    outs = [outs[0]] + [swap(outs[k], "grp", k) for k in range(1, groups)]
    return tuple(place(where, outs, groups))


def solution(mesh):
    return jax.shard_map(
        per_device,
        mesh=mesh,
        in_specs=(P("grp", None, "slab", None, None), P("slab", None, None)),
        out_specs=(P("grp", "slab", None, None), P("grp", "slab", None, None)),
        check_vma=False,
    )
```

time: 262 us -> 126 us (0.48)
  waiting for transfers between devices: 154 us -> 59 us
  other arithmetic: 37.5 us -> 0.22 us
  Pallas kernels: 0 us -> 36.9 us
  blocking collectives: 19 us -> 0 us
  between operations: 14.7 us -> 0.73 us
  local copies, waits for them, and re-layouts: 16.5 us -> 2.57 us
  starting transfers between devices: 12.4 us -> 26 us
  matrix products: 6.64 us -> 0 us
    psum x2 -> x0, waiting for transfers between devices: 104 us -> none  [the longest x1 53.4 us: per_device(): coupling = lax.psum(partial_value, 'slab') * norm_scale]
    pallas_call x0 -> x4, Pallas kernels: none -> 36.9 us  [the longest x1 17.7 us: place(): pl.pallas_call(functools.partial(place_kernel, groups), out_shape=[out, o...]
    ppermute x10 -> x18, waiting for transfers between devices: 27.1 us -> 59 us  [the longest x14 36.6 us: swap(): return lax.ppermute(value, axis, [(i, i ^ step) for i in range(count)])]
    reduce_scatter x1 -> x0, waiting for transfers between devices: 22.9 us -> none  [per_device(): lax.psum_scatter(jnp.dot(row_block, direct_flat, preferred_element_type=j...]
    another operation x5 -> x1, other arithmetic: 22.9 us -> 0.08 us  [per_device(): where = jnp.stack([me, half]).astype(jnp.int32)]
    psum x1 -> x0, blocking collectives: 19 us -> none  [per_device(): lax.psum(own_gram.astype(jnp.bfloat16), 'grp').astype(jnp.float32)]
    ppermute x10 -> x18, starting transfers between devices: 12.3 us -> 26 us  [the longest x14 19.9 us: swap(): return lax.ppermute(value, axis, [(i, i ^ step) for i in range(count)])]
    dynamic_update_slice x8 -> x0, other arithmetic: 11.9 us -> none  [blockwise(): result = lax.map(sweep_block, blocks)]
  transfers between devices with their start and end apart: 13 -> 18, of which waited for: 8 -> 11; matrix products, arithmetic and copies ran while one was open for 1% -> 0% of each run, Pallas kernels for 0% -> 0%
where the time goes in v1:
time: 126 us; the launch traced here: 125 us
  waiting for transfers between devices  59 us (47%)
  Pallas kernels  36.9 us (29%)
  starting transfers between devices  26 us (21%)
  local copies, waits for them, and re-layouts  2.57 us (2%)
    ppermute x14, waiting for transfers between devices, swap(): return lax.ppermute(value, axis, [(i, i ^ step) for i in range(count)])  36.6 us
    ppermute x4, waiting for transfers between devices, shift(): lax.ppermute(value, axis, [(i, (i + step) % count) for i in range(count)])  22.3 us
    ppermute x14, starting transfers between devices, swap(): return lax.ppermute(value, axis, [(i, i ^ step) for i in range(count)])  19.9 us
    pallas_call x1, Pallas kernels, place(): pl.pallas_call(functools.partial(place_kernel, groups), out_shape=[out, o...  17.7 us
    pallas_call x1, Pallas kernels, sections(): pl.pallas_call(functools.partial(sections_kernel, groups, rows), out_shap...  9.94 us
    pallas_call x1, Pallas kernels, modes(): pl.pallas_call(functools.partial(modes_kernel, groups), out_shape=[jax.Sh...  8.23 us
    ppermute x4, starting transfers between devices, shift(): lax.ppermute(value, axis, [(i, (i + step) % count) for i in range(count)])  6.06 us
    unnamed x14, local copies, waits for them, and re-layouts  2.57 us
  transfers between devices with their start and end apart: 18, of which 11 were waited for; matrix products, arithmetic and copies ran while one was open for 0% of the time, Pallas kernels for 0%

profile of v1, /device:TPU:0, one launch (start us, length us, event | category | flops | bytes accessed | tf_op | source)
XLA Modules:
  0.0 125.4 jit_solution(14605039157931094248)
XLA Ops:
  0.6 3.4 %collective-permute-start.3 = (bf16[128,4,8,128]{3,2,1,0:T(8,128)(2,1)}, bf16[128,4,8,128]{3,2,1,0:T(8,128)(2,1)S(1)}, u32[]{:S(2)}, u32[]{:S(2)}) collective-permute-start(bf16[128,4,8,128]{3,2,1,0:T(8,128)(2,1)} %bitcast.3), channel_id=1, source_target_pairs={{0,7},{1,0},{2,1},{3,2},{4,3},{5,4},{6,5},{7,6},{8,15},{9,8},{10,9... | collective-permute-start | bytes 3145736 | tf_op jit(solution)/shard_map/ppermute | solution.py:37
  4.0 2.7 %collective-permute-start.1 = (f32[4,8,128]{2,1,0:T(8,128)}, f32[4,8,128]{2,1,0:T(8,128)S(1)}, u32[]{:S(2)}, u32[]{:S(2)}) collective-permute-start(f32[4,8,128]{2,1,0:T(8,128)} %flow_ref.1), channel_id=1, source_target_pairs={{0,7},{1,0},{2,1},{3,2},{4,3},{5,4},{6,5},{7,6},{8,15},{9,8},{10,9... | collective-permute-start | bytes 49160 | tf_op jit(solution)/shard_map/ppermute | solution.py:37
  6.8 22.3 %collective-permute-done.flow_lo = f32[4,8,128]{2,1,0:T(8,128)S(1)} collective-permute-done((f32[4,8,128]{2,1,0:T(8,128)}, f32[4,8,128]{2,1,0:T(8,128)S(1)}, u32[]{:S(2)}, u32[]{:S(2)}) %collective-permute-start) | collective-permute-done | bytes 16416 | tf_op jit(solution)/shard_map/ppermute | solution.py:37
  29.2 1.2 copy-done
  30.4 9.9 %sections.1 = (bf16[8,128,128]{2,1,0:T(8,128)(2,1)S(1)}, bf16[8,128,128]{2,1,0:T(8,128)(2,1)S(1)}, bf16[8,128,128]{2,1,0:T(8,128)(2,1)S(1)}, bf16[8,128,128]{2,1,0:T(8,128)(2,1)S(1)}) custom-call(s32[2]{0:T(128)S(1)} %pad_add_fusion.where_ref, f32[4,8,128]{2,1,0:T(8,128)S(1)} %copy-done.2, f32[4,8,128]{2,1,0:T(8,128)S(1)} %collective-permute-done.flow_lo, ...), custom_call_target="tpu_custom_call" | custom-call | tf_op jit(solution)/shard_map/sections/pallas_call | solution.py:101
  40.4 1.6 %collective-permute-start.4 = (bf16[8,128,128]{2,1,0:T(8,128)(2,1)S(1)}, bf16[8,128,128]{2,1,0:T(8,128)(2,1)S(1)}, u32[]{:S(2)}, u32[]{:S(2)}) collective-permute-start(bf16[8,128,128]{2,1,0:T(8,128)(2,1)S(1)} %get-tuple-element.14), channel_id=1, source_target_pairs={{0,8},{8,0},{16,24},{24,16},{1,9},{9,1},{17,25},{25,17},{2,10},{10... | collective-permute-start | bytes 786440 | tf_op jit(solution)/shard_map/ppermute | solution.py:32
  42.0 2.6 %collective-permute-start.5 = (bf16[8,128,128]{2,1,0:T(8,128)(2,1)S(1)}, bf16[8,128,128]{2,1,0:T(8,128)(2,1)S(1)}, u32[]{:S(2)}, u32[]{:S(2)}) collective-permute-start(bf16[8,128,128]{2,1,0:T(8,128)(2,1)S(1)} %get-tuple-element.15), channel_id=1, source_target_pairs={{0,16},{8,24},{16,0},{24,8},{1,17},{9,25},{17,1},{25,9},{2,18},{10... | collective-permute-start | bytes 786440 | tf_op jit(solution)/shard_map/ppermute | solution.py:32
  44.8 4.7 %collective-permute-done.4.rest_1_ = bf16[8,128,128]{2,1,0:T(8,128)(2,1)S(1)} collective-permute-done((bf16[8,128,128]{2,1,0:T(8,128)(2,1)S(1)}, bf16[8,128,128]{2,1,0:T(8,128)(2,1)S(1)}, u32[]{:S(2)}, u32[]{:S(2)}) %collective-permute-start.4) | collective-permute-done | bytes 262176 | tf_op jit(solution)/shard_map/ppermute | solution.py:32
  49.5 12.8 %collective-permute-done.5.rest_2_ = bf16[8,128,128]{2,1,0:T(8,128)(2,1)S(1)} collective-permute-done((bf16[8,128,128]{2,1,0:T(8,128)(2,1)S(1)}, bf16[8,128,128]{2,1,0:T(8,128)(2,1)S(1)}, u32[]{:S(2)}, u32[]{:S(2)}) %collective-permute-start.5) | collective-permute-done | bytes 262176 | tf_op jit(solution)/shard_map/ppermute | solution.py:32
  62.2 1.0 coupling.1
  63.3 1.3 %collective-permute-done.7 = f32[64,384]{1,0:T(8,128)S(1)} collective-permute-done((f32[64,384]{1,0:T(8,128)S(1)}, f32[64,384]{1,0:T(8,128)S(1)}, u32[]{:S(2)}, u32[]{:S(2)}) %collective-permute-start.7) | collective-permute-done | bytes 98336 | tf_op jit(solution)/shard_map/ppermute | solution.py:32
  64.7 2.6 %collective-permute-start.10 = (bf16[64,384]{1,0:T(8,128)(2,1)S(1)}, bf16[64,384]{1,0:T(8,128)(2,1)S(1)}, u32[]{:S(2)}, u32[]{:S(2)}) collective-permute-start(bf16[64,384]{1,0:T(8,128)(2,1)S(1)} %get-tuple-element.24), channel_id=1, source_target_pairs={{0,6},{1,7},{2,4},{3,5},{4,2},{5,3},{6,0},{7,1},{8,14},{9,15},{10,... | collective-permute-start | bytes 147464 | tf_op jit(solution)/shard_map/ppermute | solution.py:32
  68.2 1.5 %collective-permute-done.10 = bf16[64,384]{1,0:T(8,128)(2,1)S(1)} collective-permute-done((bf16[64,384]{1,0:T(8,128)(2,1)S(1)}, bf16[64,384]{1,0:T(8,128)(2,1)S(1)}, u32[]{:S(2)}, u32[]{:S(2)}) %collective-permute-start.10) | collective-permute-done | bytes 49184 | tf_op jit(solution)/shard_map/ppermute | solution.py:32
  69.7 1.6 %collective-permute-done.9 = bf16[64,384]{1,0:T(8,128)(2,1)S(1)} collective-permute-done((bf16[64,384]{1,0:T(8,128)(2,1)S(1)}, bf16[64,384]{1,0:T(8,128)(2,1)S(1)}, u32[]{:S(2)}, u32[]{:S(2)}) %collective-permute-start.9) | collective-permute-done | bytes 49184 | tf_op jit(solution)/shard_map/ppermute | solution.py:32
  71.4 2.5 %collective-permute-start.13 = (bf16[64,384]{1,0:T(8,128)(2,1)S(1)}, bf16[64,384]{1,0:T(8,128)(2,1)S(1)}, u32[]{:S(2)}, u32[]{:S(2)}) collective-permute-start(bf16[64,384]{1,0:T(8,128)(2,1)S(1)} %fusion.4), channel_id=1, source_target_pairs={{0,24},{8,16},{16,8},{24,0},{1,25},{9,17},{17,9},{25,1},{2,26},{10... | collective-permute-start | bytes 147464 | tf_op jit(solution)/shard_map/ppermute | solution.py:32
  73.9 4.7 %collective-permute-start.12 = (bf16[64,384]{1,0:T(8,128)(2,1)S(1)}, bf16[64,384]{1,0:T(8,128)(2,1)S(1)}, u32[]{:S(2)}, u32[]{:S(2)}) collective-permute-start(bf16[64,384]{1,0:T(8,128)(2,1)S(1)} %fusion.4), channel_id=1, source_target_pairs={{0,16},{8,24},{16,0},{24,8},{1,17},{9,25},{17,1},{25,9},{2,18},{10... | collective-permute-start | bytes 147464 | tf_op jit(solution)/shard_map/ppermute | solution.py:32
  78.8 3.0 %collective-permute-done.12 = bf16[64,384]{1,0:T(8,128)(2,1)S(1)} collective-permute-done((bf16[64,384]{1,0:T(8,128)(2,1)S(1)}, bf16[64,384]{1,0:T(8,128)(2,1)S(1)}, u32[]{:S(2)}, u32[]{:S(2)}) %collective-permute-start.12) | collective-permute-done | bytes 49184 | tf_op jit(solution)/shard_map/ppermute | solution.py:32
  82.8 1.3 %collective-permute-done.14.other_ref = f32[64,384]{1,0:T(8,128)S(1)} collective-permute-done((f32[64,384]{1,0:T(8,128)S(1)}, f32[64,384]{1,0:T(8,128)S(1)}, u32[]{:S(2)}, u32[]{:S(2)}) %collective-permute-start.14) | collective-permute-done | bytes 98336 | tf_op jit(solution)/shard_map/ppermute | solution.py:32
  84.1 8.2 %modes.1 = (bf16[2,32,1,8,128]{4,3,2,1,0:T(8,128)(2,1)S(1)}, bf16[2,32,1,8,128]{4,3,2,1,0:T(8,128)(2,1)S(1)}, bf16[2,32,1,8,128]{4,3,2,1,0:T(8,128)(2,1)S(1)}, bf16[2,32,1,8,128]{4,3,2,1,0:T(8,128)(2,1)S(1)}) custom-call(s32[2]{0:T(128)S(1)} %pad_add_fusion.where_ref, f32[64,384]{1,0:T(8,128)S(1)} %add_multiply_fusion.mine_ref, ...), custom_call_target="tpu_custom_call" | custom-call | tf_op jit(solution)/shard_map/modes/pallas_call | solution.py:283
  94.1 2.0 %collective-permute-start.16 = (bf16[2,32,1,8,128]{4,3,2,1,0:T(8,128)(2,1)S(1)}, bf16[2,32,1,8,128]{4,3,2,1,0:T(8,128)(2,1)S(1)}, u32[]{:S(2)}, u32[]{:S(2)}) collective-permute-start(bf16[2,32,1,8,128]{4,3,2,1,0:T(8,128)(2,1)S(1)} %get-tuple-element.22), channel_id=1, source_target_pairs={{0,16},{8,24},{16,0},{24,8},{1,17},{9,25},{17,1},{25,9},{2,18},{10... | collective-permute-start | bytes 393224 | tf_op jit(solution)/shard_map/ppermute | solution.py:32
  96.1 1.3 %collective-permute-start.17 = (bf16[2,32,1,8,128]{4,3,2,1,0:T(8,128)(2,1)S(1)}, bf16[2,32,1,8,128]{4,3,2,1,0:T(8,128)(2,1)S(1)}, u32[]{:S(2)}, u32[]{:S(2)}) collective-permute-start(bf16[2,32,1,8,128]{4,3,2,1,0:T(8,128)(2,1)S(1)} %get-tuple-element.23), channel_id=1, source_target_pairs={{0,24},{8,16},{16,8},{24,0},{1,25},{9,17},{17,9},{25,1},{2,26},{10... | collective-permute-start | bytes 393224 | tf_op jit(solution)/shard_map/ppermute | solution.py:32
  97.4 3.1 %collective-permute-done.15.rest_1_ = bf16[2,32,1,8,128]{4,3,2,1,0:T(8,128)(2,1)S(1)} collective-permute-done((bf16[2,32,1,8,128]{4,3,2,1,0:T(8,128)(2,1)S(1)}, bf16[2,32,1,8,128]{4,3,2,1,0:T(8,128)(2,1)S(1)}, u32[]{:S(2)}, u32[]{:S(2)}) %collective-permute-start.15) | collective-permute-done | bytes 131104 | tf_op jit(solution)/shard_map/ppermute | solution.py:32
  100.6 6.4 %collective-permute-done.16.rest_2_ = bf16[2,32,1,8,128]{4,3,2,1,0:T(8,128)(2,1)S(1)} collective-permute-done((bf16[2,32,1,8,128]{4,3,2,1,0:T(8,128)(2,1)S(1)}, bf16[2,32,1,8,128]{4,3,2,1,0:T(8,128)(2,1)S(1)}, u32[]{:S(2)}, u32[]{:S(2)}) %collective-permute-start.16) | collective-permute-done | bytes 131104 | tf_op jit(solution)/shard_map/ppermute | solution.py:32
  107.7 17.7 %place.1 = (bf16[32,4,8,128]{3,2,1,0:T(8,128)(2,1)}, bf16[32,4,8,128]{3,2,1,0:T(8,128)(2,1)}) custom-call(s32[2]{0:T(128)} %copy-done.3, bf16[2,32,1,8,128]{4,3,2,1,0:T(8,128)(2,1)} %copy-done.1, bf16[2,32,1,8,128]{4,3,2,1,0:T(8,128)(2,1)} %copy-done.4, bf16[2,32,1,8,128]{4,3,2,1,0:T(8,128)(2,1)} %copy-done.5, bf16[2,32,1,8,128]{4,3,2,1,0:T(8,128)(2,1)} %copy-done.6), custom_call_target="tpu_custom_call" | custom-call | tf_op jit(solution)/shard_map/place/pallas_call | solution.py:316
  (35 shorter events, 5.1 us)
Async XLA Ops:
  0.6 28.5 %collective-permute-start.3 = (bf16[128,4,8,128]{3,2,1,0:T(8,128)(2,1)}, bf16[128,4,8,128]{3,2,1,0:T(8,128)(2,1)S(1)}, u32[]{:S(2)}, u32[]{:S(2)}) collective-permute-start(bf16[128,4,8,128]{3,2,1,0:T(8,128)(2,1)} %bitcast.3), channel_id=1, source_target_pairs={{0,7},{1,0},{2,1},{3,2},{4,3},{5,4},{6,5},{7,6},{8,15},{9,8},{10,9... | collective-permute-start | bytes 3145736 | tf_op jit(solution)/shard_map/ppermute | solution.py:37
  4.0 25.1 %collective-permute-start.2 = (bf16[128,4,8,128]{3,2,1,0:T(8,128)(2,1)}, bf16[128,4,8,128]{3,2,1,0:T(8,128)(2,1)S(1)}, u32[]{:S(2)}, u32[]{:S(2)}) collective-permute-start(bf16[128,4,8,128]{3,2,1,0:T(8,128)(2,1)} %bitcast.4), channel_id=1, source_target_pairs={{0,1},{1,2},{2,3},{3,4},{4,5},{5,6},{6,7},{7,0},{8,9},{9,10},{10,1... | collective-permute-start | bytes 3145736 | tf_op jit(solution)/shard_map/ppermute | solution.py:37
  4.0 25.1 %collective-permute-start = (f32[4,8,128]{2,1,0:T(8,128)}, f32[4,8,128]{2,1,0:T(8,128)S(1)}, u32[]{:S(2)}, u32[]{:S(2)}) collective-permute-start(f32[4,8,128]{2,1,0:T(8,128)} %flow_ref.1), channel_id=1, source_target_pairs={{0,1},{1,2},{2,3},{3,4},{4,5},{5,6},{6,7},{7,0},{8,9},{9,10},{10,1... | collective-permute-start | bytes 49160 | tf_op jit(solution)/shard_map/ppermute | solution.py:37
  4.0 25.1 %collective-permute-start.1 = (f32[4,8,128]{2,1,0:T(8,128)}, f32[4,8,128]{2,1,0:T(8,128)S(1)}, u32[]{:S(2)}, u32[]{:S(2)}) collective-permute-start(f32[4,8,128]{2,1,0:T(8,128)} %flow_ref.1), channel_id=1, source_target_pairs={{0,7},{1,0},{2,1},{3,2},{4,3},{5,4},{6,5},{7,6},{8,15},{9,8},{10,9... | collective-permute-start | bytes 49160 | tf_op jit(solution)/shard_map/ppermute | solution.py:37
  6.7 22.5 %copy-start.2 = (f32[4,8,128]{2,1,0:T(8,128)S(1)}, f32[4,8,128]{2,1,0:T(8,128)}, u32[]{:S(2)}) copy-start(f32[4,8,128]{2,1,0:T(8,128)} %flow_ref.1) | copy-start | bytes 49156
  6.8 77.3 %copy-start.3 = (s32[2]{0:T(128)}, s32[2]{0:T(128)S(1)}, u32[]{:S(2)}) copy-start(s32[2]{0:T(128)S(1)} %pad_add_fusion.where_ref) | copy-start | bytes 28
  29.2 1.2 copy-start
  40.4 9.1 %collective-permute-start.4 = (bf16[8,128,128]{2,1,0:T(8,128)(2,1)S(1)}, bf16[8,128,128]{2,1,0:T(8,128)(2,1)S(1)}, u32[]{:S(2)}, u32[]{:S(2)}) collective-permute-start(bf16[8,128,128]{2,1,0:T(8,128)(2,1)S(1)} %get-tuple-element.14), channel_id=1, source_target_pairs={{0,8},{8,0},{16,24},{24,16},{1,9},{9,1},{17,25},{25,17},{2,10},{10... | collective-permute-start | bytes 786440 | tf_op jit(solution)/shard_map/ppermute | solution.py:32
  42.0 20.2 %collective-permute-start.5 = (bf16[8,128,128]{2,1,0:T(8,128)(2,1)S(1)}, bf16[8,128,128]{2,1,0:T(8,128)(2,1)S(1)}, u32[]{:S(2)}, u32[]{:S(2)}) collective-permute-start(bf16[8,128,128]{2,1,0:T(8,128)(2,1)S(1)} %get-tuple-element.15), channel_id=1, source_target_pairs={{0,16},{8,24},{16,0},{24,8},{1,17},{9,25},{17,1},{25,9},{2,18},{10... | collective-permute-start | bytes 786440 | tf_op jit(solution)/shard_map/ppermute | solution.py:32
  44.6 17.6 %collective-permute-start.6 = (bf16[8,128,128]{2,1,0:T(8,128)(2,1)S(1)}, bf16[8,128,128]{2,1,0:T(8,128)(2,1)S(1)}, u32[]{:S(2)}, u32[]{:S(2)}) collective-permute-start(bf16[8,128,128]{2,1,0:T(8,128)(2,1)S(1)} %get-tuple-element.16), channel_id=1, source_target_pairs={{0,24},{8,16},{16,8},{24,0},{1,25},{9,17},{17,9},{25,1},{2,26},{10... | collective-permute-start | bytes 786440 | tf_op jit(solution)/shard_map/ppermute | solution.py:32
  63.3 1.4 %collective-permute-start.7 = (f32[64,384]{1,0:T(8,128)S(1)}, f32[64,384]{1,0:T(8,128)S(1)}, u32[]{:S(2)}, u32[]{:S(2)}) collective-permute-start(f32[64,384]{1,0:T(8,128)S(1)} %get-tuple-element.18), channel_id=1, source_target_pairs={{0,1},{1,0},{2,3},{3,2},{4,5},{5,4},{6,7},{7,6},{8,9},{9,8},{10,11... | collective-permute-start | bytes 294920 | tf_op jit(solution)/shard_map/ppermute | solution.py:32
  64.7 5.1 %collective-permute-start.10 = (bf16[64,384]{1,0:T(8,128)(2,1)S(1)}, bf16[64,384]{1,0:T(8,128)(2,1)S(1)}, u32[]{:S(2)}, u32[]{:S(2)}) collective-permute-start(bf16[64,384]{1,0:T(8,128)(2,1)S(1)} %get-tuple-element.24), channel_id=1, source_target_pairs={{0,6},{1,7},{2,4},{3,5},{4,2},{5,3},{6,0},{7,1},{8,14},{9,15},{10,... | collective-permute-start | bytes 147464 | tf_op jit(solution)/shard_map/ppermute | solution.py:32
  67.3 4.1 %collective-permute-start.9 = (bf16[64,384]{1,0:T(8,128)(2,1)S(1)}, bf16[64,384]{1,0:T(8,128)(2,1)S(1)}, u32[]{:S(2)}, u32[]{:S(2)}) collective-permute-start(bf16[64,384]{1,0:T(8,128)(2,1)S(1)} %get-tuple-element.24), channel_id=1, source_target_pairs={{0,4},{1,5},{2,6},{3,7},{4,0},{5,1},{6,2},{7,3},{8,12},{9,13},{10,... | collective-permute-start | bytes 147464 | tf_op jit(solution)/shard_map/ppermute | solution.py:32
  67.3 4.1 %collective-permute-start.8 = (bf16[64,384]{1,0:T(8,128)(2,1)S(1)}, bf16[64,384]{1,0:T(8,128)(2,1)S(1)}, u32[]{:S(2)}, u32[]{:S(2)}) collective-permute-start(bf16[64,384]{1,0:T(8,128)(2,1)S(1)} %get-tuple-element.24), channel_id=1, source_target_pairs={{0,2},{1,3},{2,0},{3,1},{4,6},{5,7},{6,4},{7,5},{8,10},{9,11},{10,... | collective-permute-start | bytes 147464 | tf_op jit(solution)/shard_map/ppermute | solution.py:32
  71.4 7.4 %collective-permute-start.13 = (bf16[64,384]{1,0:T(8,128)(2,1)S(1)}, bf16[64,384]{1,0:T(8,128)(2,1)S(1)}, u32[]{:S(2)}, u32[]{:S(2)}) collective-permute-start(bf16[64,384]{1,0:T(8,128)(2,1)S(1)} %fusion.4), channel_id=1, source_target_pairs={{0,24},{8,16},{16,8},{24,0},{1,25},{9,17},{17,9},{25,1},{2,26},{10... | collective-permute-start | bytes 147464 | tf_op jit(solution)/shard_map/ppermute | solution.py:32
  73.9 7.8 %collective-permute-start.12 = (bf16[64,384]{1,0:T(8,128)(2,1)S(1)}, bf16[64,384]{1,0:T(8,128)(2,1)S(1)}, u32[]{:S(2)}, u32[]{:S(2)}) collective-permute-start(bf16[64,384]{1,0:T(8,128)(2,1)S(1)} %fusion.4), channel_id=1, source_target_pairs={{0,16},{8,24},{16,0},{24,8},{1,17},{9,25},{17,1},{25,9},{2,18},{10... | collective-permute-start | bytes 147464 | tf_op jit(solution)/shard_map/ppermute | solution.py:32
  78.6 4.1 %collective-permute-start.11 = (bf16[64,384]{1,0:T(8,128)(2,1)S(1)}, bf16[64,384]{1,0:T(8,128)(2,1)S(1)}, u32[]{:S(2)}, u32[]{:S(2)}) collective-permute-start(bf16[64,384]{1,0:T(8,128)(2,1)S(1)} %fusion.4), channel_id=1, source_target_pairs={{0,8},{8,0},{16,24},{24,16},{1,9},{9,1},{17,25},{25,17},{2,10},{10... | collective-permute-start | bytes 147464 | tf_op jit(solution)/shard_map/ppermute | solution.py:32
  82.8 1.4 %collective-permute-start.14 = (f32[64,384]{1,0:T(8,128)S(1)}, f32[64,384]{1,0:T(8,128)S(1)}, u32[]{:S(2)}, u32[]{:S(2)}) collective-permute-start(f32[64,384]{1,0:T(8,128)S(1)} %add_multiply_fusion.mine_ref), channel_id=1, source_target_pairs={{0,1},{1,0},{2,3},{3,2},{4,5},{5,4},{6,7},{7,6},{8,9},{9,8},{10,11... | collective-permute-start | bytes 294920 | tf_op jit(solution)/shard_map/ppermute | solution.py:32
  92.4 0.7 copy-start.1
  93.0 7.5 %collective-permute-start.15 = (bf16[2,32,1,8,128]{4,3,2,1,0:T(8,128)(2,1)S(1)}, bf16[2,32,1,8,128]{4,3,2,1,0:T(8,128)(2,1)S(1)}, u32[]{:S(2)}, u32[]{:S(2)}) collective-permute-start(bf16[2,32,1,8,128]{4,3,2,1,0:T(8,128)(2,1)S(1)} %get-tuple-element.21), channel_id=1, source_target_pairs={{0,8},{8,0},{16,24},{24,16},{1,9},{9,1},{17,25},{25,17},{2,10},{10... | collective-permute-start | bytes 393224 | tf_op jit(solution)/shard_map/ppermute | solution.py:32
  94.1 12.9 %collective-permute-start.16 = (bf16[2,32,1,8,128]{4,3,2,1,0:T(8,128)(2,1)S(1)}, bf16[2,32,1,8,128]{4,3,2,1,0:T(8,128)(2,1)S(1)}, u32[]{:S(2)}, u32[]{:S(2)}) collective-permute-start(bf16[2,32,1,8,128]{4,3,2,1,0:T(8,128)(2,1)S(1)} %get-tuple-element.22), channel_id=1, source_target_pairs={{0,16},{8,24},{16,0},{24,8},{1,17},{9,25},{17,1},{25,9},{2,18},{10... | collective-permute-start | bytes 393224 | tf_op jit(solution)/shard_map/ppermute | solution.py:32
  96.1 10.9 %collective-permute-start.17 = (bf16[2,32,1,8,128]{4,3,2,1,0:T(8,128)(2,1)S(1)}, bf16[2,32,1,8,128]{4,3,2,1,0:T(8,128)(2,1)S(1)}, u32[]{:S(2)}, u32[]{:S(2)}) collective-permute-start(bf16[2,32,1,8,128]{4,3,2,1,0:T(8,128)(2,1)S(1)} %get-tuple-element.23), channel_id=1, source_target_pairs={{0,24},{8,16},{16,8},{24,0},{1,25},{9,17},{17,9},{25,1},{2,26},{10... | collective-permute-start | bytes 393224 | tf_op jit(solution)/shard_map/ppermute | solution.py:32
  100.6 6.4 %copy-start.4 = (bf16[2,32,1,8,128]{4,3,2,1,0:T(8,128)(2,1)}, bf16[2,32,1,8,128]{4,3,2,1,0:T(8,128)(2,1)S(1)}, u32[]{:S(2)}) copy-start(bf16[2,32,1,8,128]{4,3,2,1,0:T(8,128)(2,1)S(1)} %collective-permute-done.15.rest_1_) | copy-start | bytes 393220
  107.0 0.7 copy-start.6
  (1 other events, 0.7 us)

commit v2 on v1

--- a/solution.py
+++ b/solution.py
@@ -9,7 +9,9 @@
 from jax.sharding import PartitionSpec as P
 
 SECTIONS = 4
-CHUNKS = 1
+CHUNKS = (1, 1)
+ORDER = (1, 2, 3)
+UNROLL = 2
 
 diffuse_x = 0.35
 diffuse_side = 0.05
@@ -19,6 +21,7 @@
 vmem = pl.BlockSpec(memory_space=pltpu.VMEM)
 smem = pl.BlockSpec(memory_space=pltpu.SMEM)
 anywhere = pl.BlockSpec(memory_space=pl.ANY)
+hbm = pl.BlockSpec(memory_space=pltpu.HBM)
 f32 = jnp.float32
 bf16 = jnp.bfloat16
 
@@ -37,55 +40,106 @@
     return lax.ppermute(value, axis, [(i, (i + step) % count) for i in range(count)])
 
 
-def sections_kernel(groups, rows, where_ref, flow_ref, flow_lo, flow_hi, ring_ref,
-                    own_ref, lo_ref, hi_ref, *rest):
-    outs = rest[:groups]
-    flow_ext, plus, minus, stage, first, second = rest[groups:]
-    snaps, _, ny, nz = own_ref.shape
+def pack_kernel(start, with_flow, flow_ref, field_ref, out, block, stage, sem):
+    step, rows, ny, nz = block.shape
+    copy = pltpu.make_async_copy(field_ref.at[pl.ds(start, step)], block, sem)
+    copy.start()
+    if with_flow:
+        per = step // (rows * ny)
+        left = flow_ref[...].reshape(rows * ny, nz)
+        for p in range(3):
+            part = left.astype(bf16)
+            left = left - part.astype(f32)
+            at = p % per * rows * ny
+            out[rows * ny + p // per, at:at + rows * ny] = part
+    copy.wait()
+    for r in range(rows):
+        stage[r % 2] = block[:, r].astype(f32).reshape(step * ny, nz)
+        for y in range(ny):
+            out[r * ny + y] = stage[r % 2, pl.ds(y, step, stride=ny), :].astype(bf16)
+
+
+def pack(flow, field, start, step, with_flow):
+    _, rows, ny, nz = field.shape
+    extra = -(-3 // (step // (rows * ny))) if with_flow else 0
+    return pl.pallas_call(
+        functools.partial(pack_kernel, start, with_flow),
+        out_shape=jax.ShapeDtypeStruct((rows * ny + extra, step, nz), bf16),
+        in_specs=[vmem, hbm],
+        out_specs=vmem,
+        scratch_shapes=[
+            pltpu.VMEM((step, rows, ny, nz), bf16),
+            pltpu.VMEM((2, step * ny, nz), f32),
+            pltpu.SemaphoreType.DMA(()),
+        ],
+        compiler_params=pltpu.CompilerParams(vmem_limit_bytes=VMEM_LIMIT),
+        name="pack",
+    )(flow, field)
+
+
+def sections_kernel(groups, rows, ny, lead, where_ref, ring_ref, *rest):
     reach = SECTIONS
+    total = rows + 2 * reach
     me = where_ref[0]
-    adj = (me == groups - 1).astype(jnp.int32)
-    sign = jnp.where(me == groups - 1, f32(0.5), f32(-0.5))
-    flow_ext[0:reach] = flow_lo[...]
-    flow_ext[reach:reach + rows] = flow_ref[...]
-    flow_ext[reach + rows:] = flow_hi[...]
-    total = rows + 2 * reach
+    if lead:
+        flow_ref, own_ref, lo_ref, hi_ref = rest[:4]
+        outs = rest[4:4 + groups]
+        plus, minus, flow_ext, first, second = rest[4 + groups:]
+    else:
+        plus, minus, own_ref, lo_ref, hi_ref, _ = rest[:6]
+        outs = rest[6:6 + groups]
+        first, second = rest[6 + groups:]
+    step, nz = own_ref.shape[1:]
+    if lead:
+        adj = (me == groups - 1).astype(jnp.int32)
+        sign = jnp.where(me == groups - 1, f32(0.5), f32(-0.5))
+        per = step // (rows * ny)
+
+        def flow_of(ref):
+            flow = None
+            for p in (2, 1, 0):
+                at = p % per * rows * ny
+                part = ref[rows * ny + p // per, at:at + rows * ny].astype(f32)
+                flow = part if flow is None else flow + part
+            return flow.reshape(rows, ny, nz)
+
+        flow_ext[0:reach] = flow_of(lo_ref)[rows - reach:]
+        flow_ext[reach:reach + rows] = flow_ref[...]
+        flow_ext[reach + rows:] = flow_of(hi_ref)[:reach]
+        for e in range(1, total - 1):
+            plus[e] = diffuse_x + sign * flow_ext[e + adj]
+            minus[e] = diffuse_x - sign * flow_ext[e - adj]
+    ring = ring_ref[...]
+
+    def entry(e, y):
+        if e < reach:
+            return lo_ref[(rows - reach + e) * ny + y]
+        if e < reach + rows:
+            return own_ref[(e - reach) * ny + y]
+        return hi_ref[(e - reach - rows) * ny + y]
+
+    def one(src, e, y):
+        get = entry if src is None else lambda at, w: src[at, w]
+        side = jnp.dot(get(e, y), ring, preferred_element_type=f32)
+        side = side + get(e, (y + 1) % ny).astype(f32) + get(e, (y - 1) % ny).astype(f32)
+        updated = diffuse_side * side
+        updated = updated + plus[e, y:y + 1, :] * get(e + 1, y).astype(f32)
+        updated = updated + minus[e, y:y + 1, :] * get(e - 1, y).astype(f32)
+        return updated.astype(bf16)
+
     for e in range(1, total - 1):
-        plus[e] = diffuse_x + sign * flow_ext[e + adj]
-        minus[e] = diffuse_x - sign * flow_ext[e - adj]
-
-    def turn(source, base, count):
-        def body(r, carry):
-            block = source[:, pl.ds(r, 1)]
-            stage[...] = block.astype(f32).reshape(snaps * ny, nz)
-            for y in range(ny):
-                first[base + r, y] = stage[pl.ds(y, snaps, stride=ny), :].astype(bf16)
-            return carry
-        lax.fori_loop(0, count, body, 0)
-
-    turn(lo_ref, 0, reach)
-    turn(own_ref, reach, rows)
-    turn(hi_ref, reach + rows, reach)
-    ring = ring_ref[...]
-
-    def one(src, e, y):
-        side = jnp.dot(src[e, y], ring, preferred_element_type=f32)
-        side = side + src[e, (y + 1) % ny].astype(f32) + src[e, (y - 1) % ny].astype(f32)
-        updated = diffuse_side * side
-        updated = updated + plus[e][y:y + 1] * src[e + 1, y].astype(f32)
-        updated = updated + minus[e][y:y + 1] * src[e - 1, y].astype(f32)
-        return updated.astype(bf16)
-
+        for y in range(ny):
+            first[e, y] = one(None, e, y)
     bufs = (first, second)
-    for s in range(1, SECTIONS):
-        src, dst = bufs[(s - 1) % 2], bufs[s % 2]
+    for s in range(2, SECTIONS):
+        src, dst = bufs[s % 2], bufs[(s - 1) % 2]
 
         def body(e, carry, src=src, dst=dst):
             for y in range(ny):
                 dst[e, y] = one(src, e, y)
             return carry
-        lax.fori_loop(s, total - s, body, 0)
-    src = bufs[(SECTIONS - 1) % 2]
+        lax.fori_loop(s, total - s, body, 0, unroll=UNROLL)
+    src = bufs[SECTIONS % 2]
     share = rows // groups
     for k in range(groups):
         for j in range(share):
@@ -94,40 +148,46 @@
                 outs[k][j * ny + y] = one(src, e, y)
 
 
-def sections(where, flow, flow_lo, flow_hi, ring, own, lo, hi, groups):
-    snaps, rows, ny, nz = own.shape
+def sections(where, ring, coefs, own, lo, hi, groups, flow, before):
+    rows, ny, nz = flow.shape
+    step = own.shape[1]
     share = rows // groups
     total = rows + 2 * SECTIONS
-    return pl.pallas_call(
-        functools.partial(sections_kernel, groups, rows),
-        out_shape=[jax.ShapeDtypeStruct((share * ny, snaps, nz), bf16)] * groups,
-        in_specs=[smem] + [vmem] * 7,
-        out_specs=[vmem] * groups,
-        scratch_shapes=[
-            pltpu.VMEM((total, ny, nz), f32),
-            pltpu.VMEM((total, ny, nz), f32),
-            pltpu.VMEM((total, ny, nz), f32),
-            pltpu.VMEM((snaps * ny, nz), f32),
-            pltpu.VMEM((total, ny, snaps, nz), bf16),
-            pltpu.VMEM((total, ny, snaps, nz), bf16),
-        ],
+    lead = coefs is None
+    out = [jax.ShapeDtypeStruct((share * ny, step, nz), bf16)] * groups
+    scratch = [pltpu.VMEM((total, ny, step, nz), bf16)] * 2
+    if lead:
+        out += [jax.ShapeDtypeStruct((total, ny, nz), f32)] * 2
+        scratch = [pltpu.VMEM((total, ny, nz), f32)] + scratch
+        coefs = [flow]
+    outs = pl.pallas_call(
+        functools.partial(sections_kernel, groups, rows, ny, lead),
+        out_shape=out,
+        in_specs=[smem] + [vmem] * (4 + len(coefs)) + [anywhere] * len(before),
+        out_specs=[vmem] * len(out),
+        scratch_shapes=scratch,
         compiler_params=pltpu.CompilerParams(vmem_limit_bytes=VMEM_LIMIT),
+        cost_estimate=pl.CostEstimate(
+            flops=8 * SECTIONS * step * total * ny * nz, bytes_accessed=8 * step * rows * ny * nz, transcendentals=0),
         name="sections",
-    )(where, flow, flow_lo, flow_hi, ring, own, lo, hi)
+    )(where, ring, *coefs, own, lo, hi, *before)
+    return outs[:groups], outs[groups:]
 
 
 def coupling_kernel(groups, chunks, where_ref, *rest):
     blocks = rest[: groups * chunks]
     fields, keep, send, scratch, sem = rest[groups * chunks:]
     me, half = where_ref[0], where_ref[1]
-    step = blocks[0].shape[1]
     copies = []
     for k in range(groups):
+        start = 0
         for c in range(chunks):
+            step = blocks[c].shape[1]
             copies.append(pltpu.make_async_copy(
                 blocks[k * chunks + c],
-                fields.at[peer(me, k), :, pl.ds(c * step, step)],
+                fields.at[peer(me, k), :, pl.ds(start, step)],
                 sem.at[k * chunks + c]))
+            start += step
     for copy in copies:
         copy.start()
     for copy in copies:
@@ -151,8 +211,8 @@
 
 
 def coupling(where, blocks, groups, chunks):
-    parts, step, nz = blocks[0].shape
-    snaps = step * chunks
+    parts, _, nz = blocks[0].shape
+    snaps = sum(block.shape[1] for block in blocks[:chunks])
     wide = (groups - 1) * snaps
     return pl.pallas_call(
         functools.partial(coupling_kernel, groups, chunks),
@@ -294,20 +354,13 @@
 
 def place_kernel(groups, where_ref, *rest):
     blocks = rest[:groups]
-    direct, adjoint, sem = rest[groups:]
+    outs = rest[groups:]
     me = where_ref[0]
     layers = blocks[0].shape[2]
-    copies = []
     for k in range(groups):
-        for which, out in enumerate((direct, adjoint)):
-            copies.append(pltpu.make_async_copy(
-                blocks[k].at[which],
-                out.at[:, pl.ds(peer(me, k) * layers, layers)],
-                sem.at[2 * k + which]))
-    for copy in copies:
-        copy.start()
-    for copy in copies:
-        copy.wait()
+        for which in range(2):
+            for layer in range(layers):
+                outs[which][:, peer(me, k) * layers + layer] = blocks[k][which, :, layer]
 
 
 def place(where, blocks, groups):
@@ -316,9 +369,8 @@
     return pl.pallas_call(
         functools.partial(place_kernel, groups),
         out_shape=[out, out],
-        in_specs=[smem] + [anywhere] * groups,
-        out_specs=[anywhere] * 2,
-        scratch_shapes=[pltpu.SemaphoreType.DMA((2 * groups,))],
+        in_specs=[smem] + [vmem] * groups,
+        out_specs=[vmem] * 2,
         name="place",
     )(where, *blocks)
 
@@ -331,23 +383,25 @@
     me = lax.axis_index("grp")
     half = lax.axis_index("slab") % 2
     where = jnp.stack([me, half]).astype(jnp.int32)
-    flow_lo = shift(base_flow[rows - SECTIONS:], "slab", 1)
-    flow_hi = shift(base_flow[:SECTIONS], "slab", -1)
     at = jnp.arange(nz)
     gap = (at[:, None] - at[None, :]) % nz
     ring = (2 * (gap == 0) + (gap == 1) + (gap == nz - 1)).astype(bf16)
-    step = snaps // CHUNKS
-    blocks = [[None] * CHUNKS for _ in range(groups)]
-    for c in range(CHUNKS):
-        own = field[c * step:(c + 1) * step]
-        lo = shift(own[:, rows - SECTIONS:], "slab", 1)
-        hi = shift(own[:, :SECTIONS], "slab", -1)
-        parts = sections(where, base_flow, flow_lo, flow_hi, ring, own, lo, hi, groups)
+    sizes = [snaps * part // sum(CHUNKS) for part in CHUNKS]
+    chunks = len(sizes)
+    blocks = [[None] * chunks for _ in range(groups)]
+    coefs = None
+    for c in range(chunks):
+        own = pack(base_flow, field, sum(sizes[:c]), sizes[c], c == 0)
+        lo = shift(own, "slab", 1)
+        hi = shift(own, "slab", -1)
+        before = [blocks[ORDER[0]][c - 1]] if c else []
+        parts, made = sections(where, ring, coefs, own, lo, hi, groups, base_flow, before)
+        coefs = coefs or made
         blocks[0][c] = parts[0]
-        for k in range(1, groups):
+        for k in ORDER:
             blocks[k][c] = swap(parts[k], "grp", k)
-    flat = [blocks[k][c] for k in range(groups) for c in range(CHUNKS)]
-    fields, keep, send = coupling(where, flat, groups, CHUNKS)
+    flat = [blocks[k][c] for k in range(groups) for c in range(chunks)]
+    fields, keep, send = coupling(where, flat, groups, chunks)
     total = keep + swap(send, "slab", 1)
     bit = 2
     while bit < slabs:

time: 126 us -> 97 us (0.77)
  waiting for transfers between devices: 59 us -> 40.3 us
  Pallas kernels: 36.9 us -> 20.6 us
  starting transfers between devices: 26 us -> 31.5 us
    pallas_call x1, Pallas kernels: 17.7 us -> 1.98 us  [place(): pl.pallas_call(functools.partial(place_kernel, groups), out_shape=[out, o...]
    ppermute x4, waiting for transfers between devices: 22.3 us -> 10.7 us  [shift(): lax.ppermute(value, axis, [(i, (i + step) % count) for i in range(count)])]
    ppermute x14 -> x17, waiting for transfers between devices: 36.6 us -> 29.6 us  [swap(): return lax.ppermute(value, axis, [(i, i ^ step) for i in range(count)])]
    ppermute x14 -> x17, starting transfers between devices: 19.9 us -> 25.4 us  [swap(): return lax.ppermute(value, axis, [(i, i ^ step) for i in range(count)])]
    pallas_call x1 -> x4, Pallas kernels: 9.94 us -> 9.22 us  [the longest x2 8.65 us: sections(): pl.pallas_call(functools.partial(sections_kernel, groups, rows, ny, lead)...]
    unnamed x14 -> x16, local copies, waits for them, and re-layouts: 2.57 us -> 3.28 us
  transfers between devices with their start and end apart: 18 -> 21, of which waited for: 11 -> 15; matrix products, arithmetic and copies ran while one was open for 0% -> 0% of each run, Pallas kernels for 0% -> 9%
where the time goes in v2:
time: 97 us; the launch traced here: 96.8 us
  waiting for transfers between devices  40.3 us (42%)
  starting transfers between devices  31.5 us (32%)
  Pallas kernels  20.6 us (21%)
  local copies, waits for them, and re-layouts  3.28 us (3%)
    ppermute x17, waiting for transfers between devices, swap(): return lax.ppermute(value, axis, [(i, i ^ step) for i in range(count)])  29.6 us
    ppermute x17, starting transfers between devices, swap(): return lax.ppermute(value, axis, [(i, i ^ step) for i in range(count)])  25.4 us
    ppermute x4, waiting for transfers between devices, shift(): lax.ppermute(value, axis, [(i, (i + step) % count) for i in range(count)])  10.7 us
    pallas_call x2, Pallas kernels, sections(): pl.pallas_call(functools.partial(sections_kernel, groups, rows, ny, lead)...  8.65 us
    pallas_call x1, Pallas kernels, modes(): pl.pallas_call(functools.partial(modes_kernel, groups), out_shape=[jax.Sh...  8.23 us
    ppermute x4, starting transfers between devices, shift(): lax.ppermute(value, axis, [(i, (i + step) % count) for i in range(count)])  6.14 us
    unnamed x16, local copies, waits for them, and re-layouts  3.28 us
    pallas_call x1, Pallas kernels, place(): pl.pallas_call(functools.partial(place_kernel, groups), out_shape=[out, o...  1.98 us
  transfers between devices with their start and end apart: 21, of which 15 were waited for; matrix products, arithmetic and copies ran while one was open for 0% of the time, Pallas kernels for 9%

profile of v2, /device:TPU:0, one launch (start us, length us, event | category | flops | bytes accessed | tf_op | source)
XLA Modules:
  0.0 96.8 jit_solution(11818071970147461263)
XLA Ops:
  3.4 2.9 %collective-permute-start.1 = (bf16[34,64,128]{2,1,0:T(8,128)(2,1)S(1)}, bf16[34,64,128]{2,1,0:T(8,128)(2,1)S(1)}, u32[]{:S(2)}, u32[]{:S(2)}) collective-permute-start(bf16[34,64,128]{2,1,0:T(8,128)(2,1)S(1)} %pack.2.rest_1_), channel_id=1, source_target_pairs={{0,7},{1,0},{2,1},{3,2},{4,3},{5,4},{6,5},{7,6},{8,15},{9,8},{10,9... | collective-permute-start | bytes 1671176 | tf_op jit(solution)/shard_map/ppermute | solution.py:40
  6.7 2.6 %collective-permute-start.3 = (bf16[32,64,128]{2,1,0:T(8,128)(2,1)S(1)}, bf16[32,64,128]{2,1,0:T(8,128)(2,1)S(1)}, u32[]{:S(2)}, u32[]{:S(2)}) collective-permute-start(bf16[32,64,128]{2,1,0:T(8,128)(2,1)S(1)} %pack.3.rest_2_), channel_id=1, source_target_pairs={{0,7},{1,0},{2,1},{3,2},{4,3},{5,4},{6,5},{7,6},{8,15},{9,8},{10,9... | collective-permute-start | bytes 1572872 | tf_op jit(solution)/shard_map/ppermute | solution.py:40
  9.4 7.3 %collective-permute-done.rest_2_ = bf16[34,64,128]{2,1,0:T(8,128)(2,1)S(1)} collective-permute-done((bf16[34,64,128]{2,1,0:T(8,128)(2,1)S(1)}, bf16[34,64,128]{2,1,0:T(8,128)(2,1)S(1)}, u32[]{:S(2)}, u32[]{:S(2)}) %collective-permute-start) | collective-permute-done | bytes 557088 | tf_op jit(solution)/shard_map/ppermute | solution.py:40
  16.8 2.6 %collective-permute-done.1.rest_3_ = bf16[34,64,128]{2,1,0:T(8,128)(2,1)S(1)} collective-permute-done((bf16[34,64,128]{2,1,0:T(8,128)(2,1)S(1)}, bf16[34,64,128]{2,1,0:T(8,128)(2,1)S(1)}, u32[]{:S(2)}, u32[]{:S(2)}) %collective-permute-start.1) | collective-permute-done | bytes 557088 | tf_op jit(solution)/shard_map/ppermute | solution.py:40
  19.3 4.4 %sections.2 = (bf16[8,64,128]{2,1,0:T(8,128)(2,1)S(1)}, bf16[8,64,128]{2,1,0:T(8,128)(2,1)S(1)}, bf16[8,64,128]{2,1,0:T(8,128)(2,1)S(1)}, bf16[8,64,128]{2,1,0:T...) custom-call(s32[2]{0:T(128)S(1)} %pad_add_fusion.where_ref, ...), custom_call_target="tpu_custom_call" | custom-call | flops 25165824 | bytes 2097152 | tf_op jit(solution)/shard_map/sections/pallas_call | solution.py:163
  23.7 2.4 %collective-permute-start.4 = (bf16[8,64,128]{2,1,0:T(8,128)(2,1)S(1)}, bf16[8,64,128]{2,1,0:T(8,128)(2,1)S(1)}, u32[]{:S(2)}, u32[]{:S(2)}) collective-permute-start(bf16[8,64,128]{2,1,0:T(8,128)(2,1)S(1)} %get-tuple-element.22), channel_id=1, source_target_pairs={{0,8},{8,0},{16,24},{24,16},{1,9},{9,1},{17,25},{25,17},{2,10},{10... | collective-permute-start | bytes 393224 | tf_op jit(solution)/shard_map/ppermute | solution.py:35
  26.1 2.6 %collective-permute-start.6 = (bf16[8,64,128]{2,1,0:T(8,128)(2,1)S(1)}, bf16[8,64,128]{2,1,0:T(8,128)(2,1)S(1)}, u32[]{:S(2)}, u32[]{:S(2)}) collective-permute-start(bf16[8,64,128]{2,1,0:T(8,128)(2,1)S(1)} %get-tuple-element.25), channel_id=1, source_target_pairs={{0,16},{8,24},{16,0},{24,8},{1,17},{9,25},{17,1},{25,9},{2,18},{10... | collective-permute-start | bytes 393224 | tf_op jit(solution)/shard_map/ppermute | solution.py:35
  29.9 4.3 %sections.3 = (bf16[8,64,128]{2,1,0:T(8,128)(2,1)S(1)}, bf16[8,64,128]{2,1,0:T(8,128)(2,1)S(1)}, bf16[8,64,128]{2,1,0:T(8,128)(2,1)S(1)}, bf16[8,64,128]{2,1,0:T(8,128)(2,1)S(1)}) custom-call(s32[2]{0:T(128)S(1)} %pad_add_fusion.where_ref, bf16[128,128]{1,0:T(8,128)(2,1)S(1)} %add_convert_fusion.ring_ref, f32[12,8,128]{2,1,0:T(8,128)S(1)} %get-tuple-element.20.rest_0_, ...), custom_call_target="tpu_custom_call" | custom-call | flops 25165824 | bytes 2097152 | tf_op jit(solution)/shard_map/sections/pallas_call | solution.py:163
  34.3 2.5 %collective-permute-start.5 = (bf16[8,64,128]{2,1,0:T(8,128)(2,1)S(1)}, bf16[8,64,128]{2,1,0:T(8,128)(2,1)S(1)}, u32[]{:S(2)}, u32[]{:S(2)}) collective-permute-start(bf16[8,64,128]{2,1,0:T(8,128)(2,1)S(1)} %get-tuple-element.24), channel_id=1, source_target_pairs={{0,8},{8,0},{16,24},{24,16},{1,9},{9,1},{17,25},{25,17},{2,10},{10... | collective-permute-start | bytes 393224 | tf_op jit(solution)/shard_map/ppermute | solution.py:35
  36.7 4.1 %collective-permute-start.7 = (bf16[8,64,128]{2,1,0:T(8,128)(2,1)S(1)}, bf16[8,64,128]{2,1,0:T(8,128)(2,1)S(1)}, u32[]{:S(2)}, u32[]{:S(2)}) collective-permute-start(bf16[8,64,128]{2,1,0:T(8,128)(2,1)S(1)} %get-tuple-element.26), channel_id=1, source_target_pairs={{0,16},{8,24},{16,0},{24,8},{1,17},{9,25},{17,1},{25,9},{2,18},{10... | collective-permute-start | bytes 393224 | tf_op jit(solution)/shard_map/ppermute | solution.py:35
  41.6 9.1 %collective-permute-done.7.rest_5_ = bf16[8,64,128]{2,1,0:T(8,128)(2,1)S(1)} collective-permute-done((bf16[8,64,128]{2,1,0:T(8,128)(2,1)S(1)}, bf16[8,64,128]{2,1,0:T(8,128)(2,1)S(1)}, u32[]{:S(2)}, u32[]{:S(2)}) %collective-permute-start.7) | collective-permute-done | bytes 131104 | tf_op jit(solution)/shard_map/ppermute | solution.py:35
  54.9 1.9 %collective-permute-start.13 = (bf16[64,384]{1,0:T(8,128)(2,1)S(1)}, bf16[64,384]{1,0:T(8,128)(2,1)S(1)}, u32[]{:S(2)}, u32[]{:S(2)}) collective-permute-start(bf16[64,384]{1,0:T(8,128)(2,1)S(1)} %get-tuple-element.36), channel_id=1, source_target_pairs={{0,6},{1,7},{2,4},{3,5},{4,2},{5,3},{6,0},{7,1},{8,14},{9,15},{10,... | collective-permute-start | bytes 147464 | tf_op jit(solution)/shard_map/ppermute | solution.py:35
  57.7 2.2 %collective-permute-done.13 = bf16[64,384]{1,0:T(8,128)(2,1)S(1)} collective-permute-done((bf16[64,384]{1,0:T(8,128)(2,1)S(1)}, bf16[64,384]{1,0:T(8,128)(2,1)S(1)}, u32[]{:S(2)}, u32[]{:S(2)}) %collective-permute-start.13) | collective-permute-done | bytes 49184 | tf_op jit(solution)/shard_map/ppermute | solution.py:35
  59.9 3.4 %collective-permute-start.14 = (bf16[64,384]{1,0:T(8,128)(2,1)S(1)}, bf16[64,384]{1,0:T(8,128)(2,1)S(1)}, u32[]{:S(2)}, u32[]{:S(2)}) collective-permute-start(bf16[64,384]{1,0:T(8,128)(2,1)S(1)} %fusion.4), channel_id=1, source_target_pairs={{0,8},{8,0},{16,24},{24,16},{1,9},{9,1},{17,25},{25,17},{2,10},{10... | collective-permute-start | bytes 147464 | tf_op jit(solution)/shard_map/ppermute | solution.py:35
  64.4 1.4 %collective-permute-start.16 = (bf16[64,384]{1,0:T(8,128)(2,1)S(1)}, bf16[64,384]{1,0:T(8,128)(2,1)S(1)}, u32[]{:S(2)}, u32[]{:S(2)}) collective-permute-start(bf16[64,384]{1,0:T(8,128)(2,1)S(1)} %fusion.4), channel_id=1, source_target_pairs={{0,24},{8,16},{16,8},{24,0},{1,25},{9,17},{17,9},{25,1},{2,26},{10... | collective-permute-start | bytes 147464 | tf_op jit(solution)/shard_map/ppermute | solution.py:35
  65.8 3.0 %collective-permute-done.15 = bf16[64,384]{1,0:T(8,128)(2,1)S(1)} collective-permute-done((bf16[64,384]{1,0:T(8,128)(2,1)S(1)}, bf16[64,384]{1,0:T(8,128)(2,1)S(1)}, u32[]{:S(2)}, u32[]{:S(2)}) %collective-permute-start.15) | collective-permute-done | bytes 49184 | tf_op jit(solution)/shard_map/ppermute | solution.py:35
  68.8 1.5 %collective-permute-done.16 = bf16[64,384]{1,0:T(8,128)(2,1)S(1)} collective-permute-done((bf16[64,384]{1,0:T(8,128)(2,1)S(1)}, bf16[64,384]{1,0:T(8,128)(2,1)S(1)}, u32[]{:S(2)}, u32[]{:S(2)}) %collective-permute-start.16) | collective-permute-done | bytes 49184 | tf_op jit(solution)/shard_map/ppermute | solution.py:35
  70.5 1.3 %collective-permute-done.17.other_ref = f32[64,384]{1,0:T(8,128)S(1)} collective-permute-done((f32[64,384]{1,0:T(8,128)S(1)}, f32[64,384]{1,0:T(8,128)S(1)}, u32[]{:S(2)}, u32[]{:S(2)}) %collective-permute-start.17) | collective-permute-done | bytes 98336 | tf_op jit(solution)/shard_map/ppermute | solution.py:35
  71.8 8.2 %modes.1 = (bf16[2,32,1,8,128]{4,3,2,1,0:T(8,128)(2,1)S(1)}, bf16[2,32,1,8,128]{4,3,2,1,0:T(8,128)(2,1)S(1)}, bf16[2,32,1,8,128]{4,3,2,1,0:T(8,128)(2,1)S(1)}, bf16[2,32,1,8,128]{4,3,2,1,0:T(8,128)(2,1)S(1)}) custom-call(s32[2]{0:T(128)S(1)} %pad_add_fusion.where_ref, f32[64,384]{1,0:T(8,128)S(1)} %add_multiply_fusion.mine_ref, ...), custom_call_target="tpu_custom_call" | custom-call | tf_op jit(solution)/shard_map/modes/pallas_call | solution.py:343
  81.2 1.4 %collective-permute-start.19 = (bf16[2,32,1,8,128]{4,3,2,1,0:T(8,128)(2,1)S(1)}, bf16[2,32,1,8,128]{4,3,2,1,0:T(8,128)(2,1)S(1)}, u32[]{:S(2)}, u32[]{:S(2)}) collective-permute-start(bf16[2,32,1,8,128]{4,3,2,1,0:T(8,128)(2,1)S(1)} %get-tuple-element.34), channel_id=1, source_target_pairs={{0,16},{8,24},{16,0},{24,8},{1,17},{9,25},{17,1},{25,9},{2,18},{10... | collective-permute-start | bytes 393224 | tf_op jit(solution)/shard_map/ppermute | solution.py:35
  82.6 2.4 %collective-permute-start.20 = (bf16[2,32,1,8,128]{4,3,2,1,0:T(8,128)(2,1)S(1)}, bf16[2,32,1,8,128]{4,3,2,1,0:T(8,128)(2,1)S(1)}, u32[]{:S(2)}, u32[]{:S(2)}) collective-permute-start(bf16[2,32,1,8,128]{4,3,2,1,0:T(8,128)(2,1)S(1)} %get-tuple-element.35), channel_id=1, source_target_pairs={{0,24},{8,16},{16,8},{24,0},{1,25},{9,17},{17,9},{25,1},{2,26},{10... | collective-permute-start | bytes 393224 | tf_op jit(solution)/shard_map/ppermute | solution.py:35
  85.1 2.8 %collective-permute-done.18.rest_1_ = bf16[2,32,1,8,128]{4,3,2,1,0:T(8,128)(2,1)S(1)} collective-permute-done((bf16[2,32,1,8,128]{4,3,2,1,0:T(8,128)(2,1)S(1)}, bf16[2,32,1,8,128]{4,3,2,1,0:T(8,128)(2,1)S(1)}, u32[]{:S(2)}, u32[]{:S(2)}) %collective-permute-start.18) | collective-permute-done | bytes 131104 | tf_op jit(solution)/shard_map/ppermute | solution.py:35
  87.9 6.2 %collective-permute-done.19.rest_2_ = bf16[2,32,1,8,128]{4,3,2,1,0:T(8,128)(2,1)S(1)} collective-permute-done((bf16[2,32,1,8,128]{4,3,2,1,0:T(8,128)(2,1)S(1)}, bf16[2,32,1,8,128]{4,3,2,1,0:T(8,128)(2,1)S(1)}, u32[]{:S(2)}, u32[]{:S(2)}) %collective-permute-start.19) | collective-permute-done | bytes 131104 | tf_op jit(solution)/shard_map/ppermute | solution.py:35
  94.8 2.0 %place.1 = (bf16[32,4,8,128]{3,2,1,0:T(8,128)(2,1)}, bf16[32,4,8,128]{3,2,1,0:T(8,128)(2,1)}) custom-call(s32[2]{0:T(128)} %copy-done.4, bf16[2,32,1,8,128]{4,3,2,1,0:T(8,128)(2,1)} %copy-done.3, bf16[2,32,1,8,128]{4,3,2,1,0:T(8,128)(2,1)} %copy-done.5, bf16[2,32,1,8,128]{4,3,2,1,0:T(8,128)(2,1)} %copy-done.6, bf16[2,32,1,8,128]{4,3,2,1,0:T(8,128)(2,1)} %copy-done.7), custom_call_target="tpu_custom_call" | custom-call | tf_op jit(solution)/shard_map/place/pallas_call | solution.py:369
  (46 shorter events, 13.5 us)
Async XLA Ops:
  2.9 13.9 %collective-permute-start = (bf16[34,64,128]{2,1,0:T(8,128)(2,1)S(1)}, bf16[34,64,128]{2,1,0:T(8,128)(2,1)S(1)}, u32[]{:S(2)}, u32[]{:S(2)}) collective-permute-start(bf16[34,64,128]{2,1,0:T(8,128)(2,1)S(1)} %pack.2.rest_1_), channel_id=1, source_target_pairs={{0,1},{1,2},{2,3},{3,4},{4,5},{5,6},{6,7},{7,0},{8,9},{9,10},{10,1... | collective-permute-start | bytes 1671176 | tf_op jit(solution)/shard_map/ppermute | solution.py:40
  3.4 16.0 %collective-permute-start.1 = (bf16[34,64,128]{2,1,0:T(8,128)(2,1)S(1)}, bf16[34,64,128]{2,1,0:T(8,128)(2,1)S(1)}, u32[]{:S(2)}, u32[]{:S(2)}) collective-permute-start(bf16[34,64,128]{2,1,0:T(8,128)(2,1)S(1)} %pack.2.rest_1_), channel_id=1, source_target_pairs={{0,7},{1,0},{2,1},{3,2},{4,3},{5,4},{6,5},{7,6},{8,15},{9,8},{10,9... | collective-permute-start | bytes 1671176 | tf_op jit(solution)/shard_map/ppermute | solution.py:40
  6.6 22.1 %collective-permute-start.2 = (bf16[32,64,128]{2,1,0:T(8,128)(2,1)S(1)}, bf16[32,64,128]{2,1,0:T(8,128)(2,1)S(1)}, u32[]{:S(2)}, u32[]{:S(2)}) collective-permute-start(bf16[32,64,128]{2,1,0:T(8,128)(2,1)S(1)} %pack.3.rest_2_), channel_id=1, source_target_pairs={{0,1},{1,2},{2,3},{3,4},{4,5},{5,6},{6,7},{7,0},{8,9},{9,10},{10,1... | collective-permute-start | bytes 1572872 | tf_op jit(solution)/shard_map/ppermute | solution.py:40
  6.7 22.9 %collective-permute-start.3 = (bf16[32,64,128]{2,1,0:T(8,128)(2,1)S(1)}, bf16[32,64,128]{2,1,0:T(8,128)(2,1)S(1)}, u32[]{:S(2)}, u32[]{:S(2)}) collective-permute-start(bf16[32,64,128]{2,1,0:T(8,128)(2,1)S(1)} %pack.3.rest_2_), channel_id=1, source_target_pairs={{0,7},{1,0},{2,1},{3,2},{4,3},{5,4},{6,5},{7,6},{8,15},{9,8},{10,9... | collective-permute-start | bytes 1572872 | tf_op jit(solution)/shard_map/ppermute | solution.py:40
  9.4 62.4 %copy-start.4 = (s32[2]{0:T(128)}, s32[2]{0:T(128)S(1)}, u32[]{:S(2)}) copy-start(s32[2]{0:T(128)S(1)} %pad_add_fusion.where_ref) | copy-start | bytes 28
  9.4 10.0 %copy-start.2 = (f32[4,8,128]{2,1,0:T(8,128)S(1)}, f32[4,8,128]{2,1,0:T(8,128)}, u32[]{:S(2)}) copy-start(f32[4,8,128]{2,1,0:T(8,128)} %flow_ref.3) | copy-start | bytes 49156
  23.7 6.2 %collective-permute-start.4 = (bf16[8,64,128]{2,1,0:T(8,128)(2,1)S(1)}, bf16[8,64,128]{2,1,0:T(8,128)(2,1)S(1)}, u32[]{:S(2)}, u32[]{:S(2)}) collective-permute-start(bf16[8,64,128]{2,1,0:T(8,128)(2,1)S(1)} %get-tuple-element.22), channel_id=1, source_target_pairs={{0,8},{8,0},{16,24},{24,16},{1,9},{9,1},{17,25},{25,17},{2,10},{10... | collective-permute-start | bytes 393224 | tf_op jit(solution)/shard_map/ppermute | solution.py:35
  26.1 14.7 %collective-permute-start.6 = (bf16[8,64,128]{2,1,0:T(8,128)(2,1)S(1)}, bf16[8,64,128]{2,1,0:T(8,128)(2,1)S(1)}, u32[]{:S(2)}, u32[]{:S(2)}) collective-permute-start(bf16[8,64,128]{2,1,0:T(8,128)(2,1)S(1)} %get-tuple-element.25), channel_id=1, source_target_pairs={{0,16},{8,24},{16,0},{24,8},{1,17},{9,25},{17,1},{25,9},{2,18},{10... | collective-permute-start | bytes 393224 | tf_op jit(solution)/shard_map/ppermute | solution.py:35
  28.7 12.1 %collective-permute-start.8 = (bf16[8,64,128]{2,1,0:T(8,128)(2,1)S(1)}, bf16[8,64,128]{2,1,0:T(8,128)(2,1)S(1)}, u32[]{:S(2)}, u32[]{:S(2)}) collective-permute-start(bf16[8,64,128]{2,1,0:T(8,128)(2,1)S(1)} %get-tuple-element.27), channel_id=1, source_target_pairs={{0,24},{8,16},{16,8},{24,0},{1,25},{9,17},{17,9},{25,1},{2,26},{10... | collective-permute-start | bytes 393224 | tf_op jit(solution)/shard_map/ppermute | solution.py:35
  34.3 7.3 %collective-permute-start.5 = (bf16[8,64,128]{2,1,0:T(8,128)(2,1)S(1)}, bf16[8,64,128]{2,1,0:T(8,128)(2,1)S(1)}, u32[]{:S(2)}, u32[]{:S(2)}) collective-permute-start(bf16[8,64,128]{2,1,0:T(8,128)(2,1)S(1)} %get-tuple-element.24), channel_id=1, source_target_pairs={{0,8},{8,0},{16,24},{24,16},{1,9},{9,1},{17,25},{25,17},{2,10},{10... | collective-permute-start | bytes 393224 | tf_op jit(solution)/shard_map/ppermute | solution.py:35
  36.7 14.0 %collective-permute-start.7 = (bf16[8,64,128]{2,1,0:T(8,128)(2,1)S(1)}, bf16[8,64,128]{2,1,0:T(8,128)(2,1)S(1)}, u32[]{:S(2)}, u32[]{:S(2)}) collective-permute-start(bf16[8,64,128]{2,1,0:T(8,128)(2,1)S(1)} %get-tuple-element.26), channel_id=1, source_target_pairs={{0,16},{8,24},{16,0},{24,8},{1,17},{9,25},{17,1},{25,9},{2,18},{10... | collective-permute-start | bytes 393224 | tf_op jit(solution)/shard_map/ppermute | solution.py:35
  40.8 9.9 %collective-permute-start.9 = (bf16[8,64,128]{2,1,0:T(8,128)(2,1)S(1)}, bf16[8,64,128]{2,1,0:T(8,128)(2,1)S(1)}, u32[]{:S(2)}, u32[]{:S(2)}) collective-permute-start(bf16[8,64,128]{2,1,0:T(8,128)(2,1)S(1)} %get-tuple-element.28), channel_id=1, source_target_pairs={{0,24},{8,16},{16,8},{24,0},{1,25},{9,17},{17,9},{25,1},{2,26},{10... | collective-permute-start | bytes 393224 | tf_op jit(solution)/shard_map/ppermute | solution.py:35
  51.9 1.4 %collective-permute-start.10 = (f32[64,384]{1,0:T(8,128)S(1)}, f32[64,384]{1,0:T(8,128)S(1)}, u32[]{:S(2)}, u32[]{:S(2)}) collective-permute-start(f32[64,384]{1,0:T(8,128)S(1)} %get-tuple-element.30), channel_id=1, source_target_pairs={{0,1},{1,0},{2,3},{3,2},{4,5},{5,4},{6,7},{7,6},{8,9},{9,8},{10,11... | collective-permute-start | bytes 294920 | tf_op jit(solution)/shard_map/ppermute | solution.py:35
  53.3 4.2 %collective-permute-start.11 = (bf16[64,384]{1,0:T(8,128)(2,1)S(1)}, bf16[64,384]{1,0:T(8,128)(2,1)S(1)}, u32[]{:S(2)}, u32[]{:S(2)}) collective-permute-start(bf16[64,384]{1,0:T(8,128)(2,1)S(1)} %get-tuple-element.36), channel_id=1, source_target_pairs={{0,2},{1,3},{2,0},{3,1},{4,6},{5,7},{6,4},{7,5},{8,10},{9,11},{10,... | collective-permute-start | bytes 147464 | tf_op jit(solution)/shard_map/ppermute | solution.py:35
  53.7 4.1 %collective-permute-start.12 = (bf16[64,384]{1,0:T(8,128)(2,1)S(1)}, bf16[64,384]{1,0:T(8,128)(2,1)S(1)}, u32[]{:S(2)}, u32[]{:S(2)}) collective-permute-start(bf16[64,384]{1,0:T(8,128)(2,1)S(1)} %get-tuple-element.36), channel_id=1, source_target_pairs={{0,4},{1,5},{2,6},{3,7},{4,0},{5,1},{6,2},{7,3},{8,12},{9,13},{10,... | collective-permute-start | bytes 147464 | tf_op jit(solution)/shard_map/ppermute | solution.py:35
  54.9 5.0 %collective-permute-start.13 = (bf16[64,384]{1,0:T(8,128)(2,1)S(1)}, bf16[64,384]{1,0:T(8,128)(2,1)S(1)}, u32[]{:S(2)}, u32[]{:S(2)}) collective-permute-start(bf16[64,384]{1,0:T(8,128)(2,1)S(1)} %get-tuple-element.36), channel_id=1, source_target_pairs={{0,6},{1,7},{2,4},{3,5},{4,2},{5,3},{6,0},{7,1},{8,14},{9,15},{10,... | collective-permute-start | bytes 147464 | tf_op jit(solution)/shard_map/ppermute | solution.py:35
  59.9 5.9 %collective-permute-start.14 = (bf16[64,384]{1,0:T(8,128)(2,1)S(1)}, bf16[64,384]{1,0:T(8,128)(2,1)S(1)}, u32[]{:S(2)}, u32[]{:S(2)}) collective-permute-start(bf16[64,384]{1,0:T(8,128)(2,1)S(1)} %fusion.4), channel_id=1, source_target_pairs={{0,8},{8,0},{16,24},{24,16},{1,9},{9,1},{17,25},{25,17},{2,10},{10... | collective-permute-start | bytes 147464 | tf_op jit(solution)/shard_map/ppermute | solution.py:35
  63.3 5.5 %collective-permute-start.15 = (bf16[64,384]{1,0:T(8,128)(2,1)S(1)}, bf16[64,384]{1,0:T(8,128)(2,1)S(1)}, u32[]{:S(2)}, u32[]{:S(2)}) collective-permute-start(bf16[64,384]{1,0:T(8,128)(2,1)S(1)} %fusion.4), channel_id=1, source_target_pairs={{0,16},{8,24},{16,0},{24,8},{1,17},{9,25},{17,1},{25,9},{2,18},{10... | collective-permute-start | bytes 147464 | tf_op jit(solution)/shard_map/ppermute | solution.py:35
  64.4 6.0 %collective-permute-start.16 = (bf16[64,384]{1,0:T(8,128)(2,1)S(1)}, bf16[64,384]{1,0:T(8,128)(2,1)S(1)}, u32[]{:S(2)}, u32[]{:S(2)}) collective-permute-start(bf16[64,384]{1,0:T(8,128)(2,1)S(1)} %fusion.4), channel_id=1, source_target_pairs={{0,24},{8,16},{16,8},{24,0},{1,25},{9,17},{17,9},{25,1},{2,26},{10... | collective-permute-start | bytes 147464 | tf_op jit(solution)/shard_map/ppermute | solution.py:35
  70.4 1.4 %collective-permute-start.17 = (f32[64,384]{1,0:T(8,128)S(1)}, f32[64,384]{1,0:T(8,128)S(1)}, u32[]{:S(2)}, u32[]{:S(2)}) collective-permute-start(f32[64,384]{1,0:T(8,128)S(1)} %add_multiply_fusion.mine_ref), channel_id=1, source_target_pairs={{0,1},{1,0},{2,3},{3,2},{4,5},{5,4},{6,7},{7,6},{8,9},{9,8},{10,11... | collective-permute-start | bytes 294920 | tf_op jit(solution)/shard_map/ppermute | solution.py:35
  80.7 7.2 %collective-permute-start.18 = (bf16[2,32,1,8,128]{4,3,2,1,0:T(8,128)(2,1)S(1)}, bf16[2,32,1,8,128]{4,3,2,1,0:T(8,128)(2,1)S(1)}, u32[]{:S(2)}, u32[]{:S(2)}) collective-permute-start(bf16[2,32,1,8,128]{4,3,2,1,0:T(8,128)(2,1)S(1)} %get-tuple-element.33), channel_id=1, source_target_pairs={{0,8},{8,0},{16,24},{24,16},{1,9},{9,1},{17,25},{25,17},{2,10},{10... | collective-permute-start | bytes 393224 | tf_op jit(solution)/shard_map/ppermute | solution.py:35
  81.2 12.9 %collective-permute-start.19 = (bf16[2,32,1,8,128]{4,3,2,1,0:T(8,128)(2,1)S(1)}, bf16[2,32,1,8,128]{4,3,2,1,0:T(8,128)(2,1)S(1)}, u32[]{:S(2)}, u32[]{:S(2)}) collective-permute-start(bf16[2,32,1,8,128]{4,3,2,1,0:T(8,128)(2,1)S(1)} %get-tuple-element.34), channel_id=1, source_target_pairs={{0,16},{8,24},{16,0},{24,8},{1,17},{9,25},{17,1},{25,9},{2,18},{10... | collective-permute-start | bytes 393224 | tf_op jit(solution)/shard_map/ppermute | solution.py:35
  82.6 11.5 %collective-permute-start.20 = (bf16[2,32,1,8,128]{4,3,2,1,0:T(8,128)(2,1)S(1)}, bf16[2,32,1,8,128]{4,3,2,1,0:T(8,128)(2,1)S(1)}, u32[]{:S(2)}, u32[]{:S(2)}) collective-permute-start(bf16[2,32,1,8,128]{4,3,2,1,0:T(8,128)(2,1)S(1)} %get-tuple-element.35), channel_id=1, source_target_pairs={{0,24},{8,16},{16,8},{24,0},{1,25},{9,17},{17,9},{25,1},{2,26},{10... | collective-permute-start | bytes 393224 | tf_op jit(solution)/shard_map/ppermute | solution.py:35
  87.9 6.2 %copy-start.5 = (bf16[2,32,1,8,128]{4,3,2,1,0:T(8,128)(2,1)}, bf16[2,32,1,8,128]{4,3,2,1,0:T(8,128)(2,1)S(1)}, u32[]{:S(2)}) copy-start(bf16[2,32,1,8,128]{4,3,2,1,0:T(8,128)(2,1)S(1)} %collective-permute-done.18.rest_1_) | copy-start | bytes 393220
  (5 other events, 3.9 us)

commit v3 on v2

--- a/solution.py
+++ b/solution.py
@@ -10,8 +10,7 @@
 
 SECTIONS = 4
 CHUNKS = (1, 1)
-ORDER = (1, 2, 3)
-UNROLL = 2
+UNROLL = 4
 
 diffuse_x = 0.35
 diffuse_side = 0.05
@@ -92,7 +91,7 @@
     step, nz = own_ref.shape[1:]
     if lead:
         adj = (me == groups - 1).astype(jnp.int32)
-        sign = jnp.where(me == groups - 1, f32(0.5), f32(-0.5))
+        sign = jnp.where(me == groups - 1, f32(1.0), f32(-1.0))
         per = step // (rows * ny)
 
         def flow_of(ref):
@@ -174,57 +173,49 @@
     return outs[:groups], outs[groups:]
 
 
+def by_group(me, groups, action):
+    for g in range(groups):
+        pl.when(me == g)(functools.partial(action, g))
+
+
 def coupling_kernel(groups, chunks, where_ref, *rest):
     blocks = rest[: groups * chunks]
-    fields, keep, send, scratch, sem = rest[groups * chunks:]
+    keep, send, scratch = rest[groups * chunks:]
     me, half = where_ref[0], where_ref[1]
-    copies = []
-    for k in range(groups):
-        start = 0
-        for c in range(chunks):
-            step = blocks[c].shape[1]
-            copies.append(pltpu.make_async_copy(
-                blocks[k * chunks + c],
-                fields.at[peer(me, k), :, pl.ds(start, step)],
-                sem.at[k * chunks + c]))
-            start += step
-    for copy in copies:
-        copy.start()
-    for copy in copies:
-        copy.wait()
-    parts, snaps = fields.shape[1], fields.shape[2]
+    parts = blocks[0].shape[0]
     width = 2 if parts % 2 == 0 else 1
-
-    def wide(g, y):
-        return jnp.concatenate([fields[g, y + i] for i in range(width)], axis=1)
-
-    for g in range(groups - 1):
-        acc = None
+    snaps = scratch.shape[0]
+
+    def action(mine):
+        def wide(g, y):
+            own = blocks[peer(mine, g) * chunks:(peer(mine, g) + 1) * chunks]
+            return jnp.concatenate([
+                jnp.concatenate([block[y + i] for block in own], axis=0) for i in range(width)
+            ], axis=1)
+
+        total = None
         for y in range(0, parts, width):
-            term = lax.dot_general(wide(groups - 1, y), wide(g, y), (((1,), (1,)), ((), ())),
+            direct = jnp.concatenate([wide(g, y) for g in range(groups - 1)], axis=0)
+            term = lax.dot_general(wide(groups - 1, y), direct, (((1,), (1,)), ((), ())),
                                    preferred_element_type=f32)
-            acc = term if acc is None else acc + term
-        scratch[:, g * snaps:(g + 1) * snaps] = acc
+            total = term if total is None else total + term
+        scratch[...] = total
+
+    by_group(me, groups, action)
     mid = snaps // 2
     keep[...] = scratch[pl.ds(pl.multiple_of(half * mid, mid), mid), :]
-    send[...] = scratch[pl.ds(pl.multiple_of((1 - half) * mid, mid), mid), :].astype(send.dtype)
+    send[...] = scratch[pl.ds(pl.multiple_of((1 - half) * mid, mid), mid), :]
 
 
 def coupling(where, blocks, groups, chunks):
-    parts, _, nz = blocks[0].shape
     snaps = sum(block.shape[1] for block in blocks[:chunks])
     wide = (groups - 1) * snaps
     return pl.pallas_call(
         functools.partial(coupling_kernel, groups, chunks),
-        out_shape=[
-            jax.ShapeDtypeStruct((groups, parts, snaps, nz), bf16),
-            jax.ShapeDtypeStruct((snaps // 2, wide), f32),
-            jax.ShapeDtypeStruct((snaps // 2, wide), f32),
-        ],
-        in_specs=[smem] + [anywhere] * (groups * chunks),
-        out_specs=[vmem] * 3,
-        scratch_shapes=[pltpu.VMEM((snaps, wide), f32),
-                        pltpu.SemaphoreType.DMA((groups * chunks,))],
+        out_shape=[jax.ShapeDtypeStruct((snaps // 2, wide), f32)] * 2,
+        in_specs=[smem] + [vmem] * (groups * chunks),
+        out_specs=[vmem] * 2,
+        scratch_shapes=[pltpu.VMEM((snaps, wide), f32)],
         compiler_params=pltpu.CompilerParams(vmem_limit_bytes=VMEM_LIMIT),
         name="coupling",
     )(where, *blocks)
@@ -243,7 +234,10 @@
         return jnp.broadcast_to(value[j:j + 1], (8, size))
 
     def small_inverse(a, b, d):
-        det = 1.0 / (a * d - b * b)
+        det = a * d - b * b
+        guess = pl.reciprocal(det, approx=True)
+        guess = guess * (2.0 - det * guess)
+        det = guess * (2.0 - det * guess)
         return d * det, -b * det, a * det
 
     for p in range(size // 8):
@@ -292,14 +286,14 @@
     return jnp.concatenate(panels, axis=0)
 
 
-def modes_kernel(groups, where_ref, mine_ref, other_ref, fields, *rest):
-    outs = rest[:groups]
-    coupling_ref, stage = rest[groups:]
+def modes_kernel(groups, chunks, where_ref, mine_ref, other_ref, *rest):
+    blocks = rest[:groups * chunks]
+    outs = rest[groups * chunks:groups * (chunks + 1)]
+    coupling_ref, stage = rest[groups * (chunks + 1):]
     me, half = where_ref[0], where_ref[1]
     mid = mine_ref.shape[0]
     snaps = 2 * mid
-    parts = fields.shape[1]
-    scale = where_ref.shape[0]
+    parts = blocks[0].shape[0]
     coupling_ref[pl.ds(pl.multiple_of(half * mid, mid), mid), :] = mine_ref[...]
     coupling_ref[pl.ds(pl.multiple_of((1 - half) * mid, mid), mid), :] = other_ref[...]
     coupled = coupling_ref[...]
@@ -318,16 +312,22 @@
     share = snaps // groups
     ny = outs[0].shape[3]
     layers = parts // ny
-    for which in range(2):
+
+    def action(mine):
+        def group(g, at):
+            return [block[at] for block in blocks[peer(mine, g) * chunks:(peer(mine, g) + 1) * chunks]]
+
         for layer in range(layers):
             for y in range(ny):
                 at = layer * ny + y
-                if which == 0:
-                    stacked = jnp.concatenate([fields[g, at] for g in range(groups - 1)], axis=0)
-                    value = jnp.dot(weights, stacked, preferred_element_type=f32)
-                else:
-                    value = jnp.dot(inverse, fields[groups - 1, at], preferred_element_type=f32)
-                stage[which, layer, pl.ds(y, snaps, stride=ny), :] = value
+                rows = pl.ds(y, snaps, stride=ny)
+                direct = jnp.concatenate(
+                    [part for g in range(groups - 1) for part in group(g, at)], axis=0)
+                adjoint = jnp.concatenate(group(groups - 1, at), axis=0)
+                stage[0, layer, rows, :] = jnp.dot(weights, direct, preferred_element_type=f32)
+                stage[1, layer, rows, :] = jnp.dot(inverse, adjoint, preferred_element_type=f32)
+
+    by_group(me, groups, action)
     for k in range(groups):
         start = pl.multiple_of(peer(me, k) * (share * ny), share * ny)
         for which in range(2):
@@ -336,20 +336,22 @@
                 outs[k][which, :, layer] = value.reshape(share, ny, value.shape[1]).astype(bf16)
 
 
-def modes(where, mine, other, fields, groups, ny):
-    _, parts, snaps, nz = fields.shape
+def modes(where, mine, other, blocks, groups, ny):
+    chunks = len(blocks) // groups
+    parts, _, nz = blocks[0].shape
+    snaps = 2 * mine.shape[0]
     layers = parts // ny
     share = snaps // groups
     return pl.pallas_call(
-        functools.partial(modes_kernel, groups),
+        functools.partial(modes_kernel, groups, chunks),
         out_shape=[jax.ShapeDtypeStruct((2, share, layers, ny, nz), bf16)] * groups,
-        in_specs=[smem, vmem, vmem, vmem],
+        in_specs=[smem, vmem, vmem] + [vmem] * len(blocks),
         out_specs=[vmem] * groups,
         scratch_shapes=[pltpu.VMEM((snaps, mine.shape[1]), f32),
                         pltpu.VMEM((2, layers, snaps * ny, nz), f32)],
         compiler_params=pltpu.CompilerParams(vmem_limit_bytes=VMEM_LIMIT),
         name="modes",
-    )(where, mine, other, fields)
+    )(where, mine, other, *blocks)
 
 
 def place_kernel(groups, where_ref, *rest):
@@ -371,6 +373,7 @@
         out_shape=[out, out],
         in_specs=[smem] + [vmem] * groups,
         out_specs=[vmem] * 2,
+        compiler_params=pltpu.CompilerParams(vmem_limit_bytes=8 * 1024 * 1024),
         name="place",
     )(where, *blocks)
 
@@ -383,6 +386,7 @@
     me = lax.axis_index("grp")
     half = lax.axis_index("slab") % 2
     where = jnp.stack([me, half]).astype(jnp.int32)
+    flow = 0.5 * base_flow
     at = jnp.arange(nz)
     gap = (at[:, None] - at[None, :]) % nz
     ring = (2 * (gap == 0) + (gap == 1) + (gap == nz - 1)).astype(bf16)
@@ -391,17 +395,17 @@
     blocks = [[None] * chunks for _ in range(groups)]
     coefs = None
     for c in range(chunks):
-        own = pack(base_flow, field, sum(sizes[:c]), sizes[c], c == 0)
+        own = pack(flow, field, sum(sizes[:c]), sizes[c], c == 0)
         lo = shift(own, "slab", 1)
         hi = shift(own, "slab", -1)
-        before = [blocks[ORDER[0]][c - 1]] if c else []
-        parts, made = sections(where, ring, coefs, own, lo, hi, groups, base_flow, before)
+        before = [blocks[1][c - 1]] if c else []
+        parts, made = sections(where, ring, coefs, own, lo, hi, groups, flow, before)
         coefs = coefs or made
         blocks[0][c] = parts[0]
-        for k in ORDER:
+        for k in range(1, groups):
             blocks[k][c] = swap(parts[k], "grp", k)
     flat = [blocks[k][c] for k in range(groups) for c in range(chunks)]
-    fields, keep, send = coupling(where, flat, groups, chunks)
+    keep, send = coupling(where, flat, groups, chunks)
     total = keep + swap(send, "slab", 1)
     bit = 2
     while bit < slabs:
@@ -415,8 +419,10 @@
     total = sum((swap(sent, "grp", s).astype(f32) for s in range(1, groups)), total)
     mine = total * (1.0 / math.sqrt(rows * slabs * ny * nz))
     other = swap(mine, "slab", 1)
-    outs = modes(where, mine, other, fields, groups, ny)
-    outs = [outs[0]] + [swap(outs[k], "grp", k) for k in range(1, groups)]
+    outs = modes(where, mine, other, flat, groups, ny)
+    outs = list(outs)
+    for k in range(1, groups):
+        outs[k] = swap(outs[k], "grp", k)
     return tuple(place(where, outs, groups))
 
 

time: 97 us -> 94.2 us (0.971)
  local copies, waits for them, and re-layouts: 3.28 us -> 1.22 us
  Pallas kernels: 20.6 us -> 19.1 us
    unnamed x16 -> x2, local copies, waits for them, and re-layouts: 3.28 us -> 1.22 us
where the time goes in v3:
time: 94.2 us; the launch traced here: 94 us
  waiting for transfers between devices  40.4 us (43%)
  starting transfers between devices  31.6 us (34%)
  Pallas kernels  19.1 us (20%)
  local copies, waits for them, and re-layouts  1.22 us (1%)
    ppermute x17, waiting for transfers between devices, swap(): return lax.ppermute(value, axis, [(i, i ^ step) for i in range(count)])  29.5 us
    ppermute x17, starting transfers between devices, swap(): return lax.ppermute(value, axis, [(i, i ^ step) for i in range(count)])  25.5 us
    ppermute x4, waiting for transfers between devices, shift(): lax.ppermute(value, axis, [(i, (i + step) % count) for i in range(count)])  10.9 us
    pallas_call x2, Pallas kernels, sections(): pl.pallas_call(functools.partial(sections_kernel, groups, rows, ny, lead)...  8.34 us
    pallas_call x1, Pallas kernels, modes(): pl.pallas_call(functools.partial(modes_kernel, groups, chunks), out_shape...  7.67 us
    ppermute x4, starting transfers between devices, shift(): lax.ppermute(value, axis, [(i, (i + step) % count) for i in range(count)])  6.14 us
  transfers between devices with their start and end apart: 21, of which 15 were waited for; matrix products, arithmetic and copies ran while one was open for 0% of the time, Pallas kernels for 9%

profile of v3, /device:TPU:0, one launch (start us, length us, event | category | flops | bytes accessed | tf_op | source)
XLA Modules:
  0.0 94.0 jit_solution(4754386734603151970)
XLA Ops:
  3.4 2.9 %collective-permute-start.1 = (bf16[34,64,128]{2,1,0:T(8,128)(2,1)S(1)}, bf16[34,64,128]{2,1,0:T(8,128)(2,1)S(1)}, u32[]{:S(2)}, u32[]{:S(2)}) collective-permute-start(bf16[34,64,128]{2,1,0:T(8,128)(2,1)S(1)} %pack.2.rest_1_), channel_id=1, source_target_pairs={{0,7},{1,0},{2,1},{3,2},{4,3},{5,4},{6,5},{7,6},{8,15},{9,8},{10,9... | collective-permute-start | bytes 1671176 | tf_op jit(solution)/shard_map/ppermute | solution.py:39
  6.7 2.6 %collective-permute-start.3 = (bf16[32,64,128]{2,1,0:T(8,128)(2,1)S(1)}, bf16[32,64,128]{2,1,0:T(8,128)(2,1)S(1)}, u32[]{:S(2)}, u32[]{:S(2)}) collective-permute-start(bf16[32,64,128]{2,1,0:T(8,128)(2,1)S(1)} %pack.3.rest_2_), channel_id=1, source_target_pairs={{0,7},{1,0},{2,1},{3,2},{4,3},{5,4},{6,5},{7,6},{8,15},{9,8},{10,9... | collective-permute-start | bytes 1572872 | tf_op jit(solution)/shard_map/ppermute | solution.py:39
  9.4 7.3 %collective-permute-done.rest_2_ = bf16[34,64,128]{2,1,0:T(8,128)(2,1)S(1)} collective-permute-done((bf16[34,64,128]{2,1,0:T(8,128)(2,1)S(1)}, bf16[34,64,128]{2,1,0:T(8,128)(2,1)S(1)}, u32[]{:S(2)}, u32[]{:S(2)}) %collective-permute-start) | collective-permute-done | bytes 557088 | tf_op jit(solution)/shard_map/ppermute | solution.py:39
  16.8 2.6 %collective-permute-done.1.rest_3_ = bf16[34,64,128]{2,1,0:T(8,128)(2,1)S(1)} collective-permute-done((bf16[34,64,128]{2,1,0:T(8,128)(2,1)S(1)}, bf16[34,64,128]{2,1,0:T(8,128)(2,1)S(1)}, u32[]{:S(2)}, u32[]{:S(2)}) %collective-permute-start.1) | collective-permute-done | bytes 557088 | tf_op jit(solution)/shard_map/ppermute | solution.py:39
  19.3 4.2 %sections.2 = (bf16[8,64,128]{2,1,0:T(8,128)(2,1)S(1)}, bf16[8,64,128]{2,1,0:T(8,128)(2,1)S(1)}, bf16[8,64,128]{2,1,0:T(8,128)(2,1)S(1)}, bf16[8,64,128]{2,1,0:T...) custom-call(s32[2]{0:T(128)S(1)} %pad_add_fusion.where_ref, ...), custom_call_target="tpu_custom_call" | custom-call | flops 25165824 | bytes 2097152 | tf_op jit(solution)/shard_map/sections/pallas_call | solution.py:162
  23.5 2.4 %collective-permute-start.4 = (bf16[8,64,128]{2,1,0:T(8,128)(2,1)S(1)}, bf16[8,64,128]{2,1,0:T(8,128)(2,1)S(1)}, u32[]{:S(2)}, u32[]{:S(2)}) collective-permute-start(bf16[8,64,128]{2,1,0:T(8,128)(2,1)S(1)} %get-tuple-element.21), channel_id=1, source_target_pairs={{0,8},{8,0},{16,24},{24,16},{1,9},{9,1},{17,25},{25,17},{2,10},{10... | collective-permute-start | bytes 393224 | tf_op jit(solution)/shard_map/ppermute | solution.py:34
  25.9 2.6 %collective-permute-start.6 = (bf16[8,64,128]{2,1,0:T(8,128)(2,1)S(1)}, bf16[8,64,128]{2,1,0:T(8,128)(2,1)S(1)}, u32[]{:S(2)}, u32[]{:S(2)}) collective-permute-start(bf16[8,64,128]{2,1,0:T(8,128)(2,1)S(1)} %get-tuple-element.24), channel_id=1, source_target_pairs={{0,16},{8,24},{16,0},{24,8},{1,17},{9,25},{17,1},{25,9},{2,18},{10... | collective-permute-start | bytes 393224 | tf_op jit(solution)/shard_map/ppermute | solution.py:34
  29.8 4.1 %sections.3 = (bf16[8,64,128]{2,1,0:T(8,128)(2,1)S(1)}, bf16[8,64,128]{2,1,0:T(8,128)(2,1)S(1)}, bf16[8,64,128]{2,1,0:T(8,128)(2,1)S(1)}, bf16[8,64,128]{2,1,0:T(8,128)(2,1)S(1)}) custom-call(s32[2]{0:T(128)S(1)} %pad_add_fusion.where_ref, bf16[128,128]{1,0:T(8,128)(2,1)S(1)} %add_convert_fusion.ring_ref, f32[12,8,128]{2,1,0:T(8,128)S(1)} %get-tuple-element.19.rest_0_, ...), custom_call_target="tpu_custom_call" | custom-call | flops 25165824 | bytes 2097152 | tf_op jit(solution)/shard_map/sections/pallas_call | solution.py:162
  34.0 2.5 %collective-permute-start.5 = (bf16[8,64,128]{2,1,0:T(8,128)(2,1)S(1)}, bf16[8,64,128]{2,1,0:T(8,128)(2,1)S(1)}, u32[]{:S(2)}, u32[]{:S(2)}) collective-permute-start(bf16[8,64,128]{2,1,0:T(8,128)(2,1)S(1)} %get-tuple-element.23), channel_id=1, source_target_pairs={{0,8},{8,0},{16,24},{24,16},{1,9},{9,1},{17,25},{25,17},{2,10},{10... | collective-permute-start | bytes 393224 | tf_op jit(solution)/shard_map/ppermute | solution.py:34
  36.4 4.1 %collective-permute-start.7 = (bf16[8,64,128]{2,1,0:T(8,128)(2,1)S(1)}, bf16[8,64,128]{2,1,0:T(8,128)(2,1)S(1)}, u32[]{:S(2)}, u32[]{:S(2)}) collective-permute-start(bf16[8,64,128]{2,1,0:T(8,128)(2,1)S(1)} %get-tuple-element.25), channel_id=1, source_target_pairs={{0,16},{8,24},{16,0},{24,8},{1,17},{9,25},{17,1},{25,9},{2,18},{10... | collective-permute-start | bytes 393224 | tf_op jit(solution)/shard_map/ppermute | solution.py:34
  41.6 9.0 %collective-permute-done.7.rest_5_ = bf16[8,64,128]{2,1,0:T(8,128)(2,1)S(1)} collective-permute-done((bf16[8,64,128]{2,1,0:T(8,128)(2,1)S(1)}, bf16[8,64,128]{2,1,0:T(8,128)(2,1)S(1)}, u32[]{:S(2)}, u32[]{:S(2)}) %collective-permute-start.7) | collective-permute-done | bytes 131104 | tf_op jit(solution)/shard_map/ppermute | solution.py:34
  51.7 1.3 %collective-permute-done.10 = f32[64,384]{1,0:T(8,128)S(1)} collective-permute-done((f32[64,384]{1,0:T(8,128)S(1)}, f32[64,384]{1,0:T(8,128)S(1)}, u32[]{:S(2)}, u32[]{:S(2)}) %collective-permute-start.10) | collective-permute-done | bytes 98336 | tf_op jit(solution)/shard_map/ppermute | solution.py:34
  54.6 2.0 %collective-permute-start.13 = (bf16[64,384]{1,0:T(8,128)(2,1)S(1)}, bf16[64,384]{1,0:T(8,128)(2,1)S(1)}, u32[]{:S(2)}, u32[]{:S(2)}) collective-permute-start(bf16[64,384]{1,0:T(8,128)(2,1)S(1)} %get-tuple-element.34), channel_id=1, source_target_pairs={{0,6},{1,7},{2,4},{3,5},{4,2},{5,3},{6,0},{7,1},{8,14},{9,15},{10,... | collective-permute-start | bytes 147464 | tf_op jit(solution)/shard_map/ppermute | solution.py:34
  57.5 2.1 %collective-permute-done.13 = bf16[64,384]{1,0:T(8,128)(2,1)S(1)} collective-permute-done((bf16[64,384]{1,0:T(8,128)(2,1)S(1)}, bf16[64,384]{1,0:T(8,128)(2,1)S(1)}, u32[]{:S(2)}, u32[]{:S(2)}) %collective-permute-start.13) | collective-permute-done | bytes 49184 | tf_op jit(solution)/shard_map/ppermute | solution.py:34
  59.6 3.3 %collective-permute-start.14 = (bf16[64,384]{1,0:T(8,128)(2,1)S(1)}, bf16[64,384]{1,0:T(8,128)(2,1)S(1)}, u32[]{:S(2)}, u32[]{:S(2)}) collective-permute-start(bf16[64,384]{1,0:T(8,128)(2,1)S(1)} %fusion.4), channel_id=1, source_target_pairs={{0,8},{8,0},{16,24},{24,16},{1,9},{9,1},{17,25},{25,17},{2,10},{10... | collective-permute-start | bytes 147464 | tf_op jit(solution)/shard_map/ppermute | solution.py:34
  64.0 1.4 %collective-permute-start.16 = (bf16[64,384]{1,0:T(8,128)(2,1)S(1)}, bf16[64,384]{1,0:T(8,128)(2,1)S(1)}, u32[]{:S(2)}, u32[]{:S(2)}) collective-permute-start(bf16[64,384]{1,0:T(8,128)(2,1)S(1)} %fusion.4), channel_id=1, source_target_pairs={{0,24},{8,16},{16,8},{24,0},{1,25},{9,17},{17,9},{25,1},{2,26},{10... | collective-permute-start | bytes 147464 | tf_op jit(solution)/shard_map/ppermute | solution.py:34
  65.4 3.0 %collective-permute-done.15 = bf16[64,384]{1,0:T(8,128)(2,1)S(1)} collective-permute-done((bf16[64,384]{1,0:T(8,128)(2,1)S(1)}, bf16[64,384]{1,0:T(8,128)(2,1)S(1)}, u32[]{:S(2)}, u32[]{:S(2)}) %collective-permute-start.15) | collective-permute-done | bytes 49184 | tf_op jit(solution)/shard_map/ppermute | solution.py:34
  68.5 1.6 %collective-permute-done.16 = bf16[64,384]{1,0:T(8,128)(2,1)S(1)} collective-permute-done((bf16[64,384]{1,0:T(8,128)(2,1)S(1)}, bf16[64,384]{1,0:T(8,128)(2,1)S(1)}, u32[]{:S(2)}, u32[]{:S(2)}) %collective-permute-start.16) | collective-permute-done | bytes 49184 | tf_op jit(solution)/shard_map/ppermute | solution.py:34
  71.4 7.7 %modes.1 = (bf16[2,32,1,8,128]{4,3,2,1,0:T(8,128)(2,1)S(1)}, bf16[2,32,1,8,128]{4,3,2,1,0:T(8,128)(2,1)S(1)}, bf16[2,32,1,8,128]{4,3,2,1,0:T(8,128)(2,1)S(1)}, bf16[2,32,1,8,128]{4,3,2,1,0:T(8,128)(2,1)S(1)}) custom-call(s32[2]{0:T(128)S(1)} %pad_add_fusion.where_ref, f32[64,384]{1,0:T(8,128)S(1)} %add_multiply_fusion.mine_ref, ...), custom_call_target="tpu_custom_call" | custom-call | tf_op jit(solution)/shard_map/modes/pallas_call | solution.py:345
  79.8 1.4 %collective-permute-start.19 = (bf16[2,32,1,8,128]{4,3,2,1,0:T(8,128)(2,1)S(1)}, bf16[2,32,1,8,128]{4,3,2,1,0:T(8,128)(2,1)S(1)}, u32[]{:S(2)}, u32[]{:S(2)}) collective-permute-start(bf16[2,32,1,8,128]{4,3,2,1,0:T(8,128)(2,1)S(1)} %get-tuple-element.32), channel_id=1, source_target_pairs={{0,16},{8,24},{16,0},{24,8},{1,17},{9,25},{17,1},{25,9},{2,18},{10... | collective-permute-start | bytes 393224 | tf_op jit(solution)/shard_map/ppermute | solution.py:34
  81.2 2.4 %collective-permute-start.20 = (bf16[2,32,1,8,128]{4,3,2,1,0:T(8,128)(2,1)S(1)}, bf16[2,32,1,8,128]{4,3,2,1,0:T(8,128)(2,1)S(1)}, u32[]{:S(2)}, u32[]{:S(2)}) collective-permute-start(bf16[2,32,1,8,128]{4,3,2,1,0:T(8,128)(2,1)S(1)} %get-tuple-element.33), channel_id=1, source_target_pairs={{0,24},{8,16},{16,8},{24,0},{1,25},{9,17},{17,9},{25,1},{2,26},{10... | collective-permute-start | bytes 393224 | tf_op jit(solution)/shard_map/ppermute | solution.py:34
  83.6 2.9 %collective-permute-done.18.rest_1_ = bf16[2,32,1,8,128]{4,3,2,1,0:T(8,128)(2,1)S(1)} collective-permute-done((bf16[2,32,1,8,128]{4,3,2,1,0:T(8,128)(2,1)S(1)}, bf16[2,32,1,8,128]{4,3,2,1,0:T(8,128)(2,1)S(1)}, u32[]{:S(2)}, u32[]{:S(2)}) %collective-permute-start.18) | collective-permute-done | bytes 131104 | tf_op jit(solution)/shard_map/ppermute | solution.py:34
  86.5 6.1 %collective-permute-done.19.rest_2_ = bf16[2,32,1,8,128]{4,3,2,1,0:T(8,128)(2,1)S(1)} collective-permute-done((bf16[2,32,1,8,128]{4,3,2,1,0:T(8,128)(2,1)S(1)}, bf16[2,32,1,8,128]{4,3,2,1,0:T(8,128)(2,1)S(1)}, u32[]{:S(2)}, u32[]{:S(2)}) %collective-permute-start.19) | collective-permute-done | bytes 131104 | tf_op jit(solution)/shard_map/ppermute | solution.py:34
  92.6 1.4 %place.1 = (bf16[32,4,8,128]{3,2,1,0:T(8,128)(2,1)}, bf16[32,4,8,128]{3,2,1,0:T(8,128)(2,1)}) custom-call(s32[2]{0:T(128)S(1)} %pad_add_fusion.where_ref, bf16[2,32,1,8,128]{4,3,2,1,0:T(8,128)(2,1)S(1)} %get-tuple-element.30.rest_0_, bf16[2,32,1,8,128]{4,3,2,1,0:T(8,128)(2,1)S(1)} %collective-permute-done.18.rest_1_, ...), custom_call_target="tpu_custom_call" | custom-call | tf_op jit(solution)/shard_map/place/pallas_call | solution.py:371
  (33 shorter events, 12.4 us)
Async XLA Ops:
  1.4 1.2 %copy-start = (bf16[1,128,4,8,128]{4,3,2,1,0:T(8,128)(2,1)S(1)}, bf16[1,128,4,8,128]{4,3,2,1,0:T(8,128)(2,1)}, u32[]{:S(2)}) copy-start(bf16[1,128,4,8,128]{4,3,2,1,0:T(8,128)(2,1)} %param.2) | copy-start | bytes 3145732
  2.9 13.9 %collective-permute-start = (bf16[34,64,128]{2,1,0:T(8,128)(2,1)S(1)}, bf16[34,64,128]{2,1,0:T(8,128)(2,1)S(1)}, u32[]{:S(2)}, u32[]{:S(2)}) collective-permute-start(bf16[34,64,128]{2,1,0:T(8,128)(2,1)S(1)} %pack.2.rest_1_), channel_id=1, source_target_pairs={{0,1},{1,2},{2,3},{3,4},{4,5},{5,6},{6,7},{7,0},{8,9},{9,10},{10,1... | collective-permute-start | bytes 1671176 | tf_op jit(solution)/shard_map/ppermute | solution.py:39
  3.4 16.0 %collective-permute-start.1 = (bf16[34,64,128]{2,1,0:T(8,128)(2,1)S(1)}, bf16[34,64,128]{2,1,0:T(8,128)(2,1)S(1)}, u32[]{:S(2)}, u32[]{:S(2)}) collective-permute-start(bf16[34,64,128]{2,1,0:T(8,128)(2,1)S(1)} %pack.2.rest_1_), channel_id=1, source_target_pairs={{0,7},{1,0},{2,1},{3,2},{4,3},{5,4},{6,5},{7,6},{8,15},{9,8},{10,9... | collective-permute-start | bytes 1671176 | tf_op jit(solution)/shard_map/ppermute | solution.py:39
  6.6 21.9 %collective-permute-start.2 = (bf16[32,64,128]{2,1,0:T(8,128)(2,1)S(1)}, bf16[32,64,128]{2,1,0:T(8,128)(2,1)S(1)}, u32[]{:S(2)}, u32[]{:S(2)}) collective-permute-start(bf16[32,64,128]{2,1,0:T(8,128)(2,1)S(1)} %pack.3.rest_2_), channel_id=1, source_target_pairs={{0,1},{1,2},{2,3},{3,4},{4,5},{5,6},{6,7},{7,0},{8,9},{9,10},{10,1... | collective-permute-start | bytes 1572872 | tf_op jit(solution)/shard_map/ppermute | solution.py:39
  6.7 22.9 %collective-permute-start.3 = (bf16[32,64,128]{2,1,0:T(8,128)(2,1)S(1)}, bf16[32,64,128]{2,1,0:T(8,128)(2,1)S(1)}, u32[]{:S(2)}, u32[]{:S(2)}) collective-permute-start(bf16[32,64,128]{2,1,0:T(8,128)(2,1)S(1)} %pack.3.rest_2_), channel_id=1, source_target_pairs={{0,7},{1,0},{2,1},{3,2},{4,3},{5,4},{6,5},{7,6},{8,15},{9,8},{10,9... | collective-permute-start | bytes 1572872 | tf_op jit(solution)/shard_map/ppermute | solution.py:39
  23.5 6.3 %collective-permute-start.4 = (bf16[8,64,128]{2,1,0:T(8,128)(2,1)S(1)}, bf16[8,64,128]{2,1,0:T(8,128)(2,1)S(1)}, u32[]{:S(2)}, u32[]{:S(2)}) collective-permute-start(bf16[8,64,128]{2,1,0:T(8,128)(2,1)S(1)} %get-tuple-element.21), channel_id=1, source_target_pairs={{0,8},{8,0},{16,24},{24,16},{1,9},{9,1},{17,25},{25,17},{2,10},{10... | collective-permute-start | bytes 393224 | tf_op jit(solution)/shard_map/ppermute | solution.py:34
  25.9 14.6 %collective-permute-start.6 = (bf16[8,64,128]{2,1,0:T(8,128)(2,1)S(1)}, bf16[8,64,128]{2,1,0:T(8,128)(2,1)S(1)}, u32[]{:S(2)}, u32[]{:S(2)}) collective-permute-start(bf16[8,64,128]{2,1,0:T(8,128)(2,1)S(1)} %get-tuple-element.24), channel_id=1, source_target_pairs={{0,16},{8,24},{16,0},{24,8},{1,17},{9,25},{17,1},{25,9},{2,18},{10... | collective-permute-start | bytes 393224 | tf_op jit(solution)/shard_map/ppermute | solution.py:34
  28.5 12.0 %collective-permute-start.8 = (bf16[8,64,128]{2,1,0:T(8,128)(2,1)S(1)}, bf16[8,64,128]{2,1,0:T(8,128)(2,1)S(1)}, u32[]{:S(2)}, u32[]{:S(2)}) collective-permute-start(bf16[8,64,128]{2,1,0:T(8,128)(2,1)S(1)} %get-tuple-element.26), channel_id=1, source_target_pairs={{0,24},{8,16},{16,8},{24,0},{1,25},{9,17},{17,9},{25,1},{2,26},{10... | collective-permute-start | bytes 393224 | tf_op jit(solution)/shard_map/ppermute | solution.py:34
  34.0 7.6 %collective-permute-start.5 = (bf16[8,64,128]{2,1,0:T(8,128)(2,1)S(1)}, bf16[8,64,128]{2,1,0:T(8,128)(2,1)S(1)}, u32[]{:S(2)}, u32[]{:S(2)}) collective-permute-start(bf16[8,64,128]{2,1,0:T(8,128)(2,1)S(1)} %get-tuple-element.23), channel_id=1, source_target_pairs={{0,8},{8,0},{16,24},{24,16},{1,9},{9,1},{17,25},{25,17},{2,10},{10... | collective-permute-start | bytes 393224 | tf_op jit(solution)/shard_map/ppermute | solution.py:34
  36.4 14.1 %collective-permute-start.7 = (bf16[8,64,128]{2,1,0:T(8,128)(2,1)S(1)}, bf16[8,64,128]{2,1,0:T(8,128)(2,1)S(1)}, u32[]{:S(2)}, u32[]{:S(2)}) collective-permute-start(bf16[8,64,128]{2,1,0:T(8,128)(2,1)S(1)} %get-tuple-element.25), channel_id=1, source_target_pairs={{0,16},{8,24},{16,0},{24,8},{1,17},{9,25},{17,1},{25,9},{2,18},{10... | collective-permute-start | bytes 393224 | tf_op jit(solution)/shard_map/ppermute | solution.py:34
  40.5 10.0 %collective-permute-start.9 = (bf16[8,64,128]{2,1,0:T(8,128)(2,1)S(1)}, bf16[8,64,128]{2,1,0:T(8,128)(2,1)S(1)}, u32[]{:S(2)}, u32[]{:S(2)}) collective-permute-start(bf16[8,64,128]{2,1,0:T(8,128)(2,1)S(1)} %get-tuple-element.27), channel_id=1, source_target_pairs={{0,24},{8,16},{16,8},{24,0},{1,25},{9,17},{17,9},{25,1},{2,26},{10... | collective-permute-start | bytes 393224 | tf_op jit(solution)/shard_map/ppermute | solution.py:34
  51.6 1.4 %collective-permute-start.10 = (f32[64,384]{1,0:T(8,128)S(1)}, f32[64,384]{1,0:T(8,128)S(1)}, u32[]{:S(2)}, u32[]{:S(2)}) collective-permute-start(f32[64,384]{1,0:T(8,128)S(1)} %get-tuple-element.29), channel_id=1, source_target_pairs={{0,1},{1,0},{2,3},{3,2},{4,5},{5,4},{6,7},{7,6},{8,9},{9,8},{10,11... | collective-permute-start | bytes 294920 | tf_op jit(solution)/shard_map/ppermute | solution.py:34
  53.0 4.2 %collective-permute-start.11 = (bf16[64,384]{1,0:T(8,128)(2,1)S(1)}, bf16[64,384]{1,0:T(8,128)(2,1)S(1)}, u32[]{:S(2)}, u32[]{:S(2)}) collective-permute-start(bf16[64,384]{1,0:T(8,128)(2,1)S(1)} %get-tuple-element.34), channel_id=1, source_target_pairs={{0,2},{1,3},{2,0},{3,1},{4,6},{5,7},{6,4},{7,5},{8,10},{9,11},{10,... | collective-permute-start | bytes 147464 | tf_op jit(solution)/shard_map/ppermute | solution.py:34
  53.4 4.1 %collective-permute-start.12 = (bf16[64,384]{1,0:T(8,128)(2,1)S(1)}, bf16[64,384]{1,0:T(8,128)(2,1)S(1)}, u32[]{:S(2)}, u32[]{:S(2)}) collective-permute-start(bf16[64,384]{1,0:T(8,128)(2,1)S(1)} %get-tuple-element.34), channel_id=1, source_target_pairs={{0,4},{1,5},{2,6},{3,7},{4,0},{5,1},{6,2},{7,3},{8,12},{9,13},{10,... | collective-permute-start | bytes 147464 | tf_op jit(solution)/shard_map/ppermute | solution.py:34
  54.6 5.0 %collective-permute-start.13 = (bf16[64,384]{1,0:T(8,128)(2,1)S(1)}, bf16[64,384]{1,0:T(8,128)(2,1)S(1)}, u32[]{:S(2)}, u32[]{:S(2)}) collective-permute-start(bf16[64,384]{1,0:T(8,128)(2,1)S(1)} %get-tuple-element.34), channel_id=1, source_target_pairs={{0,6},{1,7},{2,4},{3,5},{4,2},{5,3},{6,0},{7,1},{8,14},{9,15},{10,... | collective-permute-start | bytes 147464 | tf_op jit(solution)/shard_map/ppermute | solution.py:34
  59.6 5.8 %collective-permute-start.14 = (bf16[64,384]{1,0:T(8,128)(2,1)S(1)}, bf16[64,384]{1,0:T(8,128)(2,1)S(1)}, u32[]{:S(2)}, u32[]{:S(2)}) collective-permute-start(bf16[64,384]{1,0:T(8,128)(2,1)S(1)} %fusion.4), channel_id=1, source_target_pairs={{0,8},{8,0},{16,24},{24,16},{1,9},{9,1},{17,25},{25,17},{2,10},{10... | collective-permute-start | bytes 147464 | tf_op jit(solution)/shard_map/ppermute | solution.py:34
  62.9 5.5 %collective-permute-start.15 = (bf16[64,384]{1,0:T(8,128)(2,1)S(1)}, bf16[64,384]{1,0:T(8,128)(2,1)S(1)}, u32[]{:S(2)}, u32[]{:S(2)}) collective-permute-start(bf16[64,384]{1,0:T(8,128)(2,1)S(1)} %fusion.4), channel_id=1, source_target_pairs={{0,16},{8,24},{16,0},{24,8},{1,17},{9,25},{17,1},{25,9},{2,18},{10... | collective-permute-start | bytes 147464 | tf_op jit(solution)/shard_map/ppermute | solution.py:34
  64.0 6.0 %collective-permute-start.16 = (bf16[64,384]{1,0:T(8,128)(2,1)S(1)}, bf16[64,384]{1,0:T(8,128)(2,1)S(1)}, u32[]{:S(2)}, u32[]{:S(2)}) collective-permute-start(bf16[64,384]{1,0:T(8,128)(2,1)S(1)} %fusion.4), channel_id=1, source_target_pairs={{0,24},{8,16},{16,8},{24,0},{1,25},{9,17},{17,9},{25,1},{2,26},{10... | collective-permute-start | bytes 147464 | tf_op jit(solution)/shard_map/ppermute | solution.py:34
  70.1 1.4 %collective-permute-start.17 = (f32[64,384]{1,0:T(8,128)S(1)}, f32[64,384]{1,0:T(8,128)S(1)}, u32[]{:S(2)}, u32[]{:S(2)}) collective-permute-start(f32[64,384]{1,0:T(8,128)S(1)} %add_multiply_fusion.mine_ref), channel_id=1, source_target_pairs={{0,1},{1,0},{2,3},{3,2},{4,5},{5,4},{6,7},{7,6},{8,9},{9,8},{10,11... | collective-permute-start | bytes 294920 | tf_op jit(solution)/shard_map/ppermute | solution.py:34
  79.1 7.4 %collective-permute-start.18 = (bf16[2,32,1,8,128]{4,3,2,1,0:T(8,128)(2,1)S(1)}, bf16[2,32,1,8,128]{4,3,2,1,0:T(8,128)(2,1)S(1)}, u32[]{:S(2)}, u32[]{:S(2)}) collective-permute-start(bf16[2,32,1,8,128]{4,3,2,1,0:T(8,128)(2,1)S(1)} %get-tuple-element.31), channel_id=1, source_target_pairs={{0,8},{8,0},{16,24},{24,16},{1,9},{9,1},{17,25},{25,17},{2,10},{10... | collective-permute-start | bytes 393224 | tf_op jit(solution)/shard_map/ppermute | solution.py:34
  79.8 12.8 %collective-permute-start.19 = (bf16[2,32,1,8,128]{4,3,2,1,0:T(8,128)(2,1)S(1)}, bf16[2,32,1,8,128]{4,3,2,1,0:T(8,128)(2,1)S(1)}, u32[]{:S(2)}, u32[]{:S(2)}) collective-permute-start(bf16[2,32,1,8,128]{4,3,2,1,0:T(8,128)(2,1)S(1)} %get-tuple-element.32), channel_id=1, source_target_pairs={{0,16},{8,24},{16,0},{24,8},{1,17},{9,25},{17,1},{25,9},{2,18},{10... | collective-permute-start | bytes 393224 | tf_op jit(solution)/shard_map/ppermute | solution.py:34
  81.2 11.4 %collective-permute-start.20 = (bf16[2,32,1,8,128]{4,3,2,1,0:T(8,128)(2,1)S(1)}, bf16[2,32,1,8,128]{4,3,2,1,0:T(8,128)(2,1)S(1)}, u32[]{:S(2)}, u32[]{:S(2)}) collective-permute-start(bf16[2,32,1,8,128]{4,3,2,1,0:T(8,128)(2,1)S(1)} %get-tuple-element.33), channel_id=1, source_target_pairs={{0,24},{8,16},{16,8},{24,0},{1,25},{9,17},{17,9},{25,1},{2,26},{10... | collective-permute-start | bytes 393224 | tf_op jit(solution)/shard_map/ppermute | solution.py:34

commit v4 on v3

--- a/solution.py
+++ b/solution.py
@@ -10,7 +10,7 @@
 
 SECTIONS = 4
 CHUNKS = (1, 1)
-UNROLL = 4
+TALL = 32
 
 diffuse_x = 0.35
 diffuse_side = 0.05
@@ -78,16 +78,16 @@
 
 def sections_kernel(groups, rows, ny, lead, where_ref, ring_ref, *rest):
     reach = SECTIONS
-    total = rows + 2 * reach
+    total_rows = rows + 2 * reach
     me = where_ref[0]
     if lead:
         flow_ref, own_ref, lo_ref, hi_ref = rest[:4]
         outs = rest[4:4 + groups]
-        plus, minus, flow_ext, first, second = rest[4 + groups:]
+        plus, minus, flow_ext, done = rest[4 + groups:]
     else:
         plus, minus, own_ref, lo_ref, hi_ref, _ = rest[:6]
         outs = rest[6:6 + groups]
-        first, second = rest[6 + groups:]
+        done, = rest[6 + groups:]
     step, nz = own_ref.shape[1:]
     if lead:
         adj = (me == groups - 1).astype(jnp.int32)
@@ -105,46 +105,57 @@
         flow_ext[0:reach] = flow_of(lo_ref)[rows - reach:]
         flow_ext[reach:reach + rows] = flow_ref[...]
         flow_ext[reach + rows:] = flow_of(hi_ref)[:reach]
-        for e in range(1, total - 1):
+        for e in range(1, total_rows - 1):
             plus[e] = diffuse_x + sign * flow_ext[e + adj]
             minus[e] = diffuse_x - sign * flow_ext[e - adj]
     ring = ring_ref[...]
 
     def entry(e, y):
         if e < reach:
-            return lo_ref[(rows - reach + e) * ny + y]
+            return lo_ref, (rows - reach + e) * ny + y
         if e < reach + rows:
-            return own_ref[(e - reach) * ny + y]
-        return hi_ref[(e - reach - rows) * ny + y]
-
-    def one(src, e, y):
-        get = entry if src is None else lambda at, w: src[at, w]
-        side = jnp.dot(get(e, y), ring, preferred_element_type=f32)
-        side = side + get(e, (y + 1) % ny).astype(f32) + get(e, (y - 1) % ny).astype(f32)
-        updated = diffuse_side * side
-        updated = updated + plus[e, y:y + 1, :] * get(e + 1, y).astype(f32)
-        updated = updated + minus[e, y:y + 1, :] * get(e - 1, y).astype(f32)
-        return updated.astype(bf16)
-
-    for e in range(1, total - 1):
-        for y in range(ny):
-            first[e, y] = one(None, e, y)
-    bufs = (first, second)
-    for s in range(2, SECTIONS):
-        src, dst = bufs[s % 2], bufs[(s - 1) % 2]
-
-        def body(e, carry, src=src, dst=dst):
+            return own_ref, (e - reach) * ny + y
+        return hi_ref, (e - reach - rows) * ny + y
+
+    tall = math.gcd(step, TALL)
+
+    def body(block, carry):
+        at = pl.ds(pl.multiple_of(block * tall, tall), tall)
+
+        def load(e):
+            low = [ref[row, at, :] for ref, row in (entry(e, y) for y in range(ny))]
+            return low, [part.astype(f32) for part in low]
+
+        def advance(e, behind, here, ahead):
+            low, mid = here
+            side = jnp.dot(jnp.concatenate(low, axis=0), ring, preferred_element_type=f32)
+            made = []
             for y in range(ny):
-                dst[e, y] = one(src, e, y)
-            return carry
-        lax.fori_loop(s, total - s, body, 0, unroll=UNROLL)
-    src = bufs[SECTIONS % 2]
+                total = side[y * tall:(y + 1) * tall] + (mid[(y + 1) % ny] + mid[(y - 1) % ny])
+                total = diffuse_side * total + plus[e, y:y + 1, :] * ahead[1][y]
+                total = total + minus[e, y:y + 1, :] * behind[1][y]
+                made.append(total.astype(bf16))
+            return made, [part.astype(f32) for part in made]
+
+        held = [{} for _ in range(SECTIONS + 1)]
+        for t in range(total_rows):
+            held[0][t] = load(t)
+            for s in range(1, SECTIONS + 1):
+                e = t - s
+                if s <= e < total_rows - s:
+                    below = held[s - 1]
+                    held[s][e] = advance(e, below[e - 1], below[e], below[e + 1])
+                    del below[e - 1]
+                    if s == SECTIONS:
+                        for y in range(ny):
+                            done[e - reach, y, at, :] = held[s][e][0][y]
+        return carry
+
+    lax.fori_loop(0, step // tall, body, 0)
     share = rows // groups
     for k in range(groups):
         for j in range(share):
-            e = reach + peer(me, k) * share + j
-            for y in range(ny):
-                outs[k][j * ny + y] = one(src, e, y)
+            outs[k][j * ny:(j + 1) * ny] = done[peer(me, k) * share + j]
 
 
 def sections(where, ring, coefs, own, lo, hi, groups, flow, before):
@@ -154,7 +165,7 @@
     total = rows + 2 * SECTIONS
     lead = coefs is None
     out = [jax.ShapeDtypeStruct((share * ny, step, nz), bf16)] * groups
-    scratch = [pltpu.VMEM((total, ny, step, nz), bf16)] * 2
+    scratch = [pltpu.VMEM((rows, ny, step, nz), bf16)]
     if lead:
         out += [jax.ShapeDtypeStruct((total, ny, nz), f32)] * 2
         scratch = [pltpu.VMEM((total, ny, nz), f32)] + scratch

time: 94.2 us -> 93 us (0.987)
  Pallas kernels: 19.1 us -> 16.9 us
  waiting for transfers between devices: 40.4 us -> 42.1 us
    pallas_call x2, Pallas kernels: 8.34 us -> 6.35 us  [sections(): pl.pallas_call(functools.partial(sections_kernel, groups, rows, ny, lead)...]
    ppermute x4, waiting for transfers between devices: 10.9 us -> 11.9 us  [shift(): lax.ppermute(value, axis, [(i, (i + step) % count) for i in range(count)])]
  transfers between devices with their start and end apart: 21 -> 21, of which waited for: 15 -> 16; matrix products, arithmetic and copies ran while one was open for 0% -> 0% of each run, Pallas kernels for 9% -> 7%
where the time goes in v4:
time: 93 us; the launch traced here: 92.8 us
  waiting for transfers between devices  42.1 us (45%)
  starting transfers between devices  30.9 us (33%)
  Pallas kernels  16.9 us (18%)
  local copies, waits for them, and re-layouts  1.22 us (1%)
  other arithmetic  0.94 us (1%)
    ppermute x17, waiting for transfers between devices, swap(): return lax.ppermute(value, axis, [(i, i ^ step) for i in range(count)])  30.2 us
    ppermute x17, starting transfers between devices, swap(): return lax.ppermute(value, axis, [(i, i ^ step) for i in range(count)])  24.7 us
    ppermute x4, waiting for transfers between devices, shift(): lax.ppermute(value, axis, [(i, (i + step) % count) for i in range(count)])  11.9 us
    pallas_call x1, Pallas kernels, modes(): pl.pallas_call(functools.partial(modes_kernel, groups, chunks), out_shape...  7.67 us
    pallas_call x2, Pallas kernels, sections(): pl.pallas_call(functools.partial(sections_kernel, groups, rows, ny, lead)...  6.35 us
    ppermute x4, starting transfers between devices, shift(): lax.ppermute(value, axis, [(i, (i + step) % count) for i in range(count)])  6.14 us
  transfers between devices with their start and end apart: 21, of which 16 were waited for; matrix products, arithmetic and copies ran while one was open for 0% of the time, Pallas kernels for 7%

profile of v4, /device:TPU:0, one launch (start us, length us, event | category | flops | bytes accessed | tf_op | source)
XLA Modules:
  0.0 92.8 jit_solution(8821584406513511741)
XLA Ops:
  3.4 2.9 %collective-permute-start.1 = (bf16[34,64,128]{2,1,0:T(8,128)(2,1)S(1)}, bf16[34,64,128]{2,1,0:T(8,128)(2,1)S(1)}, u32[]{:S(2)}, u32[]{:S(2)}) collective-permute-start(bf16[34,64,128]{2,1,0:T(8,128)(2,1)S(1)} %pack.2.rest_1_), channel_id=1, source_target_pairs={{0,7},{1,0},{2,1},{3,2},{4,3},{5,4},{6,5},{7,6},{8,15},{9,8},{10,9... | collective-permute-start | bytes 1671176 | tf_op jit(solution)/shard_map/ppermute | solution.py:39
  6.7 2.6 %collective-permute-start.3 = (bf16[32,64,128]{2,1,0:T(8,128)(2,1)S(1)}, bf16[32,64,128]{2,1,0:T(8,128)(2,1)S(1)}, u32[]{:S(2)}, u32[]{:S(2)}) collective-permute-start(bf16[32,64,128]{2,1,0:T(8,128)(2,1)S(1)} %pack.3.rest_2_), channel_id=1, source_target_pairs={{0,7},{1,0},{2,1},{3,2},{4,3},{5,4},{6,5},{7,6},{8,15},{9,8},{10,9... | collective-permute-start | bytes 1572872 | tf_op jit(solution)/shard_map/ppermute | solution.py:39
  9.4 7.3 %collective-permute-done.rest_2_ = bf16[34,64,128]{2,1,0:T(8,128)(2,1)S(1)} collective-permute-done((bf16[34,64,128]{2,1,0:T(8,128)(2,1)S(1)}, bf16[34,64,128]{2,1,0:T(8,128)(2,1)S(1)}, u32[]{:S(2)}, u32[]{:S(2)}) %collective-permute-start) | collective-permute-done | bytes 557088 | tf_op jit(solution)/shard_map/ppermute | solution.py:39
  16.8 2.6 %collective-permute-done.1.rest_3_ = bf16[34,64,128]{2,1,0:T(8,128)(2,1)S(1)} collective-permute-done((bf16[34,64,128]{2,1,0:T(8,128)(2,1)S(1)}, bf16[34,64,128]{2,1,0:T(8,128)(2,1)S(1)}, u32[]{:S(2)}, u32[]{:S(2)}) %collective-permute-start.1) | collective-permute-done | bytes 557088 | tf_op jit(solution)/shard_map/ppermute | solution.py:39
  19.3 3.2 %sections.2 = (bf16[8,64,128]{2,1,0:T(8,128)(2,1)S(1)}, bf16[8,64,128]{2,1,0:T(8,128)(2,1)S(1)}, bf16[8,64,128]{2,1,0:T(8,128)(2,1)S(1)}, bf16[8,64,128]{2,1,0:T...) custom-call(s32[2]{0:T(128)S(1)} %pad_add_fusion.where_ref, ...), custom_call_target="tpu_custom_call" | custom-call | flops 25165824 | bytes 2097152 | tf_op jit(solution)/shard_map/sections/pallas_call | solution.py:173
  22.5 2.4 %collective-permute-start.4 = (bf16[8,64,128]{2,1,0:T(8,128)(2,1)S(1)}, bf16[8,64,128]{2,1,0:T(8,128)(2,1)S(1)}, u32[]{:S(2)}, u32[]{:S(2)}) collective-permute-start(bf16[8,64,128]{2,1,0:T(8,128)(2,1)S(1)} %get-tuple-element.21), channel_id=1, source_target_pairs={{0,8},{8,0},{16,24},{24,16},{1,9},{9,1},{17,25},{25,17},{2,10},{10... | collective-permute-start | bytes 393224 | tf_op jit(solution)/shard_map/ppermute | solution.py:34
  24.9 2.6 %collective-permute-start.6 = (bf16[8,64,128]{2,1,0:T(8,128)(2,1)S(1)}, bf16[8,64,128]{2,1,0:T(8,128)(2,1)S(1)}, u32[]{:S(2)}, u32[]{:S(2)}) collective-permute-start(bf16[8,64,128]{2,1,0:T(8,128)(2,1)S(1)} %get-tuple-element.24), channel_id=1, source_target_pairs={{0,16},{8,24},{16,0},{24,8},{1,17},{9,25},{17,1},{25,9},{2,18},{10... | collective-permute-start | bytes 393224 | tf_op jit(solution)/shard_map/ppermute | solution.py:34
  28.0 1.5 %collective-permute-done.3.rest_4_ = bf16[32,64,128]{2,1,0:T(8,128)(2,1)S(1)} collective-permute-done((bf16[32,64,128]{2,1,0:T(8,128)(2,1)S(1)}, bf16[32,64,128]{2,1,0:T(8,128)(2,1)S(1)}, u32[]{:S(2)}, u32[]{:S(2)}) %collective-permute-start.3) | collective-permute-done | bytes 524320 | tf_op jit(solution)/shard_map/ppermute | solution.py:39
  29.5 3.2 %sections.3 = (bf16[8,64,128]{2,1,0:T(8,128)(2,1)S(1)}, bf16[8,64,128]{2,1,0:T(8,128)(2,1)S(1)}, bf16[8,64,128]{2,1,0:T(8,128)(2,1)S(1)}, bf16[8,64,128]{2,1,0:T(8,128)(2,1)S(1)}) custom-call(s32[2]{0:T(128)S(1)} %pad_add_fusion.where_ref, bf16[128,128]{1,0:T(8,128)(2,1)S(1)} %add_convert_fusion.ring_ref, f32[12,8,128]{2,1,0:T(8,128)S(1)} %get-tuple-element.19.rest_0_, ...), custom_call_target="tpu_custom_call" | custom-call | flops 25165824 | bytes 2097152 | tf_op jit(solution)/shard_map/sections/pallas_call | solution.py:173
  32.7 1.7 %collective-permute-start.5 = (bf16[8,64,128]{2,1,0:T(8,128)(2,1)S(1)}, bf16[8,64,128]{2,1,0:T(8,128)(2,1)S(1)}, u32[]{:S(2)}, u32[]{:S(2)}) collective-permute-start(bf16[8,64,128]{2,1,0:T(8,128)(2,1)S(1)} %get-tuple-element.23), channel_id=1, source_target_pairs={{0,8},{8,0},{16,24},{24,16},{1,9},{9,1},{17,25},{25,17},{2,10},{10... | collective-permute-start | bytes 393224 | tf_op jit(solution)/shard_map/ppermute | solution.py:34
  34.5 4.0 %collective-permute-start.7 = (bf16[8,64,128]{2,1,0:T(8,128)(2,1)S(1)}, bf16[8,64,128]{2,1,0:T(8,128)(2,1)S(1)}, u32[]{:S(2)}, u32[]{:S(2)}) collective-permute-start(bf16[8,64,128]{2,1,0:T(8,128)(2,1)S(1)} %get-tuple-element.25), channel_id=1, source_target_pairs={{0,16},{8,24},{16,0},{24,8},{1,17},{9,25},{17,1},{25,9},{2,18},{10... | collective-permute-start | bytes 393224 | tf_op jit(solution)/shard_map/ppermute | solution.py:34
  38.5 1.9 %collective-permute-done.5.rest_3_ = bf16[8,64,128]{2,1,0:T(8,128)(2,1)S(1)} collective-permute-done((bf16[8,64,128]{2,1,0:T(8,128)(2,1)S(1)}, bf16[8,64,128]{2,1,0:T(8,128)(2,1)S(1)}, u32[]{:S(2)}, u32[]{:S(2)}) %collective-permute-start.5) | collective-permute-done | bytes 131104 | tf_op jit(solution)/shard_map/ppermute | solution.py:34
  40.5 8.6 %collective-permute-done.7.rest_5_ = bf16[8,64,128]{2,1,0:T(8,128)(2,1)S(1)} collective-permute-done((bf16[8,64,128]{2,1,0:T(8,128)(2,1)S(1)}, bf16[8,64,128]{2,1,0:T(8,128)(2,1)S(1)}, u32[]{:S(2)}, u32[]{:S(2)}) %collective-permute-start.7) | collective-permute-done | bytes 131104 | tf_op jit(solution)/shard_map/ppermute | solution.py:34
  53.4 1.6 %collective-permute-start.13 = (bf16[64,384]{1,0:T(8,128)(2,1)S(1)}, bf16[64,384]{1,0:T(8,128)(2,1)S(1)}, u32[]{:S(2)}, u32[]{:S(2)}) collective-permute-start(bf16[64,384]{1,0:T(8,128)(2,1)S(1)} %get-tuple-element.34), channel_id=1, source_target_pairs={{0,6},{1,7},{2,4},{3,5},{4,2},{5,3},{6,0},{7,1},{8,14},{9,15},{10,... | collective-permute-start | bytes 147464 | tf_op jit(solution)/shard_map/ppermute | solution.py:34
  56.3 2.1 %collective-permute-done.13 = bf16[64,384]{1,0:T(8,128)(2,1)S(1)} collective-permute-done((bf16[64,384]{1,0:T(8,128)(2,1)S(1)}, bf16[64,384]{1,0:T(8,128)(2,1)S(1)}, u32[]{:S(2)}, u32[]{:S(2)}) %collective-permute-start.13) | collective-permute-done | bytes 49184 | tf_op jit(solution)/shard_map/ppermute | solution.py:34
  58.4 3.3 %collective-permute-start.14 = (bf16[64,384]{1,0:T(8,128)(2,1)S(1)}, bf16[64,384]{1,0:T(8,128)(2,1)S(1)}, u32[]{:S(2)}, u32[]{:S(2)}) collective-permute-start(bf16[64,384]{1,0:T(8,128)(2,1)S(1)} %fusion.4), channel_id=1, source_target_pairs={{0,8},{8,0},{16,24},{24,16},{1,9},{9,1},{17,25},{25,17},{2,10},{10... | collective-permute-start | bytes 147464 | tf_op jit(solution)/shard_map/ppermute | solution.py:34
  62.8 1.4 %collective-permute-start.16 = (bf16[64,384]{1,0:T(8,128)(2,1)S(1)}, bf16[64,384]{1,0:T(8,128)(2,1)S(1)}, u32[]{:S(2)}, u32[]{:S(2)}) collective-permute-start(bf16[64,384]{1,0:T(8,128)(2,1)S(1)} %fusion.4), channel_id=1, source_target_pairs={{0,24},{8,16},{16,8},{24,0},{1,25},{9,17},{17,9},{25,1},{2,26},{10... | collective-permute-start | bytes 147464 | tf_op jit(solution)/shard_map/ppermute | solution.py:34
  64.3 3.0 %collective-permute-done.15 = bf16[64,384]{1,0:T(8,128)(2,1)S(1)} collective-permute-done((bf16[64,384]{1,0:T(8,128)(2,1)S(1)}, bf16[64,384]{1,0:T(8,128)(2,1)S(1)}, u32[]{:S(2)}, u32[]{:S(2)}) %collective-permute-start.15) | collective-permute-done | bytes 49184 | tf_op jit(solution)/shard_map/ppermute | solution.py:34
  67.3 1.6 %collective-permute-done.16 = bf16[64,384]{1,0:T(8,128)(2,1)S(1)} collective-permute-done((bf16[64,384]{1,0:T(8,128)(2,1)S(1)}, bf16[64,384]{1,0:T(8,128)(2,1)S(1)}, u32[]{:S(2)}, u32[]{:S(2)}) %collective-permute-start.16) | collective-permute-done | bytes 49184 | tf_op jit(solution)/shard_map/ppermute | solution.py:34
  70.3 7.7 %modes.1 = (bf16[2,32,1,8,128]{4,3,2,1,0:T(8,128)(2,1)S(1)}, bf16[2,32,1,8,128]{4,3,2,1,0:T(8,128)(2,1)S(1)}, bf16[2,32,1,8,128]{4,3,2,1,0:T(8,128)(2,1)S(1)}, bf16[2,32,1,8,128]{4,3,2,1,0:T(8,128)(2,1)S(1)}) custom-call(s32[2]{0:T(128)S(1)} %pad_add_fusion.where_ref, f32[64,384]{1,0:T(8,128)S(1)} %add_multiply_fusion.mine_ref, ...), custom_call_target="tpu_custom_call" | custom-call | tf_op jit(solution)/shard_map/modes/pallas_call | solution.py:356
  80.0 2.4 %collective-permute-start.20 = (bf16[2,32,1,8,128]{4,3,2,1,0:T(8,128)(2,1)S(1)}, bf16[2,32,1,8,128]{4,3,2,1,0:T(8,128)(2,1)S(1)}, u32[]{:S(2)}, u32[]{:S(2)}) collective-permute-start(bf16[2,32,1,8,128]{4,3,2,1,0:T(8,128)(2,1)S(1)} %get-tuple-element.33), channel_id=1, source_target_pairs={{0,24},{8,16},{16,8},{24,0},{1,25},{9,17},{17,9},{25,1},{2,26},{10... | collective-permute-start | bytes 393224 | tf_op jit(solution)/shard_map/ppermute | solution.py:34
  82.4 2.9 %collective-permute-done.18.rest_1_ = bf16[2,32,1,8,128]{4,3,2,1,0:T(8,128)(2,1)S(1)} collective-permute-done((bf16[2,32,1,8,128]{4,3,2,1,0:T(8,128)(2,1)S(1)}, bf16[2,32,1,8,128]{4,3,2,1,0:T(8,128)(2,1)S(1)}, u32[]{:S(2)}, u32[]{:S(2)}) %collective-permute-start.18) | collective-permute-done | bytes 131104 | tf_op jit(solution)/shard_map/ppermute | solution.py:34
  85.3 6.1 %collective-permute-done.19.rest_2_ = bf16[2,32,1,8,128]{4,3,2,1,0:T(8,128)(2,1)S(1)} collective-permute-done((bf16[2,32,1,8,128]{4,3,2,1,0:T(8,128)(2,1)S(1)}, bf16[2,32,1,8,128]{4,3,2,1,0:T(8,128)(2,1)S(1)}, u32[]{:S(2)}, u32[]{:S(2)}) %collective-permute-start.19) | collective-permute-done | bytes 131104 | tf_op jit(solution)/shard_map/ppermute | solution.py:34
  91.4 1.4 %place.1 = (bf16[32,4,8,128]{3,2,1,0:T(8,128)(2,1)}, bf16[32,4,8,128]{3,2,1,0:T(8,128)(2,1)}) custom-call(s32[2]{0:T(128)S(1)} %pad_add_fusion.where_ref, bf16[2,32,1,8,128]{4,3,2,1,0:T(8,128)(2,1)S(1)} %get-tuple-element.30.rest_0_, bf16[2,32,1,8,128]{4,3,2,1,0:T(8,128)(2,1)S(1)} %collective-permute-done.18.rest_1_, ...), custom_call_target="tpu_custom_call" | custom-call | tf_op jit(solution)/shard_map/place/pallas_call | solution.py:382
  (33 shorter events, 13.9 us)
Async XLA Ops:
  1.4 1.2 %copy-start = (bf16[1,128,4,8,128]{4,3,2,1,0:T(8,128)(2,1)S(1)}, bf16[1,128,4,8,128]{4,3,2,1,0:T(8,128)(2,1)}, u32[]{:S(2)}) copy-start(bf16[1,128,4,8,128]{4,3,2,1,0:T(8,128)(2,1)} %param.2) | copy-start | bytes 3145732
  2.9 13.9 %collective-permute-start = (bf16[34,64,128]{2,1,0:T(8,128)(2,1)S(1)}, bf16[34,64,128]{2,1,0:T(8,128)(2,1)S(1)}, u32[]{:S(2)}, u32[]{:S(2)}) collective-permute-start(bf16[34,64,128]{2,1,0:T(8,128)(2,1)S(1)} %pack.2.rest_1_), channel_id=1, source_target_pairs={{0,1},{1,2},{2,3},{3,4},{4,5},{5,6},{6,7},{7,0},{8,9},{9,10},{10,1... | collective-permute-start | bytes 1671176 | tf_op jit(solution)/shard_map/ppermute | solution.py:39
  3.4 16.0 %collective-permute-start.1 = (bf16[34,64,128]{2,1,0:T(8,128)(2,1)S(1)}, bf16[34,64,128]{2,1,0:T(8,128)(2,1)S(1)}, u32[]{:S(2)}, u32[]{:S(2)}) collective-permute-start(bf16[34,64,128]{2,1,0:T(8,128)(2,1)S(1)} %pack.2.rest_1_), channel_id=1, source_target_pairs={{0,7},{1,0},{2,1},{3,2},{4,3},{5,4},{6,5},{7,6},{8,15},{9,8},{10,9... | collective-permute-start | bytes 1671176 | tf_op jit(solution)/shard_map/ppermute | solution.py:39
  6.6 21.4 %collective-permute-start.2 = (bf16[32,64,128]{2,1,0:T(8,128)(2,1)S(1)}, bf16[32,64,128]{2,1,0:T(8,128)(2,1)S(1)}, u32[]{:S(2)}, u32[]{:S(2)}) collective-permute-start(bf16[32,64,128]{2,1,0:T(8,128)(2,1)S(1)} %pack.3.rest_2_), channel_id=1, source_target_pairs={{0,1},{1,2},{2,3},{3,4},{4,5},{5,6},{6,7},{7,0},{8,9},{9,10},{10,1... | collective-permute-start | bytes 1572872 | tf_op jit(solution)/shard_map/ppermute | solution.py:39
  6.7 22.9 %collective-permute-start.3 = (bf16[32,64,128]{2,1,0:T(8,128)(2,1)S(1)}, bf16[32,64,128]{2,1,0:T(8,128)(2,1)S(1)}, u32[]{:S(2)}, u32[]{:S(2)}) collective-permute-start(bf16[32,64,128]{2,1,0:T(8,128)(2,1)S(1)} %pack.3.rest_2_), channel_id=1, source_target_pairs={{0,7},{1,0},{2,1},{3,2},{4,3},{5,4},{6,5},{7,6},{8,15},{9,8},{10,9... | collective-permute-start | bytes 1572872 | tf_op jit(solution)/shard_map/ppermute | solution.py:39
  22.5 7.0 %collective-permute-start.4 = (bf16[8,64,128]{2,1,0:T(8,128)(2,1)S(1)}, bf16[8,64,128]{2,1,0:T(8,128)(2,1)S(1)}, u32[]{:S(2)}, u32[]{:S(2)}) collective-permute-start(bf16[8,64,128]{2,1,0:T(8,128)(2,1)S(1)} %get-tuple-element.21), channel_id=1, source_target_pairs={{0,8},{8,0},{16,24},{24,16},{1,9},{9,1},{17,25},{25,17},{2,10},{10... | collective-permute-start | bytes 393224 | tf_op jit(solution)/shard_map/ppermute | solution.py:34
  24.9 13.6 %collective-permute-start.6 = (bf16[8,64,128]{2,1,0:T(8,128)(2,1)S(1)}, bf16[8,64,128]{2,1,0:T(8,128)(2,1)S(1)}, u32[]{:S(2)}, u32[]{:S(2)}) collective-permute-start(bf16[8,64,128]{2,1,0:T(8,128)(2,1)S(1)} %get-tuple-element.24), channel_id=1, source_target_pairs={{0,16},{8,24},{16,0},{24,8},{1,17},{9,25},{17,1},{25,9},{2,18},{10... | collective-permute-start | bytes 393224 | tf_op jit(solution)/shard_map/ppermute | solution.py:34
  27.5 11.0 %collective-permute-start.8 = (bf16[8,64,128]{2,1,0:T(8,128)(2,1)S(1)}, bf16[8,64,128]{2,1,0:T(8,128)(2,1)S(1)}, u32[]{:S(2)}, u32[]{:S(2)}) collective-permute-start(bf16[8,64,128]{2,1,0:T(8,128)(2,1)S(1)} %get-tuple-element.26), channel_id=1, source_target_pairs={{0,24},{8,16},{16,8},{24,0},{1,25},{9,17},{17,9},{25,1},{2,26},{10... | collective-permute-start | bytes 393224 | tf_op jit(solution)/shard_map/ppermute | solution.py:34
  32.7 7.7 %collective-permute-start.5 = (bf16[8,64,128]{2,1,0:T(8,128)(2,1)S(1)}, bf16[8,64,128]{2,1,0:T(8,128)(2,1)S(1)}, u32[]{:S(2)}, u32[]{:S(2)}) collective-permute-start(bf16[8,64,128]{2,1,0:T(8,128)(2,1)S(1)} %get-tuple-element.23), channel_id=1, source_target_pairs={{0,8},{8,0},{16,24},{24,16},{1,9},{9,1},{17,25},{25,17},{2,10},{10... | collective-permute-start | bytes 393224 | tf_op jit(solution)/shard_map/ppermute | solution.py:34
  34.5 14.6 %collective-permute-start.7 = (bf16[8,64,128]{2,1,0:T(8,128)(2,1)S(1)}, bf16[8,64,128]{2,1,0:T(8,128)(2,1)S(1)}, u32[]{:S(2)}, u32[]{:S(2)}) collective-permute-start(bf16[8,64,128]{2,1,0:T(8,128)(2,1)S(1)} %get-tuple-element.25), channel_id=1, source_target_pairs={{0,16},{8,24},{16,0},{24,8},{1,17},{9,25},{17,1},{25,9},{2,18},{10... | collective-permute-start | bytes 393224 | tf_op jit(solution)/shard_map/ppermute | solution.py:34
  38.5 10.6 %collective-permute-start.9 = (bf16[8,64,128]{2,1,0:T(8,128)(2,1)S(1)}, bf16[8,64,128]{2,1,0:T(8,128)(2,1)S(1)}, u32[]{:S(2)}, u32[]{:S(2)}) collective-permute-start(bf16[8,64,128]{2,1,0:T(8,128)(2,1)S(1)} %get-tuple-element.27), channel_id=1, source_target_pairs={{0,24},{8,16},{16,8},{24,0},{1,25},{9,17},{17,9},{25,1},{2,26},{10... | collective-permute-start | bytes 393224 | tf_op jit(solution)/shard_map/ppermute | solution.py:34
  50.0 1.4 %collective-permute-start.10 = (f32[64,384]{1,0:T(8,128)S(1)}, f32[64,384]{1,0:T(8,128)S(1)}, u32[]{:S(2)}, u32[]{:S(2)}) collective-permute-start(f32[64,384]{1,0:T(8,128)S(1)} %get-tuple-element.29), channel_id=1, source_target_pairs={{0,1},{1,0},{2,3},{3,2},{4,5},{5,4},{6,7},{7,6},{8,9},{9,8},{10,11... | collective-permute-start | bytes 294920 | tf_op jit(solution)/shard_map/ppermute | solution.py:34
  51.4 4.2 %collective-permute-start.11 = (bf16[64,384]{1,0:T(8,128)(2,1)S(1)}, bf16[64,384]{1,0:T(8,128)(2,1)S(1)}, u32[]{:S(2)}, u32[]{:S(2)}) collective-permute-start(bf16[64,384]{1,0:T(8,128)(2,1)S(1)} %get-tuple-element.34), channel_id=1, source_target_pairs={{0,2},{1,3},{2,0},{3,1},{4,6},{5,7},{6,4},{7,5},{8,10},{9,11},{10,... | collective-permute-start | bytes 147464 | tf_op jit(solution)/shard_map/ppermute | solution.py:34
  52.2 4.1 %collective-permute-start.12 = (bf16[64,384]{1,0:T(8,128)(2,1)S(1)}, bf16[64,384]{1,0:T(8,128)(2,1)S(1)}, u32[]{:S(2)}, u32[]{:S(2)}) collective-permute-start(bf16[64,384]{1,0:T(8,128)(2,1)S(1)} %get-tuple-element.34), channel_id=1, source_target_pairs={{0,4},{1,5},{2,6},{3,7},{4,0},{5,1},{6,2},{7,3},{8,12},{9,13},{10,... | collective-permute-start | bytes 147464 | tf_op jit(solution)/shard_map/ppermute | solution.py:34
  53.4 5.0 %collective-permute-start.13 = (bf16[64,384]{1,0:T(8,128)(2,1)S(1)}, bf16[64,384]{1,0:T(8,128)(2,1)S(1)}, u32[]{:S(2)}, u32[]{:S(2)}) collective-permute-start(bf16[64,384]{1,0:T(8,128)(2,1)S(1)} %get-tuple-element.34), channel_id=1, source_target_pairs={{0,6},{1,7},{2,4},{3,5},{4,2},{5,3},{6,0},{7,1},{8,14},{9,15},{10,... | collective-permute-start | bytes 147464 | tf_op jit(solution)/shard_map/ppermute | solution.py:34
  58.4 5.9 %collective-permute-start.14 = (bf16[64,384]{1,0:T(8,128)(2,1)S(1)}, bf16[64,384]{1,0:T(8,128)(2,1)S(1)}, u32[]{:S(2)}, u32[]{:S(2)}) collective-permute-start(bf16[64,384]{1,0:T(8,128)(2,1)S(1)} %fusion.4), channel_id=1, source_target_pairs={{0,8},{8,0},{16,24},{24,16},{1,9},{9,1},{17,25},{25,17},{2,10},{10... | collective-permute-start | bytes 147464 | tf_op jit(solution)/shard_map/ppermute | solution.py:34
  61.8 5.5 %collective-permute-start.15 = (bf16[64,384]{1,0:T(8,128)(2,1)S(1)}, bf16[64,384]{1,0:T(8,128)(2,1)S(1)}, u32[]{:S(2)}, u32[]{:S(2)}) collective-permute-start(bf16[64,384]{1,0:T(8,128)(2,1)S(1)} %fusion.4), channel_id=1, source_target_pairs={{0,16},{8,24},{16,0},{24,8},{1,17},{9,25},{17,1},{25,9},{2,18},{10... | collective-permute-start | bytes 147464 | tf_op jit(solution)/shard_map/ppermute | solution.py:34
  62.8 6.0 %collective-permute-start.16 = (bf16[64,384]{1,0:T(8,128)(2,1)S(1)}, bf16[64,384]{1,0:T(8,128)(2,1)S(1)}, u32[]{:S(2)}, u32[]{:S(2)}) collective-permute-start(bf16[64,384]{1,0:T(8,128)(2,1)S(1)} %fusion.4), channel_id=1, source_target_pairs={{0,24},{8,16},{16,8},{24,0},{1,25},{9,17},{17,9},{25,1},{2,26},{10... | collective-permute-start | bytes 147464 | tf_op jit(solution)/shard_map/ppermute | solution.py:34
  68.9 1.4 %collective-permute-start.17 = (f32[64,384]{1,0:T(8,128)S(1)}, f32[64,384]{1,0:T(8,128)S(1)}, u32[]{:S(2)}, u32[]{:S(2)}) collective-permute-start(f32[64,384]{1,0:T(8,128)S(1)} %add_multiply_fusion.mine_ref), channel_id=1, source_target_pairs={{0,1},{1,0},{2,3},{3,2},{4,5},{5,4},{6,7},{7,6},{8,9},{9,8},{10,11... | collective-permute-start | bytes 294920 | tf_op jit(solution)/shard_map/ppermute | solution.py:34
  77.9 7.4 %collective-permute-start.18 = (bf16[2,32,1,8,128]{4,3,2,1,0:T(8,128)(2,1)S(1)}, bf16[2,32,1,8,128]{4,3,2,1,0:T(8,128)(2,1)S(1)}, u32[]{:S(2)}, u32[]{:S(2)}) collective-permute-start(bf16[2,32,1,8,128]{4,3,2,1,0:T(8,128)(2,1)S(1)} %get-tuple-element.31), channel_id=1, source_target_pairs={{0,8},{8,0},{16,24},{24,16},{1,9},{9,1},{17,25},{25,17},{2,10},{10... | collective-permute-start | bytes 393224 | tf_op jit(solution)/shard_map/ppermute | solution.py:34
  78.6 12.8 %collective-permute-start.19 = (bf16[2,32,1,8,128]{4,3,2,1,0:T(8,128)(2,1)S(1)}, bf16[2,32,1,8,128]{4,3,2,1,0:T(8,128)(2,1)S(1)}, u32[]{:S(2)}, u32[]{:S(2)}) collective-permute-start(bf16[2,32,1,8,128]{4,3,2,1,0:T(8,128)(2,1)S(1)} %get-tuple-element.32), channel_id=1, source_target_pairs={{0,16},{8,24},{16,0},{24,8},{1,17},{9,25},{17,1},{25,9},{2,18},{10... | collective-permute-start | bytes 393224 | tf_op jit(solution)/shard_map/ppermute | solution.py:34
  80.0 11.4 %collective-permute-start.20 = (bf16[2,32,1,8,128]{4,3,2,1,0:T(8,128)(2,1)S(1)}, bf16[2,32,1,8,128]{4,3,2,1,0:T(8,128)(2,1)S(1)}, u32[]{:S(2)}, u32[]{:S(2)}) collective-permute-start(bf16[2,32,1,8,128]{4,3,2,1,0:T(8,128)(2,1)S(1)} %get-tuple-element.33), channel_id=1, source_target_pairs={{0,24},{8,16},{16,8},{24,0},{1,25},{9,17},{17,9},{25,1},{2,26},{10... | collective-permute-start | bytes 393224 | tf_op jit(solution)/shard_map/ppermute | solution.py:34

commit v5 on v4

--- a/solution.py
+++ b/solution.py
@@ -232,75 +232,75 @@
     )(where, *blocks)
 
 
-def invert(system):
+def invert(system, held):
     size = system.shape[0]
-    panels = [system[8 * i:8 * i + 8] for i in range(size // 8)]
+    count = size // 8
+    panels = [system[8 * i:8 * i + 8] for i in range(count)]
     lane = lax.broadcasted_iota(jnp.int32, (8, size), 1)
     row = lax.broadcasted_iota(jnp.int32, (8, size), 0)
 
-    def spread_lane(panel, j):
+    def spread(panel, j):
         return jnp.broadcast_to(panel[:, j:j + 1], (8, size))
 
-    def spread_row(value, j):
-        return jnp.broadcast_to(value[j:j + 1], (8, size))
-
-    def small_inverse(a, b, d):
-        det = a * d - b * b
-        guess = pl.reciprocal(det, approx=True)
-        guess = guess * (2.0 - det * guess)
-        det = guess * (2.0 - det * guess)
-        return d * det, -b * det, a * det
-
-    for p in range(size // 8):
-        for h in range(2):
-            base = 8 * p + 4 * h
-            lead = panels[p]
-            cols = [spread_lane(lead, base + j) for j in range(4)]
-            m = [[spread_row(cols[j], 4 * h + i) for j in range(4)] for i in range(4)]
-            a0, a1, a2 = small_inverse(m[0][0], m[0][1], m[1][1])
-            b00, b01, b10, b11 = m[0][2], m[0][3], m[1][2], m[1][3]
-            x00, x01 = a0 * b00 + a1 * b10, a0 * b01 + a1 * b11
-            x10, x11 = a1 * b00 + a2 * b10, a1 * b01 + a2 * b11
-            s0 = m[2][2] - (b00 * x00 + b10 * x10)
-            s1 = m[2][3] - (b00 * x01 + b10 * x11)
-            s2 = m[3][3] - (b01 * x01 + b11 * x11)
-            d0, d1, d2 = small_inverse(s0, s1, s2)
-            y00, y01 = x00 * d0 + x01 * d1, x00 * d1 + x01 * d2
-            y10, y11 = x10 * d0 + x11 * d1, x10 * d1 + x11 * d2
-            inv = [
-                [a0 + y00 * x00 + y01 * x01, a1 + y00 * x10 + y01 * x11, -y00, -y01],
-                [None, a2 + y10 * x10 + y11 * x11, -y10, -y11],
-                [None, None, d0, d1],
-                [None, None, None, d2],
-            ]
-            for i in range(4):
-                for j in range(i):
-                    inv[i][j] = inv[j][i]
-            rows4 = [spread_row(lead, 4 * h + i) for i in range(4)]
-            for i in range(4):
-                for j in range(4):
-                    rows4[i] = jnp.where(lane == base + j, f32(1.0 if i == j else 0.0), rows4[i])
-            new = [sum(inv[i][j] * rows4[j] for j in range(4)) for i in range(4)]
-            block = (lane >= base) & (lane < base + 4)
-            for q in range(size // 8):
-                target = panels[q]
-                kept = jnp.where(block, f32(0.0), target)
-                if q == p:
-                    factors = cols
-                else:
-                    factors = [spread_lane(target, base + j) for j in range(4)]
-                out = kept - sum(factors[j] * new[j] for j in range(4))
-                if q == p:
-                    for i in range(4):
-                        out = jnp.where(row == 4 * h + i, new[i], out)
-                panels[q] = out
+    def reciprocal(value):
+        guess = pl.reciprocal(value, approx=True)
+        guess = guess * (2.0 - value * guess)
+        return guess * (2.0 - value * guess)
+
+    for p in range(count):
+        base, slot = 8 * p, p % 2
+        lead = panels[p]
+        for j in range(8):
+            held[slot, 8 * j:8 * j + 8, :] = spread(lead, base + j)
+        held[slot, 64:72, :] = lead
+
+        def row_of(at, slot=slot):
+            return jnp.broadcast_to(held[slot, at:at + 1, :], (8, size))
+
+        m = {(i, j): row_of(8 * j + i) for j in range(8) for i in range(j + 1)}
+        block = (lane >= base) & (lane < base + 8)
+        r = [jnp.where(lane == base + i, f32(1.0), jnp.where(block, f32(0.0), row_of(64 + i)))
+             for i in range(8)]
+        blocks, x = [], {}
+        for i in range(0, 8, 2):
+            a, b, d = m[i, i], m[i, i + 1], m[i + 1, i + 1]
+            det = reciprocal(a * d - b * b)
+            v0, v1, v2 = d * det, -b * det, a * det
+            blocks.append((v0, v1, v2))
+            for j in range(i + 2, 8):
+                x[i, j] = v0 * m[i, j] + v1 * m[i + 1, j]
+                x[i + 1, j] = v1 * m[i, j] + v2 * m[i + 1, j]
+            for j in range(i + 2, 8):
+                for h in range(i + 2, j + 1):
+                    m[h, j] = m[h, j] - (m[i, h] * x[i, j] + m[i + 1, h] * x[i + 1, j])
+            for j in range(i + 2, 8):
+                r[j] = r[j] - (x[i, j] * r[i] + x[i + 1, j] * r[i + 1])
+        new = [None] * 8
+        for i in (6, 4, 2, 0):
+            v0, v1, v2 = blocks[i // 2]
+            top = v0 * r[i] + v1 * r[i + 1]
+            low = v1 * r[i] + v2 * r[i + 1]
+            for j in range(i + 2, 8):
+                top = top - x[i, j] * new[j]
+                low = low - x[i + 1, j] * new[j]
+            new[i], new[i + 1] = top, low
+        for q in [(p + 1 + z) % count for z in range(count)]:
+            target = panels[q]
+            if q == p:
+                out = new[0]
+                for i in range(1, 8):
+                    out = jnp.where(row == i, new[i], out)
+            else:
+                out = jnp.where(block, f32(0.0), target)
+                out = out - sum(spread(target, base + j) * new[j] for j in range(8))
+            panels[q] = out
     return jnp.concatenate(panels, axis=0)
 
 
 def modes_kernel(groups, chunks, where_ref, mine_ref, other_ref, *rest):
     blocks = rest[:groups * chunks]
     outs = rest[groups * chunks:groups * (chunks + 1)]
-    coupling_ref, stage = rest[groups * (chunks + 1):]
+    coupling_ref, stage, held = rest[groups * (chunks + 1):]
     me, half = where_ref[0], where_ref[1]
     mid = mine_ref.shape[0]
     snaps = 2 * mid
@@ -315,7 +315,7 @@
     diagonal = jnp.where(r == c, gram, 0.0)
     energy = jnp.sum(jnp.sum(diagonal, axis=0, keepdims=True), axis=1, keepdims=True) / snaps
     system = gram / energy + jnp.where(r == c, f32(damping), f32(0.0))
-    inverse = invert(system)
+    inverse = invert(system, held)
     weights = jnp.dot(inverse, coupled, precision=lax.Precision.HIGHEST,
                       preferred_element_type=f32) / jnp.sqrt(energy)
     weights = weights.astype(bf16)
@@ -359,7 +359,8 @@
         in_specs=[smem, vmem, vmem] + [vmem] * len(blocks),
         out_specs=[vmem] * groups,
         scratch_shapes=[pltpu.VMEM((snaps, mine.shape[1]), f32),
-                        pltpu.VMEM((2, layers, snaps * ny, nz), f32)],
+                        pltpu.VMEM((2, layers, snaps * ny, nz), f32),
+                        pltpu.VMEM((2, 72, snaps), f32)],
         compiler_params=pltpu.CompilerParams(vmem_limit_bytes=VMEM_LIMIT),
         name="modes",
     )(where, mine, other, *blocks)

time: 93 us -> 91 us (0.978)
  Pallas kernels: 16.9 us -> 14.9 us
    pallas_call x1, Pallas kernels: 7.67 us -> 5.65 us  [modes(): pl.pallas_call(functools.partial(modes_kernel, groups, chunks), out_shape...]
where the time goes in v5:
time: 91 us; the launch traced here: 90.8 us
  waiting for transfers between devices  42.1 us (46%)
  starting transfers between devices  30.9 us (34%)
  Pallas kernels  14.9 us (16%)
  local copies, waits for them, and re-layouts  1.22 us (1%)
  other arithmetic  0.94 us (1%)
    ppermute x17, waiting for transfers between devices, swap(): return lax.ppermute(value, axis, [(i, i ^ step) for i in range(count)])  30.2 us
    ppermute x17, starting transfers between devices, swap(): return lax.ppermute(value, axis, [(i, i ^ step) for i in range(count)])  24.7 us
    ppermute x4, waiting for transfers between devices, shift(): lax.ppermute(value, axis, [(i, (i + step) % count) for i in range(count)])  11.9 us
    pallas_call x2, Pallas kernels, sections(): pl.pallas_call(functools.partial(sections_kernel, groups, rows, ny, lead)...  6.35 us
    ppermute x4, starting transfers between devices, shift(): lax.ppermute(value, axis, [(i, (i + step) % count) for i in range(count)])  6.14 us
    pallas_call x1, Pallas kernels, modes(): pl.pallas_call(functools.partial(modes_kernel, groups, chunks), out_shape...  5.65 us
  transfers between devices with their start and end apart: 21, of which 16 were waited for; matrix products, arithmetic and copies ran while one was open for 0% of the time, Pallas kernels for 7%

profile of v5, /device:TPU:0, one launch (start us, length us, event | category | flops | bytes accessed | tf_op | source)
XLA Modules:
  0.0 90.8 jit_solution(5759501713083047512)
XLA Ops:
  3.4 2.9 %collective-permute-start.1 = (bf16[34,64,128]{2,1,0:T(8,128)(2,1)S(1)}, bf16[34,64,128]{2,1,0:T(8,128)(2,1)S(1)}, u32[]{:S(2)}, u32[]{:S(2)}) collective-permute-start(bf16[34,64,128]{2,1,0:T(8,128)(2,1)S(1)} %pack.2.rest_1_), channel_id=1, source_target_pairs={{0,7},{1,0},{2,1},{3,2},{4,3},{5,4},{6,5},{7,6},{8,15},{9,8},{10,9... | collective-permute-start | bytes 1671176 | tf_op jit(solution)/shard_map/ppermute | solution.py:39
  6.7 2.6 %collective-permute-start.3 = (bf16[32,64,128]{2,1,0:T(8,128)(2,1)S(1)}, bf16[32,64,128]{2,1,0:T(8,128)(2,1)S(1)}, u32[]{:S(2)}, u32[]{:S(2)}) collective-permute-start(bf16[32,64,128]{2,1,0:T(8,128)(2,1)S(1)} %pack.3.rest_2_), channel_id=1, source_target_pairs={{0,7},{1,0},{2,1},{3,2},{4,3},{5,4},{6,5},{7,6},{8,15},{9,8},{10,9... | collective-permute-start | bytes 1572872 | tf_op jit(solution)/shard_map/ppermute | solution.py:39
  9.4 7.3 %collective-permute-done.rest_2_ = bf16[34,64,128]{2,1,0:T(8,128)(2,1)S(1)} collective-permute-done((bf16[34,64,128]{2,1,0:T(8,128)(2,1)S(1)}, bf16[34,64,128]{2,1,0:T(8,128)(2,1)S(1)}, u32[]{:S(2)}, u32[]{:S(2)}) %collective-permute-start) | collective-permute-done | bytes 557088 | tf_op jit(solution)/shard_map/ppermute | solution.py:39
  16.8 2.6 %collective-permute-done.1.rest_3_ = bf16[34,64,128]{2,1,0:T(8,128)(2,1)S(1)} collective-permute-done((bf16[34,64,128]{2,1,0:T(8,128)(2,1)S(1)}, bf16[34,64,128]{2,1,0:T(8,128)(2,1)S(1)}, u32[]{:S(2)}, u32[]{:S(2)}) %collective-permute-start.1) | collective-permute-done | bytes 557088 | tf_op jit(solution)/shard_map/ppermute | solution.py:39
  19.3 3.2 %sections.2 = (bf16[8,64,128]{2,1,0:T(8,128)(2,1)S(1)}, bf16[8,64,128]{2,1,0:T(8,128)(2,1)S(1)}, bf16[8,64,128]{2,1,0:T(8,128)(2,1)S(1)}, bf16[8,64,128]{2,1,0:T...) custom-call(s32[2]{0:T(128)S(1)} %pad_add_fusion.where_ref, ...), custom_call_target="tpu_custom_call" | custom-call | flops 25165824 | bytes 2097152 | tf_op jit(solution)/shard_map/sections/pallas_call | solution.py:173
  22.5 2.4 %collective-permute-start.4 = (bf16[8,64,128]{2,1,0:T(8,128)(2,1)S(1)}, bf16[8,64,128]{2,1,0:T(8,128)(2,1)S(1)}, u32[]{:S(2)}, u32[]{:S(2)}) collective-permute-start(bf16[8,64,128]{2,1,0:T(8,128)(2,1)S(1)} %get-tuple-element.21), channel_id=1, source_target_pairs={{0,8},{8,0},{16,24},{24,16},{1,9},{9,1},{17,25},{25,17},{2,10},{10... | collective-permute-start | bytes 393224 | tf_op jit(solution)/shard_map/ppermute | solution.py:34
  24.9 2.6 %collective-permute-start.6 = (bf16[8,64,128]{2,1,0:T(8,128)(2,1)S(1)}, bf16[8,64,128]{2,1,0:T(8,128)(2,1)S(1)}, u32[]{:S(2)}, u32[]{:S(2)}) collective-permute-start(bf16[8,64,128]{2,1,0:T(8,128)(2,1)S(1)} %get-tuple-element.24), channel_id=1, source_target_pairs={{0,16},{8,24},{16,0},{24,8},{1,17},{9,25},{17,1},{25,9},{2,18},{10... | collective-permute-start | bytes 393224 | tf_op jit(solution)/shard_map/ppermute | solution.py:34
  28.0 1.5 %collective-permute-done.3.rest_4_ = bf16[32,64,128]{2,1,0:T(8,128)(2,1)S(1)} collective-permute-done((bf16[32,64,128]{2,1,0:T(8,128)(2,1)S(1)}, bf16[32,64,128]{2,1,0:T(8,128)(2,1)S(1)}, u32[]{:S(2)}, u32[]{:S(2)}) %collective-permute-start.3) | collective-permute-done | bytes 524320 | tf_op jit(solution)/shard_map/ppermute | solution.py:39
  29.5 3.2 %sections.3 = (bf16[8,64,128]{2,1,0:T(8,128)(2,1)S(1)}, bf16[8,64,128]{2,1,0:T(8,128)(2,1)S(1)}, bf16[8,64,128]{2,1,0:T(8,128)(2,1)S(1)}, bf16[8,64,128]{2,1,0:T(8,128)(2,1)S(1)}) custom-call(s32[2]{0:T(128)S(1)} %pad_add_fusion.where_ref, bf16[128,128]{1,0:T(8,128)(2,1)S(1)} %add_convert_fusion.ring_ref, f32[12,8,128]{2,1,0:T(8,128)S(1)} %get-tuple-element.19.rest_0_, ...), custom_call_target="tpu_custom_call" | custom-call | flops 25165824 | bytes 2097152 | tf_op jit(solution)/shard_map/sections/pallas_call | solution.py:173
  32.7 1.7 %collective-permute-start.5 = (bf16[8,64,128]{2,1,0:T(8,128)(2,1)S(1)}, bf16[8,64,128]{2,1,0:T(8,128)(2,1)S(1)}, u32[]{:S(2)}, u32[]{:S(2)}) collective-permute-start(bf16[8,64,128]{2,1,0:T(8,128)(2,1)S(1)} %get-tuple-element.23), channel_id=1, source_target_pairs={{0,8},{8,0},{16,24},{24,16},{1,9},{9,1},{17,25},{25,17},{2,10},{10... | collective-permute-start | bytes 393224 | tf_op jit(solution)/shard_map/ppermute | solution.py:34
  34.5 4.0 %collective-permute-start.7 = (bf16[8,64,128]{2,1,0:T(8,128)(2,1)S(1)}, bf16[8,64,128]{2,1,0:T(8,128)(2,1)S(1)}, u32[]{:S(2)}, u32[]{:S(2)}) collective-permute-start(bf16[8,64,128]{2,1,0:T(8,128)(2,1)S(1)} %get-tuple-element.25), channel_id=1, source_target_pairs={{0,16},{8,24},{16,0},{24,8},{1,17},{9,25},{17,1},{25,9},{2,18},{10... | collective-permute-start | bytes 393224 | tf_op jit(solution)/shard_map/ppermute | solution.py:34
  38.5 1.9 %collective-permute-done.5.rest_3_ = bf16[8,64,128]{2,1,0:T(8,128)(2,1)S(1)} collective-permute-done((bf16[8,64,128]{2,1,0:T(8,128)(2,1)S(1)}, bf16[8,64,128]{2,1,0:T(8,128)(2,1)S(1)}, u32[]{:S(2)}, u32[]{:S(2)}) %collective-permute-start.5) | collective-permute-done | bytes 131104 | tf_op jit(solution)/shard_map/ppermute | solution.py:34
  40.5 8.6 %collective-permute-done.7.rest_5_ = bf16[8,64,128]{2,1,0:T(8,128)(2,1)S(1)} collective-permute-done((bf16[8,64,128]{2,1,0:T(8,128)(2,1)S(1)}, bf16[8,64,128]{2,1,0:T(8,128)(2,1)S(1)}, u32[]{:S(2)}, u32[]{:S(2)}) %collective-permute-start.7) | collective-permute-done | bytes 131104 | tf_op jit(solution)/shard_map/ppermute | solution.py:34
  53.4 1.6 %collective-permute-start.13 = (bf16[64,384]{1,0:T(8,128)(2,1)S(1)}, bf16[64,384]{1,0:T(8,128)(2,1)S(1)}, u32[]{:S(2)}, u32[]{:S(2)}) collective-permute-start(bf16[64,384]{1,0:T(8,128)(2,1)S(1)} %get-tuple-element.34), channel_id=1, source_target_pairs={{0,6},{1,7},{2,4},{3,5},{4,2},{5,3},{6,0},{7,1},{8,14},{9,15},{10,... | collective-permute-start | bytes 147464 | tf_op jit(solution)/shard_map/ppermute | solution.py:34
  56.3 2.1 %collective-permute-done.13 = bf16[64,384]{1,0:T(8,128)(2,1)S(1)} collective-permute-done((bf16[64,384]{1,0:T(8,128)(2,1)S(1)}, bf16[64,384]{1,0:T(8,128)(2,1)S(1)}, u32[]{:S(2)}, u32[]{:S(2)}) %collective-permute-start.13) | collective-permute-done | bytes 49184 | tf_op jit(solution)/shard_map/ppermute | solution.py:34
  58.4 3.3 %collective-permute-start.14 = (bf16[64,384]{1,0:T(8,128)(2,1)S(1)}, bf16[64,384]{1,0:T(8,128)(2,1)S(1)}, u32[]{:S(2)}, u32[]{:S(2)}) collective-permute-start(bf16[64,384]{1,0:T(8,128)(2,1)S(1)} %fusion.4), channel_id=1, source_target_pairs={{0,8},{8,0},{16,24},{24,16},{1,9},{9,1},{17,25},{25,17},{2,10},{10... | collective-permute-start | bytes 147464 | tf_op jit(solution)/shard_map/ppermute | solution.py:34
  62.8 1.4 %collective-permute-start.16 = (bf16[64,384]{1,0:T(8,128)(2,1)S(1)}, bf16[64,384]{1,0:T(8,128)(2,1)S(1)}, u32[]{:S(2)}, u32[]{:S(2)}) collective-permute-start(bf16[64,384]{1,0:T(8,128)(2,1)S(1)} %fusion.4), channel_id=1, source_target_pairs={{0,24},{8,16},{16,8},{24,0},{1,25},{9,17},{17,9},{25,1},{2,26},{10... | collective-permute-start | bytes 147464 | tf_op jit(solution)/shard_map/ppermute | solution.py:34
  64.3 3.0 %collective-permute-done.15 = bf16[64,384]{1,0:T(8,128)(2,1)S(1)} collective-permute-done((bf16[64,384]{1,0:T(8,128)(2,1)S(1)}, bf16[64,384]{1,0:T(8,128)(2,1)S(1)}, u32[]{:S(2)}, u32[]{:S(2)}) %collective-permute-start.15) | collective-permute-done | bytes 49184 | tf_op jit(solution)/shard_map/ppermute | solution.py:34
  67.3 1.6 %collective-permute-done.16 = bf16[64,384]{1,0:T(8,128)(2,1)S(1)} collective-permute-done((bf16[64,384]{1,0:T(8,128)(2,1)S(1)}, bf16[64,384]{1,0:T(8,128)(2,1)S(1)}, u32[]{:S(2)}, u32[]{:S(2)}) %collective-permute-start.16) | collective-permute-done | bytes 49184 | tf_op jit(solution)/shard_map/ppermute | solution.py:34
  70.3 5.6 %modes.1 = (bf16[2,32,1,8,128]{4,3,2,1,0:T(8,128)(2,1)S(1)}, bf16[2,32,1,8,128]{4,3,2,1,0:T(8,128)(2,1)S(1)}, bf16[2,32,1,8,128]{4,3,2,1,0:T(8,128)(2,1)S(1)}, bf16[2,32,1,8,128]{4,3,2,1,0:T(8,128)(2,1)S(1)}) custom-call(s32[2]{0:T(128)S(1)} %pad_add_fusion.where_ref, f32[64,384]{1,0:T(8,128)S(1)} %add_multiply_fusion.mine_ref, ...), custom_call_target="tpu_custom_call" | custom-call | tf_op jit(solution)/shard_map/modes/pallas_call | solution.py:356
  77.9 2.4 %collective-permute-start.20 = (bf16[2,32,1,8,128]{4,3,2,1,0:T(8,128)(2,1)S(1)}, bf16[2,32,1,8,128]{4,3,2,1,0:T(8,128)(2,1)S(1)}, u32[]{:S(2)}, u32[]{:S(2)}) collective-permute-start(bf16[2,32,1,8,128]{4,3,2,1,0:T(8,128)(2,1)S(1)} %get-tuple-element.33), channel_id=1, source_target_pairs={{0,24},{8,16},{16,8},{24,0},{1,25},{9,17},{17,9},{25,1},{2,26},{10... | collective-permute-start | bytes 393224 | tf_op jit(solution)/shard_map/ppermute | solution.py:34
  80.4 2.9 %collective-permute-done.18.rest_1_ = bf16[2,32,1,8,128]{4,3,2,1,0:T(8,128)(2,1)S(1)} collective-permute-done((bf16[2,32,1,8,128]{4,3,2,1,0:T(8,128)(2,1)S(1)}, bf16[2,32,1,8,128]{4,3,2,1,0:T(8,128)(2,1)S(1)}, u32[]{:S(2)}, u32[]{:S(2)}) %collective-permute-start.18) | collective-permute-done | bytes 131104 | tf_op jit(solution)/shard_map/ppermute | solution.py:34
  83.3 6.1 %collective-permute-done.19.rest_2_ = bf16[2,32,1,8,128]{4,3,2,1,0:T(8,128)(2,1)S(1)} collective-permute-done((bf16[2,32,1,8,128]{4,3,2,1,0:T(8,128)(2,1)S(1)}, bf16[2,32,1,8,128]{4,3,2,1,0:T(8,128)(2,1)S(1)}, u32[]{:S(2)}, u32[]{:S(2)}) %collective-permute-start.19) | collective-permute-done | bytes 131104 | tf_op jit(solution)/shard_map/ppermute | solution.py:34
  89.4 1.4 %place.1 = (bf16[32,4,8,128]{3,2,1,0:T(8,128)(2,1)}, bf16[32,4,8,128]{3,2,1,0:T(8,128)(2,1)}) custom-call(s32[2]{0:T(128)S(1)} %pad_add_fusion.where_ref, bf16[2,32,1,8,128]{4,3,2,1,0:T(8,128)(2,1)S(1)} %get-tuple-element.30.rest_0_, bf16[2,32,1,8,128]{4,3,2,1,0:T(8,128)(2,1)S(1)} %collective-permute-done.18.rest_1_, ...), custom_call_target="tpu_custom_call" | custom-call | tf_op jit(solution)/shard_map/place/pallas_call | solution.py:383
  (33 shorter events, 13.9 us)
Async XLA Ops:
  1.4 1.2 %copy-start = (bf16[1,128,4,8,128]{4,3,2,1,0:T(8,128)(2,1)S(1)}, bf16[1,128,4,8,128]{4,3,2,1,0:T(8,128)(2,1)}, u32[]{:S(2)}) copy-start(bf16[1,128,4,8,128]{4,3,2,1,0:T(8,128)(2,1)} %param.2) | copy-start | bytes 3145732
  2.9 13.9 %collective-permute-start = (bf16[34,64,128]{2,1,0:T(8,128)(2,1)S(1)}, bf16[34,64,128]{2,1,0:T(8,128)(2,1)S(1)}, u32[]{:S(2)}, u32[]{:S(2)}) collective-permute-start(bf16[34,64,128]{2,1,0:T(8,128)(2,1)S(1)} %pack.2.rest_1_), channel_id=1, source_target_pairs={{0,1},{1,2},{2,3},{3,4},{4,5},{5,6},{6,7},{7,0},{8,9},{9,10},{10,1... | collective-permute-start | bytes 1671176 | tf_op jit(solution)/shard_map/ppermute | solution.py:39
  3.4 16.0 %collective-permute-start.1 = (bf16[34,64,128]{2,1,0:T(8,128)(2,1)S(1)}, bf16[34,64,128]{2,1,0:T(8,128)(2,1)S(1)}, u32[]{:S(2)}, u32[]{:S(2)}) collective-permute-start(bf16[34,64,128]{2,1,0:T(8,128)(2,1)S(1)} %pack.2.rest_1_), channel_id=1, source_target_pairs={{0,7},{1,0},{2,1},{3,2},{4,3},{5,4},{6,5},{7,6},{8,15},{9,8},{10,9... | collective-permute-start | bytes 1671176 | tf_op jit(solution)/shard_map/ppermute | solution.py:39
  6.6 21.4 %collective-permute-start.2 = (bf16[32,64,128]{2,1,0:T(8,128)(2,1)S(1)}, bf16[32,64,128]{2,1,0:T(8,128)(2,1)S(1)}, u32[]{:S(2)}, u32[]{:S(2)}) collective-permute-start(bf16[32,64,128]{2,1,0:T(8,128)(2,1)S(1)} %pack.3.rest_2_), channel_id=1, source_target_pairs={{0,1},{1,2},{2,3},{3,4},{4,5},{5,6},{6,7},{7,0},{8,9},{9,10},{10,1... | collective-permute-start | bytes 1572872 | tf_op jit(solution)/shard_map/ppermute | solution.py:39
  6.7 22.9 %collective-permute-start.3 = (bf16[32,64,128]{2,1,0:T(8,128)(2,1)S(1)}, bf16[32,64,128]{2,1,0:T(8,128)(2,1)S(1)}, u32[]{:S(2)}, u32[]{:S(2)}) collective-permute-start(bf16[32,64,128]{2,1,0:T(8,128)(2,1)S(1)} %pack.3.rest_2_), channel_id=1, source_target_pairs={{0,7},{1,0},{2,1},{3,2},{4,3},{5,4},{6,5},{7,6},{8,15},{9,8},{10,9... | collective-permute-start | bytes 1572872 | tf_op jit(solution)/shard_map/ppermute | solution.py:39
  22.5 7.0 %collective-permute-start.4 = (bf16[8,64,128]{2,1,0:T(8,128)(2,1)S(1)}, bf16[8,64,128]{2,1,0:T(8,128)(2,1)S(1)}, u32[]{:S(2)}, u32[]{:S(2)}) collective-permute-start(bf16[8,64,128]{2,1,0:T(8,128)(2,1)S(1)} %get-tuple-element.21), channel_id=1, source_target_pairs={{0,8},{8,0},{16,24},{24,16},{1,9},{9,1},{17,25},{25,17},{2,10},{10... | collective-permute-start | bytes 393224 | tf_op jit(solution)/shard_map/ppermute | solution.py:34
  24.9 13.6 %collective-permute-start.6 = (bf16[8,64,128]{2,1,0:T(8,128)(2,1)S(1)}, bf16[8,64,128]{2,1,0:T(8,128)(2,1)S(1)}, u32[]{:S(2)}, u32[]{:S(2)}) collective-permute-start(bf16[8,64,128]{2,1,0:T(8,128)(2,1)S(1)} %get-tuple-element.24), channel_id=1, source_target_pairs={{0,16},{8,24},{16,0},{24,8},{1,17},{9,25},{17,1},{25,9},{2,18},{10... | collective-permute-start | bytes 393224 | tf_op jit(solution)/shard_map/ppermute | solution.py:34
  27.5 11.0 %collective-permute-start.8 = (bf16[8,64,128]{2,1,0:T(8,128)(2,1)S(1)}, bf16[8,64,128]{2,1,0:T(8,128)(2,1)S(1)}, u32[]{:S(2)}, u32[]{:S(2)}) collective-permute-start(bf16[8,64,128]{2,1,0:T(8,128)(2,1)S(1)} %get-tuple-element.26), channel_id=1, source_target_pairs={{0,24},{8,16},{16,8},{24,0},{1,25},{9,17},{17,9},{25,1},{2,26},{10... | collective-permute-start | bytes 393224 | tf_op jit(solution)/shard_map/ppermute | solution.py:34
  32.7 7.7 %collective-permute-start.5 = (bf16[8,64,128]{2,1,0:T(8,128)(2,1)S(1)}, bf16[8,64,128]{2,1,0:T(8,128)(2,1)S(1)}, u32[]{:S(2)}, u32[]{:S(2)}) collective-permute-start(bf16[8,64,128]{2,1,0:T(8,128)(2,1)S(1)} %get-tuple-element.23), channel_id=1, source_target_pairs={{0,8},{8,0},{16,24},{24,16},{1,9},{9,1},{17,25},{25,17},{2,10},{10... | collective-permute-start | bytes 393224 | tf_op jit(solution)/shard_map/ppermute | solution.py:34
  34.5 14.6 %collective-permute-start.7 = (bf16[8,64,128]{2,1,0:T(8,128)(2,1)S(1)}, bf16[8,64,128]{2,1,0:T(8,128)(2,1)S(1)}, u32[]{:S(2)}, u32[]{:S(2)}) collective-permute-start(bf16[8,64,128]{2,1,0:T(8,128)(2,1)S(1)} %get-tuple-element.25), channel_id=1, source_target_pairs={{0,16},{8,24},{16,0},{24,8},{1,17},{9,25},{17,1},{25,9},{2,18},{10... | collective-permute-start | bytes 393224 | tf_op jit(solution)/shard_map/ppermute | solution.py:34
  38.5 10.6 %collective-permute-start.9 = (bf16[8,64,128]{2,1,0:T(8,128)(2,1)S(1)}, bf16[8,64,128]{2,1,0:T(8,128)(2,1)S(1)}, u32[]{:S(2)}, u32[]{:S(2)}) collective-permute-start(bf16[8,64,128]{2,1,0:T(8,128)(2,1)S(1)} %get-tuple-element.27), channel_id=1, source_target_pairs={{0,24},{8,16},{16,8},{24,0},{1,25},{9,17},{17,9},{25,1},{2,26},{10... | collective-permute-start | bytes 393224 | tf_op jit(solution)/shard_map/ppermute | solution.py:34
  50.0 1.4 %collective-permute-start.10 = (f32[64,384]{1,0:T(8,128)S(1)}, f32[64,384]{1,0:T(8,128)S(1)}, u32[]{:S(2)}, u32[]{:S(2)}) collective-permute-start(f32[64,384]{1,0:T(8,128)S(1)} %get-tuple-element.29), channel_id=1, source_target_pairs={{0,1},{1,0},{2,3},{3,2},{4,5},{5,4},{6,7},{7,6},{8,9},{9,8},{10,11... | collective-permute-start | bytes 294920 | tf_op jit(solution)/shard_map/ppermute | solution.py:34
  51.4 4.2 %collective-permute-start.11 = (bf16[64,384]{1,0:T(8,128)(2,1)S(1)}, bf16[64,384]{1,0:T(8,128)(2,1)S(1)}, u32[]{:S(2)}, u32[]{:S(2)}) collective-permute-start(bf16[64,384]{1,0:T(8,128)(2,1)S(1)} %get-tuple-element.34), channel_id=1, source_target_pairs={{0,2},{1,3},{2,0},{3,1},{4,6},{5,7},{6,4},{7,5},{8,10},{9,11},{10,... | collective-permute-start | bytes 147464 | tf_op jit(solution)/shard_map/ppermute | solution.py:34
  52.2 4.1 %collective-permute-start.12 = (bf16[64,384]{1,0:T(8,128)(2,1)S(1)}, bf16[64,384]{1,0:T(8,128)(2,1)S(1)}, u32[]{:S(2)}, u32[]{:S(2)}) collective-permute-start(bf16[64,384]{1,0:T(8,128)(2,1)S(1)} %get-tuple-element.34), channel_id=1, source_target_pairs={{0,4},{1,5},{2,6},{3,7},{4,0},{5,1},{6,2},{7,3},{8,12},{9,13},{10,... | collective-permute-start | bytes 147464 | tf_op jit(solution)/shard_map/ppermute | solution.py:34
  53.4 5.0 %collective-permute-start.13 = (bf16[64,384]{1,0:T(8,128)(2,1)S(1)}, bf16[64,384]{1,0:T(8,128)(2,1)S(1)}, u32[]{:S(2)}, u32[]{:S(2)}) collective-permute-start(bf16[64,384]{1,0:T(8,128)(2,1)S(1)} %get-tuple-element.34), channel_id=1, source_target_pairs={{0,6},{1,7},{2,4},{3,5},{4,2},{5,3},{6,0},{7,1},{8,14},{9,15},{10,... | collective-permute-start | bytes 147464 | tf_op jit(solution)/shard_map/ppermute | solution.py:34
  58.4 5.9 %collective-permute-start.14 = (bf16[64,384]{1,0:T(8,128)(2,1)S(1)}, bf16[64,384]{1,0:T(8,128)(2,1)S(1)}, u32[]{:S(2)}, u32[]{:S(2)}) collective-permute-start(bf16[64,384]{1,0:T(8,128)(2,1)S(1)} %fusion.4), channel_id=1, source_target_pairs={{0,8},{8,0},{16,24},{24,16},{1,9},{9,1},{17,25},{25,17},{2,10},{10... | collective-permute-start | bytes 147464 | tf_op jit(solution)/shard_map/ppermute | solution.py:34
  61.8 5.5 %collective-permute-start.15 = (bf16[64,384]{1,0:T(8,128)(2,1)S(1)}, bf16[64,384]{1,0:T(8,128)(2,1)S(1)}, u32[]{:S(2)}, u32[]{:S(2)}) collective-permute-start(bf16[64,384]{1,0:T(8,128)(2,1)S(1)} %fusion.4), channel_id=1, source_target_pairs={{0,16},{8,24},{16,0},{24,8},{1,17},{9,25},{17,1},{25,9},{2,18},{10... | collective-permute-start | bytes 147464 | tf_op jit(solution)/shard_map/ppermute | solution.py:34
  62.8 6.0 %collective-permute-start.16 = (bf16[64,384]{1,0:T(8,128)(2,1)S(1)}, bf16[64,384]{1,0:T(8,128)(2,1)S(1)}, u32[]{:S(2)}, u32[]{:S(2)}) collective-permute-start(bf16[64,384]{1,0:T(8,128)(2,1)S(1)} %fusion.4), channel_id=1, source_target_pairs={{0,24},{8,16},{16,8},{24,0},{1,25},{9,17},{17,9},{25,1},{2,26},{10... | collective-permute-start | bytes 147464 | tf_op jit(solution)/shard_map/ppermute | solution.py:34
  68.9 1.4 %collective-permute-start.17 = (f32[64,384]{1,0:T(8,128)S(1)}, f32[64,384]{1,0:T(8,128)S(1)}, u32[]{:S(2)}, u32[]{:S(2)}) collective-permute-start(f32[64,384]{1,0:T(8,128)S(1)} %add_multiply_fusion.mine_ref), channel_id=1, source_target_pairs={{0,1},{1,0},{2,3},{3,2},{4,5},{5,4},{6,7},{7,6},{8,9},{9,8},{10,11... | collective-permute-start | bytes 294920 | tf_op jit(solution)/shard_map/ppermute | solution.py:34
  75.9 7.4 %collective-permute-start.18 = (bf16[2,32,1,8,128]{4,3,2,1,0:T(8,128)(2,1)S(1)}, bf16[2,32,1,8,128]{4,3,2,1,0:T(8,128)(2,1)S(1)}, u32[]{:S(2)}, u32[]{:S(2)}) collective-permute-start(bf16[2,32,1,8,128]{4,3,2,1,0:T(8,128)(2,1)S(1)} %get-tuple-element.31), channel_id=1, source_target_pairs={{0,8},{8,0},{16,24},{24,16},{1,9},{9,1},{17,25},{25,17},{2,10},{10... | collective-permute-start | bytes 393224 | tf_op jit(solution)/shard_map/ppermute | solution.py:34
  76.6 12.8 %collective-permute-start.19 = (bf16[2,32,1,8,128]{4,3,2,1,0:T(8,128)(2,1)S(1)}, bf16[2,32,1,8,128]{4,3,2,1,0:T(8,128)(2,1)S(1)}, u32[]{:S(2)}, u32[]{:S(2)}) collective-permute-start(bf16[2,32,1,8,128]{4,3,2,1,0:T(8,128)(2,1)S(1)} %get-tuple-element.32), channel_id=1, source_target_pairs={{0,16},{8,24},{16,0},{24,8},{1,17},{9,25},{17,1},{25,9},{2,18},{10... | collective-permute-start | bytes 393224 | tf_op jit(solution)/shard_map/ppermute | solution.py:34
  77.9 11.4 %collective-permute-start.20 = (bf16[2,32,1,8,128]{4,3,2,1,0:T(8,128)(2,1)S(1)}, bf16[2,32,1,8,128]{4,3,2,1,0:T(8,128)(2,1)S(1)}, u32[]{:S(2)}, u32[]{:S(2)}) collective-permute-start(bf16[2,32,1,8,128]{4,3,2,1,0:T(8,128)(2,1)S(1)} %get-tuple-element.33), channel_id=1, source_target_pairs={{0,24},{8,16},{16,8},{24,0},{1,25},{9,17},{17,9},{25,1},{2,26},{10... | collective-permute-start | bytes 393224 | tf_op jit(solution)/shard_map/ppermute | solution.py:34

commit v6 on v5

--- a/solution.py
+++ b/solution.py
@@ -11,6 +11,7 @@
 SECTIONS = 4
 CHUNKS = (1, 1)
 TALL = 32
+TERMS = 2
 
 diffuse_x = 0.35
 diffuse_side = 0.05
@@ -34,19 +35,20 @@
     return lax.ppermute(value, axis, [(i, i ^ step) for i in range(count)])
 
 
-def shift(value, axis, step):
+def swap_outer(value, axis):
     count = lax.axis_size(axis)
-    return lax.ppermute(value, axis, [(i, (i + step) % count) for i in range(count)])
-
-
-def pack_kernel(start, with_flow, flow_ref, field_ref, out, block, stage, sem):
+    return lax.ppermute(value, axis, [(i, (i + 2 * (i % 2) - 1) % count) for i in range(count)])
+
+
+def pack_kernel(start, with_flow, flow_ref, field_ref, *rest):
+    out, block, stage, sem = rest[-4:]
     step, rows, ny, nz = block.shape
     copy = pltpu.make_async_copy(field_ref.at[pl.ds(start, step)], block, sem)
     copy.start()
     if with_flow:
         per = step // (rows * ny)
         left = flow_ref[...].reshape(rows * ny, nz)
-        for p in range(3):
+        for p in range(TERMS):
             part = left.astype(bf16)
             left = left - part.astype(f32)
             at = p % per * rows * ny
@@ -58,13 +60,13 @@
             out[r * ny + y] = stage[r % 2, pl.ds(y, step, stride=ny), :].astype(bf16)
 
 
-def pack(flow, field, start, step, with_flow):
+def pack(flow, field, start, step, with_flow, before):
     _, rows, ny, nz = field.shape
-    extra = -(-3 // (step // (rows * ny))) if with_flow else 0
+    extra = -(-TERMS // (step // (rows * ny))) if with_flow else 0
     return pl.pallas_call(
         functools.partial(pack_kernel, start, with_flow),
         out_shape=jax.ShapeDtypeStruct((rows * ny + extra, step, nz), bf16),
-        in_specs=[vmem, hbm],
+        in_specs=[vmem, hbm] + [anywhere] * len(before),
         out_specs=vmem,
         scratch_shapes=[
             pltpu.VMEM((step, rows, ny, nz), bf16),
@@ -73,19 +75,20 @@
         ],
         compiler_params=pltpu.CompilerParams(vmem_limit_bytes=VMEM_LIMIT),
         name="pack",
-    )(flow, field)
+    )(flow, field, *before)
 
 
 def sections_kernel(groups, rows, ny, lead, where_ref, ring_ref, *rest):
     reach = SECTIONS
     total_rows = rows + 2 * reach
     me = where_ref[0]
+    low_core = where_ref[1] == 0
     if lead:
-        flow_ref, own_ref, lo_ref, hi_ref = rest[:4]
+        flow_ref, own_ref, inner_ref, outer_ref = rest[:4]
         outs = rest[4:4 + groups]
         plus, minus, flow_ext, done = rest[4 + groups:]
     else:
-        plus, minus, own_ref, lo_ref, hi_ref, _ = rest[:6]
+        plus, minus, own_ref, inner_ref, outer_ref, _ = rest[:6]
         outs = rest[6:6 + groups]
         done, = rest[6 + groups:]
     step, nz = own_ref.shape[1:]
@@ -96,26 +99,29 @@
 
         def flow_of(ref):
             flow = None
-            for p in (2, 1, 0):
+            for p in reversed(range(TERMS)):
                 at = p % per * rows * ny
                 part = ref[rows * ny + p // per, at:at + rows * ny].astype(f32)
                 flow = part if flow is None else flow + part
             return flow.reshape(rows, ny, nz)
 
-        flow_ext[0:reach] = flow_of(lo_ref)[rows - reach:]
+        inner, outer = flow_of(inner_ref), flow_of(outer_ref)
+        flow_ext[0:reach] = jnp.where(low_core, outer, inner)[rows - reach:]
         flow_ext[reach:reach + rows] = flow_ref[...]
-        flow_ext[reach + rows:] = flow_of(hi_ref)[:reach]
+        flow_ext[reach + rows:] = jnp.where(low_core, inner, outer)[:reach]
         for e in range(1, total_rows - 1):
             plus[e] = diffuse_x + sign * flow_ext[e + adj]
             minus[e] = diffuse_x - sign * flow_ext[e - adj]
     ring = ring_ref[...]
 
-    def entry(e, y):
+    def entry(e, y, at):
         if e < reach:
-            return lo_ref, (rows - reach + e) * ny + y
+            row = (rows - reach + e) * ny + y
+            return jnp.where(low_core, outer_ref[row, at, :], inner_ref[row, at, :])
         if e < reach + rows:
-            return own_ref, (e - reach) * ny + y
-        return hi_ref, (e - reach - rows) * ny + y
+            return own_ref[(e - reach) * ny + y, at, :]
+        row = (e - reach - rows) * ny + y
+        return jnp.where(low_core, inner_ref[row, at, :], outer_ref[row, at, :])
 
     tall = math.gcd(step, TALL)
 
@@ -123,7 +129,7 @@
         at = pl.ds(pl.multiple_of(block * tall, tall), tall)
 
         def load(e):
-            low = [ref[row, at, :] for ref, row in (entry(e, y) for y in range(ny))]
+            low = [entry(e, y, at) for y in range(ny)]
             return low, [part.astype(f32) for part in low]
 
         def advance(e, behind, here, ahead):
@@ -158,7 +164,7 @@
             outs[k][j * ny:(j + 1) * ny] = done[peer(me, k) * share + j]
 
 
-def sections(where, ring, coefs, own, lo, hi, groups, flow, before):
+def sections(where, ring, coefs, own, inner, outer, groups, flow, before):
     rows, ny, nz = flow.shape
     step = own.shape[1]
     share = rows // groups
@@ -180,7 +186,7 @@
         cost_estimate=pl.CostEstimate(
             flops=8 * SECTIONS * step * total * ny * nz, bytes_accessed=8 * step * rows * ny * nz, transcendentals=0),
         name="sections",
-    )(where, ring, *coefs, own, lo, hi, *before)
+    )(where, ring, *coefs, own, inner, outer, *before)
     return outs[:groups], outs[groups:]
 
 
@@ -407,11 +413,11 @@
     blocks = [[None] * chunks for _ in range(groups)]
     coefs = None
     for c in range(chunks):
-        own = pack(flow, field, sum(sizes[:c]), sizes[c], c == 0)
-        lo = shift(own, "slab", 1)
-        hi = shift(own, "slab", -1)
+        own = pack(flow, field, sum(sizes[:c]), sizes[c], c == 0, [inner] if c else [])
+        inner = swap(own, "slab", 1)
+        outer = swap_outer(own, "slab")
         before = [blocks[1][c - 1]] if c else []
-        parts, made = sections(where, ring, coefs, own, lo, hi, groups, flow, before)
+        parts, made = sections(where, ring, coefs, own, inner, outer, groups, flow, before)
         coefs = coefs or made
         blocks[0][c] = parts[0]
         for k in range(1, groups):

time: 91 us -> 88.4 us (0.971)
  starting transfers between devices: 30.9 us -> 27.8 us
    ppermute x17 -> x19, starting transfers between devices: 24.7 us -> 22.7 us  [swap(): return lax.ppermute(value, axis, [(i, i ^ step) for i in range(count)])]
    ppermute x4 -> x2, starting transfers between devices: 6.14 us -> 5.18 us  [swap_outer(): lax.ppermute(value, axis, [(i, (i + 2 * (i % 2) - 1) % count) for i in ra...]
    ppermute x17 -> x19, waiting for transfers between devices: 30.2 us -> 30.8 us  [swap(): return lax.ppermute(value, axis, [(i, i ^ step) for i in range(count)])]
    ppermute x4 -> x2, waiting for transfers between devices: 11.9 us -> 11.4 us  [swap_outer(): lax.ppermute(value, axis, [(i, (i + 2 * (i % 2) - 1) % count) for i in ra...]
  transfers between devices with their start and end apart: 21 -> 21, of which waited for: 16 -> 14; matrix products, arithmetic and copies ran while one was open for 0% -> 0% of each run, Pallas kernels for 7% -> 8%
where the time goes in v6:
time: 88.4 us; the launch traced here: 88.2 us
  waiting for transfers between devices  42.2 us (48%)
  starting transfers between devices  27.8 us (31%)
  Pallas kernels  15.2 us (17%)
  local copies, waits for them, and re-layouts  1.22 us (1%)
  other arithmetic  0.94 us (1%)
    ppermute x19, waiting for transfers between devices, swap(): return lax.ppermute(value, axis, [(i, i ^ step) for i in range(count)])  30.8 us
    ppermute x19, starting transfers between devices, swap(): return lax.ppermute(value, axis, [(i, i ^ step) for i in range(count)])  22.7 us
    ppermute x2, waiting for transfers between devices, swap_outer(): lax.ppermute(value, axis, [(i, (i + 2 * (i % 2) - 1) % count) for i in ra...  11.4 us
    pallas_call x2, Pallas kernels, sections(): pl.pallas_call(functools.partial(sections_kernel, groups, rows, ny, lead)...  6.64 us
    pallas_call x1, Pallas kernels, modes(): pl.pallas_call(functools.partial(modes_kernel, groups, chunks), out_shape...  5.65 us
    ppermute x2, starting transfers between devices, swap_outer(): lax.ppermute(value, axis, [(i, (i + 2 * (i % 2) - 1) % count) for i in ra...  5.18 us
  transfers between devices with their start and end apart: 21, of which 14 were waited for; matrix products, arithmetic and copies ran while one was open for 0% of the time, Pallas kernels for 8%

profile of v6, /device:TPU:0, one launch (start us, length us, event | category | flops | bytes accessed | tf_op | source)
XLA Modules:
  0.0 88.2 jit_solution(17910164441901691614)
XLA Ops:
  3.4 3.6 %collective-permute-start.1 = (bf16[33,64,128]{2,1,0:T(8,128)(2,1)S(1)}, bf16[33,64,128]{2,1,0:T(8,128)(2,1)S(1)}, u32[]{:S(2)}, u32[]{:S(2)}) collective-permute-start(bf16[33,64,128]{2,1,0:T(8,128)(2,1)S(1)} %pack.2.rest_1_), channel_id=1, source_target_pairs={{0,7},{1,2},{2,1},{3,4},{4,3},{5,6},{6,5},{7,0},{8,15},{9,10},{10,... | collective-permute-start | bytes 1622024 | tf_op jit(solution)/shard_map/ppermute | solution.py:40
  7.2 1.6 %collective-permute-start.3 = (bf16[32,64,128]{2,1,0:T(8,128)(2,1)S(1)}, bf16[32,64,128]{2,1,0:T(8,128)(2,1)S(1)}, u32[]{:S(2)}, u32[]{:S(2)}) collective-permute-start(bf16[32,64,128]{2,1,0:T(8,128)(2,1)S(1)} %pack.3.rest_2_), channel_id=1, source_target_pairs={{0,7},{1,2},{2,1},{3,4},{4,3},{5,6},{6,5},{7,0},{8,15},{9,10},{10,... | collective-permute-start | bytes 1572872 | tf_op jit(solution)/shard_map/ppermute | solution.py:40
  9.0 10.7 %collective-permute-done.1.rest_3_ = bf16[33,64,128]{2,1,0:T(8,128)(2,1)S(1)} collective-permute-done((bf16[33,64,128]{2,1,0:T(8,128)(2,1)S(1)}, bf16[33,64,128]{2,1,0:T(8,128)(2,1)S(1)}, u32[]{:S(2)}, u32[]{:S(2)}) %collective-permute-start.1) | collective-permute-done | bytes 540704 | tf_op jit(solution)/shard_map/ppermute | solution.py:40
  19.7 3.3 %sections.2 = (bf16[8,64,128]{2,1,0:T(8,128)(2,1)S(1)}, bf16[8,64,128]{2,1,0:T(8,128)(2,1)S(1)}, bf16[8,64,128]{2,1,0:T(8,128)(2,1)S(1)}, bf16[8,64,128]{2,1,0:T...) custom-call(s32[2]{0:T(128)S(1)} %pad_add_fusion.where_ref, ...), custom_call_target="tpu_custom_call" | custom-call | flops 25165824 | bytes 2097152 | tf_op jit(solution)/shard_map/sections/pallas_call | solution.py:179
  23.0 1.6 %collective-permute-start.4 = (bf16[8,64,128]{2,1,0:T(8,128)(2,1)S(1)}, bf16[8,64,128]{2,1,0:T(8,128)(2,1)S(1)}, u32[]{:S(2)}, u32[]{:S(2)}) collective-permute-start(bf16[8,64,128]{2,1,0:T(8,128)(2,1)S(1)} %get-tuple-element.21), channel_id=1, source_target_pairs={{0,8},{8,0},{16,24},{24,16},{1,9},{9,1},{17,25},{25,17},{2,10},{10... | collective-permute-start | bytes 393224 | tf_op jit(solution)/shard_map/ppermute | solution.py:35
  24.7 2.6 %collective-permute-start.6 = (bf16[8,64,128]{2,1,0:T(8,128)(2,1)S(1)}, bf16[8,64,128]{2,1,0:T(8,128)(2,1)S(1)}, u32[]{:S(2)}, u32[]{:S(2)}) collective-permute-start(bf16[8,64,128]{2,1,0:T(8,128)(2,1)S(1)} %get-tuple-element.24), channel_id=1, source_target_pairs={{0,16},{8,24},{16,0},{24,8},{1,17},{9,25},{17,1},{25,9},{2,18},{10... | collective-permute-start | bytes 393224 | tf_op jit(solution)/shard_map/ppermute | solution.py:35
  27.5 2.1 %collective-permute-done.4.rest_5_.rest_2_ = bf16[8,64,128]{2,1,0:T(8,128)(2,1)S(1)} collective-permute-done((bf16[8,64,128]{2,1,0:T(8,128)(2,1)S(1)}, bf16[8,64,128]{2,1,0:T(8,128)(2,1)S(1)}, u32[]{:S(2)}, u32[]{:S(2)}) %collective-permute-start.4) | collective-permute-done | bytes 131104 | tf_op jit(solution)/shard_map/ppermute | solution.py:35
  30.2 3.3 %sections.3 = (bf16[8,64,128]{2,1,0:T(8,128)(2,1)S(1)}, bf16[8,64,128]{2,1,0:T(8,128)(2,1)S(1)}, bf16[8,64,128]{2,1,0:T(8,128)(2,1)S(1)}, bf16[8,64,128]{2,1,0:T(8,128)(2,1)S(1)}) custom-call(s32[2]{0:T(128)S(1)} %pad_add_fusion.where_ref, bf16[128,128]{1,0:T(8,128)(2,1)S(1)} %add_convert_fusion.ring_ref, f32[12,8,128]{2,1,0:T(8,128)S(1)} %get-tuple-element.19.rest_0_, ...), custom_call_target="tpu_custom_call" | custom-call | flops 25165824 | bytes 2097152 | tf_op jit(solution)/shard_map/sections/pallas_call | solution.py:179
  33.5 2.0 %collective-permute-start.5 = (bf16[8,64,128]{2,1,0:T(8,128)(2,1)S(1)}, bf16[8,64,128]{2,1,0:T(8,128)(2,1)S(1)}, u32[]{:S(2)}, u32[]{:S(2)}) collective-permute-start(bf16[8,64,128]{2,1,0:T(8,128)(2,1)S(1)} %get-tuple-element.23), channel_id=1, source_target_pairs={{0,8},{8,0},{16,24},{24,16},{1,9},{9,1},{17,25},{25,17},{2,10},{10... | collective-permute-start | bytes 393224 | tf_op jit(solution)/shard_map/ppermute | solution.py:35
  35.5 2.6 %collective-permute-start.7 = (bf16[8,64,128]{2,1,0:T(8,128)(2,1)S(1)}, bf16[8,64,128]{2,1,0:T(8,128)(2,1)S(1)}, u32[]{:S(2)}, u32[]{:S(2)}) collective-permute-start(bf16[8,64,128]{2,1,0:T(8,128)(2,1)S(1)} %get-tuple-element.25), channel_id=1, source_target_pairs={{0,16},{8,24},{16,0},{24,8},{1,17},{9,25},{17,1},{25,9},{2,18},{10... | collective-permute-start | bytes 393224 | tf_op jit(solution)/shard_map/ppermute | solution.py:35
  38.1 3.7 %collective-permute-done.5.rest_3_ = bf16[8,64,128]{2,1,0:T(8,128)(2,1)S(1)} collective-permute-done((bf16[8,64,128]{2,1,0:T(8,128)(2,1)S(1)}, bf16[8,64,128]{2,1,0:T(8,128)(2,1)S(1)}, u32[]{:S(2)}, u32[]{:S(2)}) %collective-permute-start.5) | collective-permute-done | bytes 131104 | tf_op jit(solution)/shard_map/ppermute | solution.py:35
  41.8 6.6 %collective-permute-done.7.rest_5_ = bf16[8,64,128]{2,1,0:T(8,128)(2,1)S(1)} collective-permute-done((bf16[8,64,128]{2,1,0:T(8,128)(2,1)S(1)}, bf16[8,64,128]{2,1,0:T(8,128)(2,1)S(1)}, u32[]{:S(2)}, u32[]{:S(2)}) %collective-permute-start.7) | collective-permute-done | bytes 131104 | tf_op jit(solution)/shard_map/ppermute | solution.py:35
  50.8 1.8 %collective-permute-start.13 = (bf16[64,384]{1,0:T(8,128)(2,1)S(1)}, bf16[64,384]{1,0:T(8,128)(2,1)S(1)}, u32[]{:S(2)}, u32[]{:S(2)}) collective-permute-start(bf16[64,384]{1,0:T(8,128)(2,1)S(1)} %get-tuple-element.34), channel_id=1, source_target_pairs={{0,6},{1,7},{2,4},{3,5},{4,2},{5,3},{6,0},{7,1},{8,14},{9,15},{10,... | collective-permute-start | bytes 147464 | tf_op jit(solution)/shard_map/ppermute | solution.py:35
  52.6 1.7 %collective-permute-start.11 = (bf16[64,384]{1,0:T(8,128)(2,1)S(1)}, bf16[64,384]{1,0:T(8,128)(2,1)S(1)}, u32[]{:S(2)}, u32[]{:S(2)}) collective-permute-start(bf16[64,384]{1,0:T(8,128)(2,1)S(1)} %get-tuple-element.34), channel_id=1, source_target_pairs={{0,2},{1,3},{2,0},{3,1},{4,6},{5,7},{6,4},{7,5},{8,10},{9,11},{10,... | collective-permute-start | bytes 147464 | tf_op jit(solution)/shard_map/ppermute | solution.py:35
  54.3 1.6 %collective-permute-done.13 = bf16[64,384]{1,0:T(8,128)(2,1)S(1)} collective-permute-done((bf16[64,384]{1,0:T(8,128)(2,1)S(1)}, bf16[64,384]{1,0:T(8,128)(2,1)S(1)}, u32[]{:S(2)}, u32[]{:S(2)}) %collective-permute-start.13) | collective-permute-done | bytes 49184 | tf_op jit(solution)/shard_map/ppermute | solution.py:35
  56.7 2.5 %collective-permute-start.16 = (bf16[64,384]{1,0:T(8,128)(2,1)S(1)}, bf16[64,384]{1,0:T(8,128)(2,1)S(1)}, u32[]{:S(2)}, u32[]{:S(2)}) collective-permute-start(bf16[64,384]{1,0:T(8,128)(2,1)S(1)} %fusion.4), channel_id=1, source_target_pairs={{0,24},{8,16},{16,8},{24,0},{1,25},{9,17},{17,9},{25,1},{2,26},{10... | collective-permute-start | bytes 147464 | tf_op jit(solution)/shard_map/ppermute | solution.py:35
  59.2 2.4 %collective-permute-start.15 = (bf16[64,384]{1,0:T(8,128)(2,1)S(1)}, bf16[64,384]{1,0:T(8,128)(2,1)S(1)}, u32[]{:S(2)}, u32[]{:S(2)}) collective-permute-start(bf16[64,384]{1,0:T(8,128)(2,1)S(1)} %fusion.4), channel_id=1, source_target_pairs={{0,16},{8,24},{16,0},{24,8},{1,17},{9,25},{17,1},{25,9},{2,18},{10... | collective-permute-start | bytes 147464 | tf_op jit(solution)/shard_map/ppermute | solution.py:35
  62.8 1.9 %collective-permute-done.15 = bf16[64,384]{1,0:T(8,128)(2,1)S(1)} collective-permute-done((bf16[64,384]{1,0:T(8,128)(2,1)S(1)}, bf16[64,384]{1,0:T(8,128)(2,1)S(1)}, u32[]{:S(2)}, u32[]{:S(2)}) %collective-permute-start.15) | collective-permute-done | bytes 49184 | tf_op jit(solution)/shard_map/ppermute | solution.py:35
  67.1 5.7 %modes.1 = (bf16[2,32,1,8,128]{4,3,2,1,0:T(8,128)(2,1)S(1)}, bf16[2,32,1,8,128]{4,3,2,1,0:T(8,128)(2,1)S(1)}, bf16[2,32,1,8,128]{4,3,2,1,0:T(8,128)(2,1)S(1)}, bf16[2,32,1,8,128]{4,3,2,1,0:T(8,128)(2,1)S(1)}) custom-call(s32[2]{0:T(128)S(1)} %pad_add_fusion.where_ref, f32[64,384]{1,0:T(8,128)S(1)} %add_multiply_fusion.mine_ref, ...), custom_call_target="tpu_custom_call" | custom-call | tf_op jit(solution)/shard_map/modes/pallas_call | solution.py:362
  73.8 2.0 %collective-permute-start.19 = (bf16[2,32,1,8,128]{4,3,2,1,0:T(8,128)(2,1)S(1)}, bf16[2,32,1,8,128]{4,3,2,1,0:T(8,128)(2,1)S(1)}, u32[]{:S(2)}, u32[]{:S(2)}) collective-permute-start(bf16[2,32,1,8,128]{4,3,2,1,0:T(8,128)(2,1)S(1)} %get-tuple-element.32), channel_id=1, source_target_pairs={{0,16},{8,24},{16,0},{24,8},{1,17},{9,25},{17,1},{25,9},{2,18},{10... | collective-permute-start | bytes 393224 | tf_op jit(solution)/shard_map/ppermute | solution.py:35
  75.9 1.4 %collective-permute-start.20 = (bf16[2,32,1,8,128]{4,3,2,1,0:T(8,128)(2,1)S(1)}, bf16[2,32,1,8,128]{4,3,2,1,0:T(8,128)(2,1)S(1)}, u32[]{:S(2)}, u32[]{:S(2)}) collective-permute-start(bf16[2,32,1,8,128]{4,3,2,1,0:T(8,128)(2,1)S(1)} %get-tuple-element.33), channel_id=1, source_target_pairs={{0,24},{8,16},{16,8},{24,0},{1,25},{9,17},{17,9},{25,1},{2,26},{10... | collective-permute-start | bytes 393224 | tf_op jit(solution)/shard_map/ppermute | solution.py:35
  77.2 3.1 %collective-permute-done.18.rest_1_ = bf16[2,32,1,8,128]{4,3,2,1,0:T(8,128)(2,1)S(1)} collective-permute-done((bf16[2,32,1,8,128]{4,3,2,1,0:T(8,128)(2,1)S(1)}, bf16[2,32,1,8,128]{4,3,2,1,0:T(8,128)(2,1)S(1)}, u32[]{:S(2)}, u32[]{:S(2)}) %collective-permute-start.18) | collective-permute-done | bytes 131104 | tf_op jit(solution)/shard_map/ppermute | solution.py:35
  80.4 6.4 %collective-permute-done.19.rest_2_ = bf16[2,32,1,8,128]{4,3,2,1,0:T(8,128)(2,1)S(1)} collective-permute-done((bf16[2,32,1,8,128]{4,3,2,1,0:T(8,128)(2,1)S(1)}, bf16[2,32,1,8,128]{4,3,2,1,0:T(8,128)(2,1)S(1)}, u32[]{:S(2)}, u32[]{:S(2)}) %collective-permute-start.19) | collective-permute-done | bytes 131104 | tf_op jit(solution)/shard_map/ppermute | solution.py:35
  86.7 1.4 %place.1 = (bf16[32,4,8,128]{3,2,1,0:T(8,128)(2,1)}, bf16[32,4,8,128]{3,2,1,0:T(8,128)(2,1)}) custom-call(s32[2]{0:T(128)S(1)} %pad_add_fusion.where_ref, bf16[2,32,1,8,128]{4,3,2,1,0:T(8,128)(2,1)S(1)} %get-tuple-element.30.rest_0_, bf16[2,32,1,8,128]{4,3,2,1,0:T(8,128)(2,1)S(1)} %collective-permute-done.18.rest_1_, ...), custom_call_target="tpu_custom_call" | custom-call | tf_op jit(solution)/shard_map/place/pallas_call | solution.py:389
  (33 shorter events, 11.9 us)
Async XLA Ops:
  1.4 1.2 %copy-start = (bf16[1,128,4,8,128]{4,3,2,1,0:T(8,128)(2,1)S(1)}, bf16[1,128,4,8,128]{4,3,2,1,0:T(8,128)(2,1)}, u32[]{:S(2)}) copy-start(bf16[1,128,4,8,128]{4,3,2,1,0:T(8,128)(2,1)} %param.2) | copy-start | bytes 3145732
  2.9 4.1 %collective-permute-start = (bf16[33,64,128]{2,1,0:T(8,128)(2,1)S(1)}, bf16[33,64,128]{2,1,0:T(8,128)(2,1)S(1)}, u32[]{:S(2)}, u32[]{:S(2)}) collective-permute-start(bf16[33,64,128]{2,1,0:T(8,128)(2,1)S(1)} %pack.2.rest_1_), channel_id=1, source_target_pairs={{0,1},{1,0},{2,3},{3,2},{4,5},{5,4},{6,7},{7,6},{8,9},{9,8},{10,11... | collective-permute-start | bytes 1622024 | tf_op jit(solution)/shard_map/ppermute | solution.py:35
  3.4 16.3 %collective-permute-start.1 = (bf16[33,64,128]{2,1,0:T(8,128)(2,1)S(1)}, bf16[33,64,128]{2,1,0:T(8,128)(2,1)S(1)}, u32[]{:S(2)}, u32[]{:S(2)}) collective-permute-start(bf16[33,64,128]{2,1,0:T(8,128)(2,1)S(1)} %pack.2.rest_1_), channel_id=1, source_target_pairs={{0,7},{1,2},{2,1},{3,4},{4,3},{5,6},{6,5},{7,0},{8,15},{9,10},{10,... | collective-permute-start | bytes 1622024 | tf_op jit(solution)/shard_map/ppermute | solution.py:40
  7.2 23.0 %collective-permute-start.3 = (bf16[32,64,128]{2,1,0:T(8,128)(2,1)S(1)}, bf16[32,64,128]{2,1,0:T(8,128)(2,1)S(1)}, u32[]{:S(2)}, u32[]{:S(2)}) collective-permute-start(bf16[32,64,128]{2,1,0:T(8,128)(2,1)S(1)} %pack.3.rest_2_), channel_id=1, source_target_pairs={{0,7},{1,2},{2,1},{3,4},{4,3},{5,6},{6,5},{7,0},{8,15},{9,10},{10,... | collective-permute-start | bytes 1572872 | tf_op jit(solution)/shard_map/ppermute | solution.py:40
  8.9 21.4 %collective-permute-start.2 = (bf16[32,64,128]{2,1,0:T(8,128)(2,1)S(1)}, bf16[32,64,128]{2,1,0:T(8,128)(2,1)S(1)}, u32[]{:S(2)}, u32[]{:S(2)}) collective-permute-start(bf16[32,64,128]{2,1,0:T(8,128)(2,1)S(1)} %pack.3.rest_2_), channel_id=1, source_target_pairs={{0,1},{1,0},{2,3},{3,2},{4,5},{5,4},{6,7},{7,6},{8,9},{9,8},{10,11... | collective-permute-start | bytes 1572872 | tf_op jit(solution)/shard_map/ppermute | solution.py:35
  23.0 6.5 %collective-permute-start.4 = (bf16[8,64,128]{2,1,0:T(8,128)(2,1)S(1)}, bf16[8,64,128]{2,1,0:T(8,128)(2,1)S(1)}, u32[]{:S(2)}, u32[]{:S(2)}) collective-permute-start(bf16[8,64,128]{2,1,0:T(8,128)(2,1)S(1)} %get-tuple-element.21), channel_id=1, source_target_pairs={{0,8},{8,0},{16,24},{24,16},{1,9},{9,1},{17,25},{25,17},{2,10},{10... | collective-permute-start | bytes 393224 | tf_op jit(solution)/shard_map/ppermute | solution.py:35
  24.7 13.5 %collective-permute-start.6 = (bf16[8,64,128]{2,1,0:T(8,128)(2,1)S(1)}, bf16[8,64,128]{2,1,0:T(8,128)(2,1)S(1)}, u32[]{:S(2)}, u32[]{:S(2)}) collective-permute-start(bf16[8,64,128]{2,1,0:T(8,128)(2,1)S(1)} %get-tuple-element.24), channel_id=1, source_target_pairs={{0,16},{8,24},{16,0},{24,8},{1,17},{9,25},{17,1},{25,9},{2,18},{10... | collective-permute-start | bytes 393224 | tf_op jit(solution)/shard_map/ppermute | solution.py:35
  27.2 10.9 %collective-permute-start.8 = (bf16[8,64,128]{2,1,0:T(8,128)(2,1)S(1)}, bf16[8,64,128]{2,1,0:T(8,128)(2,1)S(1)}, u32[]{:S(2)}, u32[]{:S(2)}) collective-permute-start(bf16[8,64,128]{2,1,0:T(8,128)(2,1)S(1)} %get-tuple-element.26), channel_id=1, source_target_pairs={{0,24},{8,16},{16,8},{24,0},{1,25},{9,17},{17,9},{25,1},{2,26},{10... | collective-permute-start | bytes 393224 | tf_op jit(solution)/shard_map/ppermute | solution.py:35
  33.5 8.3 %collective-permute-start.5 = (bf16[8,64,128]{2,1,0:T(8,128)(2,1)S(1)}, bf16[8,64,128]{2,1,0:T(8,128)(2,1)S(1)}, u32[]{:S(2)}, u32[]{:S(2)}) collective-permute-start(bf16[8,64,128]{2,1,0:T(8,128)(2,1)S(1)} %get-tuple-element.23), channel_id=1, source_target_pairs={{0,8},{8,0},{16,24},{24,16},{1,9},{9,1},{17,25},{25,17},{2,10},{10... | collective-permute-start | bytes 393224 | tf_op jit(solution)/shard_map/ppermute | solution.py:35
  35.5 12.9 %collective-permute-start.7 = (bf16[8,64,128]{2,1,0:T(8,128)(2,1)S(1)}, bf16[8,64,128]{2,1,0:T(8,128)(2,1)S(1)}, u32[]{:S(2)}, u32[]{:S(2)}) collective-permute-start(bf16[8,64,128]{2,1,0:T(8,128)(2,1)S(1)} %get-tuple-element.25), channel_id=1, source_target_pairs={{0,16},{8,24},{16,0},{24,8},{1,17},{9,25},{17,1},{25,9},{2,18},{10... | collective-permute-start | bytes 393224 | tf_op jit(solution)/shard_map/ppermute | solution.py:35
  38.1 10.3 %collective-permute-start.9 = (bf16[8,64,128]{2,1,0:T(8,128)(2,1)S(1)}, bf16[8,64,128]{2,1,0:T(8,128)(2,1)S(1)}, u32[]{:S(2)}, u32[]{:S(2)}) collective-permute-start(bf16[8,64,128]{2,1,0:T(8,128)(2,1)S(1)} %get-tuple-element.27), channel_id=1, source_target_pairs={{0,24},{8,16},{16,8},{24,0},{1,25},{9,17},{17,9},{25,1},{2,26},{10... | collective-permute-start | bytes 393224 | tf_op jit(solution)/shard_map/ppermute | solution.py:35
  49.4 1.4 %collective-permute-start.10 = (f32[64,384]{1,0:T(8,128)S(1)}, f32[64,384]{1,0:T(8,128)S(1)}, u32[]{:S(2)}, u32[]{:S(2)}) collective-permute-start(f32[64,384]{1,0:T(8,128)S(1)} %get-tuple-element.29), channel_id=1, source_target_pairs={{0,1},{1,0},{2,3},{3,2},{4,5},{5,4},{6,7},{7,6},{8,9},{9,8},{10,11... | collective-permute-start | bytes 294920 | tf_op jit(solution)/shard_map/ppermute | solution.py:35
  50.8 5.2 %collective-permute-start.13 = (bf16[64,384]{1,0:T(8,128)(2,1)S(1)}, bf16[64,384]{1,0:T(8,128)(2,1)S(1)}, u32[]{:S(2)}, u32[]{:S(2)}) collective-permute-start(bf16[64,384]{1,0:T(8,128)(2,1)S(1)} %get-tuple-element.34), channel_id=1, source_target_pairs={{0,6},{1,7},{2,4},{3,5},{4,2},{5,3},{6,0},{7,1},{8,14},{9,15},{10,... | collective-permute-start | bytes 147464 | tf_op jit(solution)/shard_map/ppermute | solution.py:35
  52.6 4.1 %collective-permute-start.12 = (bf16[64,384]{1,0:T(8,128)(2,1)S(1)}, bf16[64,384]{1,0:T(8,128)(2,1)S(1)}, u32[]{:S(2)}, u32[]{:S(2)}) collective-permute-start(bf16[64,384]{1,0:T(8,128)(2,1)S(1)} %get-tuple-element.34), channel_id=1, source_target_pairs={{0,4},{1,5},{2,6},{3,7},{4,0},{5,1},{6,2},{7,3},{8,12},{9,13},{10,... | collective-permute-start | bytes 147464 | tf_op jit(solution)/shard_map/ppermute | solution.py:35
  52.6 4.1 %collective-permute-start.11 = (bf16[64,384]{1,0:T(8,128)(2,1)S(1)}, bf16[64,384]{1,0:T(8,128)(2,1)S(1)}, u32[]{:S(2)}, u32[]{:S(2)}) collective-permute-start(bf16[64,384]{1,0:T(8,128)(2,1)S(1)} %get-tuple-element.34), channel_id=1, source_target_pairs={{0,2},{1,3},{2,0},{3,1},{4,6},{5,7},{6,4},{7,5},{8,10},{9,11},{10,... | collective-permute-start | bytes 147464 | tf_op jit(solution)/shard_map/ppermute | solution.py:35
  56.7 6.1 %collective-permute-start.16 = (bf16[64,384]{1,0:T(8,128)(2,1)S(1)}, bf16[64,384]{1,0:T(8,128)(2,1)S(1)}, u32[]{:S(2)}, u32[]{:S(2)}) collective-permute-start(bf16[64,384]{1,0:T(8,128)(2,1)S(1)} %fusion.4), channel_id=1, source_target_pairs={{0,24},{8,16},{16,8},{24,0},{1,25},{9,17},{17,9},{25,1},{2,26},{10... | collective-permute-start | bytes 147464 | tf_op jit(solution)/shard_map/ppermute | solution.py:35
  59.2 5.4 %collective-permute-start.15 = (bf16[64,384]{1,0:T(8,128)(2,1)S(1)}, bf16[64,384]{1,0:T(8,128)(2,1)S(1)}, u32[]{:S(2)}, u32[]{:S(2)}) collective-permute-start(bf16[64,384]{1,0:T(8,128)(2,1)S(1)} %fusion.4), channel_id=1, source_target_pairs={{0,16},{8,24},{16,0},{24,8},{1,17},{9,25},{17,1},{25,9},{2,18},{10... | collective-permute-start | bytes 147464 | tf_op jit(solution)/shard_map/ppermute | solution.py:35
  61.6 4.1 %collective-permute-start.14 = (bf16[64,384]{1,0:T(8,128)(2,1)S(1)}, bf16[64,384]{1,0:T(8,128)(2,1)S(1)}, u32[]{:S(2)}, u32[]{:S(2)}) collective-permute-start(bf16[64,384]{1,0:T(8,128)(2,1)S(1)} %fusion.4), channel_id=1, source_target_pairs={{0,8},{8,0},{16,24},{24,16},{1,9},{9,1},{17,25},{25,17},{2,10},{10... | collective-permute-start | bytes 147464 | tf_op jit(solution)/shard_map/ppermute | solution.py:35
  65.8 1.4 %collective-permute-start.17 = (f32[64,384]{1,0:T(8,128)S(1)}, f32[64,384]{1,0:T(8,128)S(1)}, u32[]{:S(2)}, u32[]{:S(2)}) collective-permute-start(f32[64,384]{1,0:T(8,128)S(1)} %add_multiply_fusion.mine_ref), channel_id=1, source_target_pairs={{0,1},{1,0},{2,3},{3,2},{4,5},{5,4},{6,7},{7,6},{8,9},{9,8},{10,11... | collective-permute-start | bytes 294920 | tf_op jit(solution)/shard_map/ppermute | solution.py:35
  72.8 7.6 %collective-permute-start.18 = (bf16[2,32,1,8,128]{4,3,2,1,0:T(8,128)(2,1)S(1)}, bf16[2,32,1,8,128]{4,3,2,1,0:T(8,128)(2,1)S(1)}, u32[]{:S(2)}, u32[]{:S(2)}) collective-permute-start(bf16[2,32,1,8,128]{4,3,2,1,0:T(8,128)(2,1)S(1)} %get-tuple-element.31), channel_id=1, source_target_pairs={{0,8},{8,0},{16,24},{24,16},{1,9},{9,1},{17,25},{25,17},{2,10},{10... | collective-permute-start | bytes 393224 | tf_op jit(solution)/shard_map/ppermute | solution.py:35
  73.8 12.9 %collective-permute-start.19 = (bf16[2,32,1,8,128]{4,3,2,1,0:T(8,128)(2,1)S(1)}, bf16[2,32,1,8,128]{4,3,2,1,0:T(8,128)(2,1)S(1)}, u32[]{:S(2)}, u32[]{:S(2)}) collective-permute-start(bf16[2,32,1,8,128]{4,3,2,1,0:T(8,128)(2,1)S(1)} %get-tuple-element.32), channel_id=1, source_target_pairs={{0,16},{8,24},{16,0},{24,8},{1,17},{9,25},{17,1},{25,9},{2,18},{10... | collective-permute-start | bytes 393224 | tf_op jit(solution)/shard_map/ppermute | solution.py:35
  75.9 10.9 %collective-permute-start.20 = (bf16[2,32,1,8,128]{4,3,2,1,0:T(8,128)(2,1)S(1)}, bf16[2,32,1,8,128]{4,3,2,1,0:T(8,128)(2,1)S(1)}, u32[]{:S(2)}, u32[]{:S(2)}) collective-permute-start(bf16[2,32,1,8,128]{4,3,2,1,0:T(8,128)(2,1)S(1)} %get-tuple-element.33), channel_id=1, source_target_pairs={{0,24},{8,16},{16,8},{24,0},{1,25},{9,17},{17,9},{25,1},{2,26},{10... | collective-permute-start | bytes 393224 | tf_op jit(solution)/shard_map/ppermute | solution.py:35

commit v7 on v6

--- a/solution.py
+++ b/solution.py
@@ -10,7 +10,7 @@
 
 SECTIONS = 4
 CHUNKS = (1, 1)
-TALL = 32
+TALL = 64
 TERMS = 2
 
 diffuse_x = 0.35
@@ -41,23 +41,27 @@
 
 
 def pack_kernel(start, with_flow, flow_ref, field_ref, *rest):
-    out, block, stage, sem = rest[-4:]
+    out, block, stage, flow, sem, flow_sem = rest[-6:]
     step, rows, ny, nz = block.shape
     copy = pltpu.make_async_copy(field_ref.at[pl.ds(start, step)], block, sem)
     copy.start()
     if with_flow:
+        flow_copy = pltpu.make_async_copy(flow_ref, flow, flow_sem)
+        flow_copy.start()
+    copy.wait()
+    for r in range(rows):
+        stage[r % 2] = block[:, r].astype(f32).reshape(step * ny, nz)
+        for y in range(ny):
+            out[r * ny + y] = stage[r % 2, pl.ds(y, step, stride=ny), :].astype(bf16)
+    if with_flow:
+        flow_copy.wait()
         per = step // (rows * ny)
-        left = flow_ref[...].reshape(rows * ny, nz)
+        left = 0.5 * flow[...].reshape(rows * ny, nz)
         for p in range(TERMS):
             part = left.astype(bf16)
             left = left - part.astype(f32)
             at = p % per * rows * ny
             out[rows * ny + p // per, at:at + rows * ny] = part
-    copy.wait()
-    for r in range(rows):
-        stage[r % 2] = block[:, r].astype(f32).reshape(step * ny, nz)
-        for y in range(ny):
-            out[r * ny + y] = stage[r % 2, pl.ds(y, step, stride=ny), :].astype(bf16)
 
 
 def pack(flow, field, start, step, with_flow, before):
@@ -66,11 +70,13 @@
     return pl.pallas_call(
         functools.partial(pack_kernel, start, with_flow),
         out_shape=jax.ShapeDtypeStruct((rows * ny + extra, step, nz), bf16),
-        in_specs=[vmem, hbm] + [anywhere] * len(before),
+        in_specs=[hbm, hbm] + [anywhere] * len(before),
         out_specs=vmem,
         scratch_shapes=[
             pltpu.VMEM((step, rows, ny, nz), bf16),
             pltpu.VMEM((2, step * ny, nz), f32),
+            pltpu.VMEM((rows, ny, nz), f32),
+            pltpu.SemaphoreType.DMA(()),
             pltpu.SemaphoreType.DMA(()),
         ],
         compiler_params=pltpu.CompilerParams(vmem_limit_bytes=VMEM_LIMIT),
@@ -413,7 +419,7 @@
     blocks = [[None] * chunks for _ in range(groups)]
     coefs = None
     for c in range(chunks):
-        own = pack(flow, field, sum(sizes[:c]), sizes[c], c == 0, [inner] if c else [])
+        own = pack(base_flow, field, sum(sizes[:c]), sizes[c], c == 0, [inner] if c else [])
         inner = swap(own, "slab", 1)
         outer = swap_outer(own, "slab")
         before = [blocks[1][c - 1]] if c else []
@@ -424,7 +430,7 @@
             blocks[k][c] = swap(parts[k], "grp", k)
     flat = [blocks[k][c] for k in range(groups) for c in range(chunks)]
     keep, send = coupling(where, flat, groups, chunks)
-    total = keep + swap(send, "slab", 1)
+    total = keep + swap(send.astype(bf16), "slab", 1).astype(f32)
     bit = 2
     while bit < slabs:
         steps = [bit]

time: 88.4 us -> 88.5 us (level)
    unnamed x2 -> x8, local copies, waits for them, and re-layouts: 1.22 us -> 1.94 us
where the time goes in v7:
time: 88.5 us; the launch traced here: 88.2 us
  waiting for transfers between devices  42.2 us (48%)
  starting transfers between devices  27.7 us (31%)
  Pallas kernels  15.3 us (17%)
  local copies, waits for them, and re-layouts  1.94 us (2%)
    ppermute x19, waiting for transfers between devices, swap(): return lax.ppermute(value, axis, [(i, i ^ step) for i in range(count)])  30.8 us
    ppermute x19, starting transfers between devices, swap(): return lax.ppermute(value, axis, [(i, i ^ step) for i in range(count)])  22.6 us
    ppermute x2, waiting for transfers between devices, swap_outer(): lax.ppermute(value, axis, [(i, (i + 2 * (i % 2) - 1) % count) for i in ra...  11.4 us
    pallas_call x2, Pallas kernels, sections(): pl.pallas_call(functools.partial(sections_kernel, groups, rows, ny, lead)...  6.51 us
    pallas_call x1, Pallas kernels, modes(): pl.pallas_call(functools.partial(modes_kernel, groups, chunks), out_shape...  5.65 us
    ppermute x2, starting transfers between devices, swap_outer(): lax.ppermute(value, axis, [(i, (i + 2 * (i % 2) - 1) % count) for i in ra...  5.18 us
    unnamed x8, local copies, waits for them, and re-layouts  1.94 us
  transfers between devices with their start and end apart: 21, of which 14 were waited for; matrix products, arithmetic and copies ran while one was open for 0% of the time, Pallas kernels for 8%

profile of v7, /device:TPU:0, one launch (start us, length us, event | category | flops | bytes accessed | tf_op | source)
XLA Modules:
  0.0 88.2 jit_solution(2398187019804214424)
XLA Ops:
  3.4 3.6 %collective-permute-start.1 = (bf16[33,64,128]{2,1,0:T(8,128)(2,1)S(1)}, bf16[33,64,128]{2,1,0:T(8,128)(2,1)S(1)}, u32[]{:S(2)}, u32[]{:S(2)}) collective-permute-start(bf16[33,64,128]{2,1,0:T(8,128)(2,1)S(1)} %pack.2.rest_1_), channel_id=1, source_target_pairs={{0,7},{1,2},{2,1},{3,4},{4,3},{5,6},{6,5},{7,0},{8,15},{9,10},{10,... | collective-permute-start | bytes 1622024 | tf_op jit(solution)/shard_map/ppermute | solution.py:40
  7.3 1.6 %collective-permute-start.3 = (bf16[32,64,128]{2,1,0:T(8,128)(2,1)S(1)}, bf16[32,64,128]{2,1,0:T(8,128)(2,1)S(1)}, u32[]{:S(2)}, u32[]{:S(2)}) collective-permute-start(bf16[32,64,128]{2,1,0:T(8,128)(2,1)S(1)} %pack.3.rest_2_), channel_id=1, source_target_pairs={{0,7},{1,2},{2,1},{3,4},{4,3},{5,6},{6,5},{7,0},{8,15},{9,10},{10,... | collective-permute-start | bytes 1572872 | tf_op jit(solution)/shard_map/ppermute | solution.py:40
  9.1 10.6 %collective-permute-done.1.rest_3_ = bf16[33,64,128]{2,1,0:T(8,128)(2,1)S(1)} collective-permute-done((bf16[33,64,128]{2,1,0:T(8,128)(2,1)S(1)}, bf16[33,64,128]{2,1,0:T(8,128)(2,1)S(1)}, u32[]{:S(2)}, u32[]{:S(2)}) %collective-permute-start.1) | collective-permute-done | bytes 540704 | tf_op jit(solution)/shard_map/ppermute | solution.py:40
  19.7 3.2 %sections.2 = (bf16[8,64,128]{2,1,0:T(8,128)(2,1)S(1)}, bf16[8,64,128]{2,1,0:T(8,128)(2,1)S(1)}, bf16[8,64,128]{2,1,0:T(8,128)(2,1)S(1)}, bf16[8,64,128]{2,1,0:T...) custom-call(s32[2]{0:T(128)S(1)} %pad_add_fusion.where_ref, ...), custom_call_target="tpu_custom_call" | custom-call | flops 25165824 | bytes 2097152 | tf_op jit(solution)/shard_map/sections/pallas_call | solution.py:185
  22.9 1.6 %collective-permute-start.4 = (bf16[8,64,128]{2,1,0:T(8,128)(2,1)S(1)}, bf16[8,64,128]{2,1,0:T(8,128)(2,1)S(1)}, u32[]{:S(2)}, u32[]{:S(2)}) collective-permute-start(bf16[8,64,128]{2,1,0:T(8,128)(2,1)S(1)} %get-tuple-element.21), channel_id=1, source_target_pairs={{0,8},{8,0},{16,24},{24,16},{1,9},{9,1},{17,25},{25,17},{2,10},{10... | collective-permute-start | bytes 393224 | tf_op jit(solution)/shard_map/ppermute | solution.py:35
  24.6 2.6 %collective-permute-start.6 = (bf16[8,64,128]{2,1,0:T(8,128)(2,1)S(1)}, bf16[8,64,128]{2,1,0:T(8,128)(2,1)S(1)}, u32[]{:S(2)}, u32[]{:S(2)}) collective-permute-start(bf16[8,64,128]{2,1,0:T(8,128)(2,1)S(1)} %get-tuple-element.24), channel_id=1, source_target_pairs={{0,16},{8,24},{16,0},{24,8},{1,17},{9,25},{17,1},{25,9},{2,18},{10... | collective-permute-start | bytes 393224 | tf_op jit(solution)/shard_map/ppermute | solution.py:35
  27.4 2.1 %collective-permute-done.4.rest_5_.rest_2_ = bf16[8,64,128]{2,1,0:T(8,128)(2,1)S(1)} collective-permute-done((bf16[8,64,128]{2,1,0:T(8,128)(2,1)S(1)}, bf16[8,64,128]{2,1,0:T(8,128)(2,1)S(1)}, u32[]{:S(2)}, u32[]{:S(2)}) %collective-permute-start.4) | collective-permute-done | bytes 131104 | tf_op jit(solution)/shard_map/ppermute | solution.py:35
  30.3 3.3 %sections.3 = (bf16[8,64,128]{2,1,0:T(8,128)(2,1)S(1)}, bf16[8,64,128]{2,1,0:T(8,128)(2,1)S(1)}, bf16[8,64,128]{2,1,0:T(8,128)(2,1)S(1)}, bf16[8,64,128]{2,1,0:T(8,128)(2,1)S(1)}) custom-call(s32[2]{0:T(128)S(1)} %pad_add_fusion.where_ref, bf16[128,128]{1,0:T(8,128)(2,1)S(1)} %add_convert_fusion.ring_ref, f32[12,8,128]{2,1,0:T(8,128)S(1)} %get-tuple-element.19.rest_0_, ...), custom_call_target="tpu_custom_call" | custom-call | flops 25165824 | bytes 2097152 | tf_op jit(solution)/shard_map/sections/pallas_call | solution.py:185
  33.6 2.0 %collective-permute-start.5 = (bf16[8,64,128]{2,1,0:T(8,128)(2,1)S(1)}, bf16[8,64,128]{2,1,0:T(8,128)(2,1)S(1)}, u32[]{:S(2)}, u32[]{:S(2)}) collective-permute-start(bf16[8,64,128]{2,1,0:T(8,128)(2,1)S(1)} %get-tuple-element.23), channel_id=1, source_target_pairs={{0,8},{8,0},{16,24},{24,16},{1,9},{9,1},{17,25},{25,17},{2,10},{10... | collective-permute-start | bytes 393224 | tf_op jit(solution)/shard_map/ppermute | solution.py:35
  35.5 2.6 %collective-permute-start.7 = (bf16[8,64,128]{2,1,0:T(8,128)(2,1)S(1)}, bf16[8,64,128]{2,1,0:T(8,128)(2,1)S(1)}, u32[]{:S(2)}, u32[]{:S(2)}) collective-permute-start(bf16[8,64,128]{2,1,0:T(8,128)(2,1)S(1)} %get-tuple-element.25), channel_id=1, source_target_pairs={{0,16},{8,24},{16,0},{24,8},{1,17},{9,25},{17,1},{25,9},{2,18},{10... | collective-permute-start | bytes 393224 | tf_op jit(solution)/shard_map/ppermute | solution.py:35
  38.1 3.7 %collective-permute-done.5.rest_3_ = bf16[8,64,128]{2,1,0:T(8,128)(2,1)S(1)} collective-permute-done((bf16[8,64,128]{2,1,0:T(8,128)(2,1)S(1)}, bf16[8,64,128]{2,1,0:T(8,128)(2,1)S(1)}, u32[]{:S(2)}, u32[]{:S(2)}) %collective-permute-start.5) | collective-permute-done | bytes 131104 | tf_op jit(solution)/shard_map/ppermute | solution.py:35
  41.8 6.7 %collective-permute-done.7.rest_5_ = bf16[8,64,128]{2,1,0:T(8,128)(2,1)S(1)} collective-permute-done((bf16[8,64,128]{2,1,0:T(8,128)(2,1)S(1)}, bf16[8,64,128]{2,1,0:T(8,128)(2,1)S(1)}, u32[]{:S(2)}, u32[]{:S(2)}) %collective-permute-start.7) | collective-permute-done | bytes 131104 | tf_op jit(solution)/shard_map/ppermute | solution.py:35
  50.9 1.8 %collective-permute-start.13 = (bf16[64,384]{1,0:T(8,128)(2,1)S(1)}, bf16[64,384]{1,0:T(8,128)(2,1)S(1)}, u32[]{:S(2)}, u32[]{:S(2)}) collective-permute-start(bf16[64,384]{1,0:T(8,128)(2,1)S(1)} %fusion), channel_id=1, source_target_pairs={{0,6},{1,7},{2,4},{3,5},{4,2},{5,3},{6,0},{7,1},{8,14},{9,15},{10,... | collective-permute-start | bytes 147464 | tf_op jit(solution)/shard_map/ppermute | solution.py:35
  52.7 1.7 %collective-permute-start.11 = (bf16[64,384]{1,0:T(8,128)(2,1)S(1)}, bf16[64,384]{1,0:T(8,128)(2,1)S(1)}, u32[]{:S(2)}, u32[]{:S(2)}) collective-permute-start(bf16[64,384]{1,0:T(8,128)(2,1)S(1)} %fusion), channel_id=1, source_target_pairs={{0,2},{1,3},{2,0},{3,1},{4,6},{5,7},{6,4},{7,5},{8,10},{9,11},{10,... | collective-permute-start | bytes 147464 | tf_op jit(solution)/shard_map/ppermute | solution.py:35
  54.5 1.6 %collective-permute-done.13 = bf16[64,384]{1,0:T(8,128)(2,1)S(1)} collective-permute-done((bf16[64,384]{1,0:T(8,128)(2,1)S(1)}, bf16[64,384]{1,0:T(8,128)(2,1)S(1)}, u32[]{:S(2)}, u32[]{:S(2)}) %collective-permute-start.13) | collective-permute-done | bytes 49184 | tf_op jit(solution)/shard_map/ppermute | solution.py:35
  56.9 2.5 %collective-permute-start.16 = (bf16[64,384]{1,0:T(8,128)(2,1)S(1)}, bf16[64,384]{1,0:T(8,128)(2,1)S(1)}, u32[]{:S(2)}, u32[]{:S(2)}) collective-permute-start(bf16[64,384]{1,0:T(8,128)(2,1)S(1)} %fusion.5), channel_id=1, source_target_pairs={{0,24},{8,16},{16,8},{24,0},{1,25},{9,17},{17,9},{25,1},{2,26},{10... | collective-permute-start | bytes 147464 | tf_op jit(solution)/shard_map/ppermute | solution.py:35
  59.4 2.3 %collective-permute-start.15 = (bf16[64,384]{1,0:T(8,128)(2,1)S(1)}, bf16[64,384]{1,0:T(8,128)(2,1)S(1)}, u32[]{:S(2)}, u32[]{:S(2)}) collective-permute-start(bf16[64,384]{1,0:T(8,128)(2,1)S(1)} %fusion.5), channel_id=1, source_target_pairs={{0,16},{8,24},{16,0},{24,8},{1,17},{9,25},{17,1},{25,9},{2,18},{10... | collective-permute-start | bytes 147464 | tf_op jit(solution)/shard_map/ppermute | solution.py:35
  62.9 1.8 %collective-permute-done.15 = bf16[64,384]{1,0:T(8,128)(2,1)S(1)} collective-permute-done((bf16[64,384]{1,0:T(8,128)(2,1)S(1)}, bf16[64,384]{1,0:T(8,128)(2,1)S(1)}, u32[]{:S(2)}, u32[]{:S(2)}) %collective-permute-start.15) | collective-permute-done | bytes 49184 | tf_op jit(solution)/shard_map/ppermute | solution.py:35
  67.2 5.6 %modes.1 = (bf16[2,32,1,8,128]{4,3,2,1,0:T(8,128)(2,1)S(1)}, bf16[2,32,1,8,128]{4,3,2,1,0:T(8,128)(2,1)S(1)}, bf16[2,32,1,8,128]{4,3,2,1,0:T(8,128)(2,1)S(1)}, bf16[2,32,1,8,128]{4,3,2,1,0:T(8,128)(2,1)S(1)}) custom-call(s32[2]{0:T(128)S(1)} %pad_add_fusion.where_ref, f32[64,384]{1,0:T(8,128)S(1)} %add_multiply_fusion.mine_ref, ...), custom_call_target="tpu_custom_call" | custom-call | tf_op jit(solution)/shard_map/modes/pallas_call | solution.py:368
  73.9 2.0 %collective-permute-start.19 = (bf16[2,32,1,8,128]{4,3,2,1,0:T(8,128)(2,1)S(1)}, bf16[2,32,1,8,128]{4,3,2,1,0:T(8,128)(2,1)S(1)}, u32[]{:S(2)}, u32[]{:S(2)}) collective-permute-start(bf16[2,32,1,8,128]{4,3,2,1,0:T(8,128)(2,1)S(1)} %get-tuple-element.32), channel_id=1, source_target_pairs={{0,16},{8,24},{16,0},{24,8},{1,17},{9,25},{17,1},{25,9},{2,18},{10... | collective-permute-start | bytes 393224 | tf_op jit(solution)/shard_map/ppermute | solution.py:35
  75.9 1.4 %collective-permute-start.20 = (bf16[2,32,1,8,128]{4,3,2,1,0:T(8,128)(2,1)S(1)}, bf16[2,32,1,8,128]{4,3,2,1,0:T(8,128)(2,1)S(1)}, u32[]{:S(2)}, u32[]{:S(2)}) collective-permute-start(bf16[2,32,1,8,128]{4,3,2,1,0:T(8,128)(2,1)S(1)} %get-tuple-element.33), channel_id=1, source_target_pairs={{0,24},{8,16},{16,8},{24,0},{1,25},{9,17},{17,9},{25,1},{2,26},{10... | collective-permute-start | bytes 393224 | tf_op jit(solution)/shard_map/ppermute | solution.py:35
  77.3 3.2 %collective-permute-done.18.rest_1_ = bf16[2,32,1,8,128]{4,3,2,1,0:T(8,128)(2,1)S(1)} collective-permute-done((bf16[2,32,1,8,128]{4,3,2,1,0:T(8,128)(2,1)S(1)}, bf16[2,32,1,8,128]{4,3,2,1,0:T(8,128)(2,1)S(1)}, u32[]{:S(2)}, u32[]{:S(2)}) %collective-permute-start.18) | collective-permute-done | bytes 131104 | tf_op jit(solution)/shard_map/ppermute | solution.py:35
  80.4 6.3 %collective-permute-done.19.rest_2_ = bf16[2,32,1,8,128]{4,3,2,1,0:T(8,128)(2,1)S(1)} collective-permute-done((bf16[2,32,1,8,128]{4,3,2,1,0:T(8,128)(2,1)S(1)}, bf16[2,32,1,8,128]{4,3,2,1,0:T(8,128)(2,1)S(1)}, u32[]{:S(2)}, u32[]{:S(2)}) %collective-permute-start.19) | collective-permute-done | bytes 131104 | tf_op jit(solution)/shard_map/ppermute | solution.py:35
  86.8 1.4 %place.1 = (bf16[32,4,8,128]{3,2,1,0:T(8,128)(2,1)}, bf16[32,4,8,128]{3,2,1,0:T(8,128)(2,1)}) custom-call(s32[2]{0:T(128)S(1)} %pad_add_fusion.where_ref, bf16[2,32,1,8,128]{4,3,2,1,0:T(8,128)(2,1)S(1)} %get-tuple-element.30.rest_0_, bf16[2,32,1,8,128]{4,3,2,1,0:T(8,128)(2,1)S(1)} %collective-permute-done.18.rest_1_, ...), custom_call_target="tpu_custom_call" | custom-call | tf_op jit(solution)/shard_map/place/pallas_call | solution.py:395
  (40 shorter events, 12.2 us)
Async XLA Ops:
  0.6 1.2 %copy-start = (bf16[1,128,4,8,128]{4,3,2,1,0:T(8,128)(2,1)S(1)}, bf16[1,128,4,8,128]{4,3,2,1,0:T(8,128)(2,1)}, u32[]{:S(2)}) copy-start(bf16[1,128,4,8,128]{4,3,2,1,0:T(8,128)(2,1)} %param.2) | copy-start | bytes 3145732
  2.6 4.4 %copy-start.1 = (bf16[1,128,4,8,128]{4,3,2,1,0:T(8,128)(2,1)S(1)}, bf16[1,128,4,8,128]{4,3,2,1,0:T(8,128)(2,1)}, u32[]{:S(2)}) copy-start(bf16[1,128,4,8,128]{4,3,2,1,0:T(8,128)(2,1)} %param.2) | copy-start | bytes 3145732
  2.9 4.1 %copy-start.3 = (f32[4,8,128]{2,1,0:T(8,128)S(1)}, f32[4,8,128]{2,1,0:T(8,128)}, u32[]{:S(2)}) copy-start(f32[4,8,128]{2,1,0:T(8,128)} %flow_ref.3) | copy-start | bytes 49156
  2.9 4.1 %collective-permute-start = (bf16[33,64,128]{2,1,0:T(8,128)(2,1)S(1)}, bf16[33,64,128]{2,1,0:T(8,128)(2,1)S(1)}, u32[]{:S(2)}, u32[]{:S(2)}) collective-permute-start(bf16[33,64,128]{2,1,0:T(8,128)(2,1)S(1)} %pack.2.rest_1_), channel_id=1, source_target_pairs={{0,1},{1,0},{2,3},{3,2},{4,5},{5,4},{6,7},{7,6},{8,9},{9,8},{10,11... | collective-permute-start | bytes 1622024 | tf_op jit(solution)/shard_map/ppermute | solution.py:35
  3.4 16.3 %collective-permute-start.1 = (bf16[33,64,128]{2,1,0:T(8,128)(2,1)S(1)}, bf16[33,64,128]{2,1,0:T(8,128)(2,1)S(1)}, u32[]{:S(2)}, u32[]{:S(2)}) collective-permute-start(bf16[33,64,128]{2,1,0:T(8,128)(2,1)S(1)} %pack.2.rest_1_), channel_id=1, source_target_pairs={{0,7},{1,2},{2,1},{3,4},{4,3},{5,6},{6,5},{7,0},{8,15},{9,10},{10,... | collective-permute-start | bytes 1622024 | tf_op jit(solution)/shard_map/ppermute | solution.py:40
  7.3 23.0 %collective-permute-start.3 = (bf16[32,64,128]{2,1,0:T(8,128)(2,1)S(1)}, bf16[32,64,128]{2,1,0:T(8,128)(2,1)S(1)}, u32[]{:S(2)}, u32[]{:S(2)}) collective-permute-start(bf16[32,64,128]{2,1,0:T(8,128)(2,1)S(1)} %pack.3.rest_2_), channel_id=1, source_target_pairs={{0,7},{1,2},{2,1},{3,4},{4,3},{5,6},{6,5},{7,0},{8,15},{9,10},{10,... | collective-permute-start | bytes 1572872 | tf_op jit(solution)/shard_map/ppermute | solution.py:40
  8.9 21.3 %collective-permute-start.2 = (bf16[32,64,128]{2,1,0:T(8,128)(2,1)S(1)}, bf16[32,64,128]{2,1,0:T(8,128)(2,1)S(1)}, u32[]{:S(2)}, u32[]{:S(2)}) collective-permute-start(bf16[32,64,128]{2,1,0:T(8,128)(2,1)S(1)} %pack.3.rest_2_), channel_id=1, source_target_pairs={{0,1},{1,0},{2,3},{3,2},{4,5},{5,4},{6,7},{7,6},{8,9},{9,8},{10,11... | collective-permute-start | bytes 1572872 | tf_op jit(solution)/shard_map/ppermute | solution.py:35
  22.9 6.5 %collective-permute-start.4 = (bf16[8,64,128]{2,1,0:T(8,128)(2,1)S(1)}, bf16[8,64,128]{2,1,0:T(8,128)(2,1)S(1)}, u32[]{:S(2)}, u32[]{:S(2)}) collective-permute-start(bf16[8,64,128]{2,1,0:T(8,128)(2,1)S(1)} %get-tuple-element.21), channel_id=1, source_target_pairs={{0,8},{8,0},{16,24},{24,16},{1,9},{9,1},{17,25},{25,17},{2,10},{10... | collective-permute-start | bytes 393224 | tf_op jit(solution)/shard_map/ppermute | solution.py:35
  24.6 13.6 %collective-permute-start.6 = (bf16[8,64,128]{2,1,0:T(8,128)(2,1)S(1)}, bf16[8,64,128]{2,1,0:T(8,128)(2,1)S(1)}, u32[]{:S(2)}, u32[]{:S(2)}) collective-permute-start(bf16[8,64,128]{2,1,0:T(8,128)(2,1)S(1)} %get-tuple-element.24), channel_id=1, source_target_pairs={{0,16},{8,24},{16,0},{24,8},{1,17},{9,25},{17,1},{25,9},{2,18},{10... | collective-permute-start | bytes 393224 | tf_op jit(solution)/shard_map/ppermute | solution.py:35
  27.2 11.0 %collective-permute-start.8 = (bf16[8,64,128]{2,1,0:T(8,128)(2,1)S(1)}, bf16[8,64,128]{2,1,0:T(8,128)(2,1)S(1)}, u32[]{:S(2)}, u32[]{:S(2)}) collective-permute-start(bf16[8,64,128]{2,1,0:T(8,128)(2,1)S(1)} %get-tuple-element.26), channel_id=1, source_target_pairs={{0,24},{8,16},{16,8},{24,0},{1,25},{9,17},{17,9},{25,1},{2,26},{10... | collective-permute-start | bytes 393224 | tf_op jit(solution)/shard_map/ppermute | solution.py:35
  33.6 8.2 %collective-permute-start.5 = (bf16[8,64,128]{2,1,0:T(8,128)(2,1)S(1)}, bf16[8,64,128]{2,1,0:T(8,128)(2,1)S(1)}, u32[]{:S(2)}, u32[]{:S(2)}) collective-permute-start(bf16[8,64,128]{2,1,0:T(8,128)(2,1)S(1)} %get-tuple-element.23), channel_id=1, source_target_pairs={{0,8},{8,0},{16,24},{24,16},{1,9},{9,1},{17,25},{25,17},{2,10},{10... | collective-permute-start | bytes 393224 | tf_op jit(solution)/shard_map/ppermute | solution.py:35
  35.5 12.9 %collective-permute-start.7 = (bf16[8,64,128]{2,1,0:T(8,128)(2,1)S(1)}, bf16[8,64,128]{2,1,0:T(8,128)(2,1)S(1)}, u32[]{:S(2)}, u32[]{:S(2)}) collective-permute-start(bf16[8,64,128]{2,1,0:T(8,128)(2,1)S(1)} %get-tuple-element.25), channel_id=1, source_target_pairs={{0,16},{8,24},{16,0},{24,8},{1,17},{9,25},{17,1},{25,9},{2,18},{10... | collective-permute-start | bytes 393224 | tf_op jit(solution)/shard_map/ppermute | solution.py:35
  38.1 10.3 %collective-permute-start.9 = (bf16[8,64,128]{2,1,0:T(8,128)(2,1)S(1)}, bf16[8,64,128]{2,1,0:T(8,128)(2,1)S(1)}, u32[]{:S(2)}, u32[]{:S(2)}) collective-permute-start(bf16[8,64,128]{2,1,0:T(8,128)(2,1)S(1)} %get-tuple-element.27), channel_id=1, source_target_pairs={{0,24},{8,16},{16,8},{24,0},{1,25},{9,17},{17,9},{25,1},{2,26},{10... | collective-permute-start | bytes 393224 | tf_op jit(solution)/shard_map/ppermute | solution.py:35
  49.6 1.3 %collective-permute-start.10 = (bf16[64,384]{1,0:T(8,128)(2,1)S(1)}, bf16[64,384]{1,0:T(8,128)(2,1)S(1)}, u32[]{:S(2)}, u32[]{:S(2)}) collective-permute-start(bf16[64,384]{1,0:T(8,128)(2,1)S(1)} %convert_element_type.49), channel_id=1, source_target_pairs={{0,1},{1,0},{2,3},{3,2},{4,5},{5,4},{6,7},{7,6},{8,9},{9,8},{10,11... | collective-permute-start | bytes 147464 | tf_op jit(solution)/shard_map/ppermute | solution.py:35
  50.9 5.2 %collective-permute-start.13 = (bf16[64,384]{1,0:T(8,128)(2,1)S(1)}, bf16[64,384]{1,0:T(8,128)(2,1)S(1)}, u32[]{:S(2)}, u32[]{:S(2)}) collective-permute-start(bf16[64,384]{1,0:T(8,128)(2,1)S(1)} %fusion), channel_id=1, source_target_pairs={{0,6},{1,7},{2,4},{3,5},{4,2},{5,3},{6,0},{7,1},{8,14},{9,15},{10,... | collective-permute-start | bytes 147464 | tf_op jit(solution)/shard_map/ppermute | solution.py:35
  52.7 4.1 %collective-permute-start.12 = (bf16[64,384]{1,0:T(8,128)(2,1)S(1)}, bf16[64,384]{1,0:T(8,128)(2,1)S(1)}, u32[]{:S(2)}, u32[]{:S(2)}) collective-permute-start(bf16[64,384]{1,0:T(8,128)(2,1)S(1)} %fusion), channel_id=1, source_target_pairs={{0,4},{1,5},{2,6},{3,7},{4,0},{5,1},{6,2},{7,3},{8,12},{9,13},{10,... | collective-permute-start | bytes 147464 | tf_op jit(solution)/shard_map/ppermute | solution.py:35
  52.7 4.1 %collective-permute-start.11 = (bf16[64,384]{1,0:T(8,128)(2,1)S(1)}, bf16[64,384]{1,0:T(8,128)(2,1)S(1)}, u32[]{:S(2)}, u32[]{:S(2)}) collective-permute-start(bf16[64,384]{1,0:T(8,128)(2,1)S(1)} %fusion), channel_id=1, source_target_pairs={{0,2},{1,3},{2,0},{3,1},{4,6},{5,7},{6,4},{7,5},{8,10},{9,11},{10,... | collective-permute-start | bytes 147464 | tf_op jit(solution)/shard_map/ppermute | solution.py:35
  56.9 6.1 %collective-permute-start.16 = (bf16[64,384]{1,0:T(8,128)(2,1)S(1)}, bf16[64,384]{1,0:T(8,128)(2,1)S(1)}, u32[]{:S(2)}, u32[]{:S(2)}) collective-permute-start(bf16[64,384]{1,0:T(8,128)(2,1)S(1)} %fusion.5), channel_id=1, source_target_pairs={{0,24},{8,16},{16,8},{24,0},{1,25},{9,17},{17,9},{25,1},{2,26},{10... | collective-permute-start | bytes 147464 | tf_op jit(solution)/shard_map/ppermute | solution.py:35
  59.4 5.3 %collective-permute-start.15 = (bf16[64,384]{1,0:T(8,128)(2,1)S(1)}, bf16[64,384]{1,0:T(8,128)(2,1)S(1)}, u32[]{:S(2)}, u32[]{:S(2)}) collective-permute-start(bf16[64,384]{1,0:T(8,128)(2,1)S(1)} %fusion.5), channel_id=1, source_target_pairs={{0,16},{8,24},{16,0},{24,8},{1,17},{9,25},{17,1},{25,9},{2,18},{10... | collective-permute-start | bytes 147464 | tf_op jit(solution)/shard_map/ppermute | solution.py:35
  61.7 4.1 %collective-permute-start.14 = (bf16[64,384]{1,0:T(8,128)(2,1)S(1)}, bf16[64,384]{1,0:T(8,128)(2,1)S(1)}, u32[]{:S(2)}, u32[]{:S(2)}) collective-permute-start(bf16[64,384]{1,0:T(8,128)(2,1)S(1)} %fusion.5), channel_id=1, source_target_pairs={{0,8},{8,0},{16,24},{24,16},{1,9},{9,1},{17,25},{25,17},{2,10},{10... | collective-permute-start | bytes 147464 | tf_op jit(solution)/shard_map/ppermute | solution.py:35
  65.8 1.4 %collective-permute-start.17 = (f32[64,384]{1,0:T(8,128)S(1)}, f32[64,384]{1,0:T(8,128)S(1)}, u32[]{:S(2)}, u32[]{:S(2)}) collective-permute-start(f32[64,384]{1,0:T(8,128)S(1)} %add_multiply_fusion.mine_ref), channel_id=1, source_target_pairs={{0,1},{1,0},{2,3},{3,2},{4,5},{5,4},{6,7},{7,6},{8,9},{9,8},{10,11... | collective-permute-start | bytes 294920 | tf_op jit(solution)/shard_map/ppermute | solution.py:35
  72.8 7.6 %collective-permute-start.18 = (bf16[2,32,1,8,128]{4,3,2,1,0:T(8,128)(2,1)S(1)}, bf16[2,32,1,8,128]{4,3,2,1,0:T(8,128)(2,1)S(1)}, u32[]{:S(2)}, u32[]{:S(2)}) collective-permute-start(bf16[2,32,1,8,128]{4,3,2,1,0:T(8,128)(2,1)S(1)} %get-tuple-element.31), channel_id=1, source_target_pairs={{0,8},{8,0},{16,24},{24,16},{1,9},{9,1},{17,25},{25,17},{2,10},{10... | collective-permute-start | bytes 393224 | tf_op jit(solution)/shard_map/ppermute | solution.py:35
  73.9 12.9 %collective-permute-start.19 = (bf16[2,32,1,8,128]{4,3,2,1,0:T(8,128)(2,1)S(1)}, bf16[2,32,1,8,128]{4,3,2,1,0:T(8,128)(2,1)S(1)}, u32[]{:S(2)}, u32[]{:S(2)}) collective-permute-start(bf16[2,32,1,8,128]{4,3,2,1,0:T(8,128)(2,1)S(1)} %get-tuple-element.32), channel_id=1, source_target_pairs={{0,16},{8,24},{16,0},{24,8},{1,17},{9,25},{17,1},{25,9},{2,18},{10... | collective-permute-start | bytes 393224 | tf_op jit(solution)/shard_map/ppermute | solution.py:35
  75.9 10.9 %collective-permute-start.20 = (bf16[2,32,1,8,128]{4,3,2,1,0:T(8,128)(2,1)S(1)}, bf16[2,32,1,8,128]{4,3,2,1,0:T(8,128)(2,1)S(1)}, u32[]{:S(2)}, u32[]{:S(2)}) collective-permute-start(bf16[2,32,1,8,128]{4,3,2,1,0:T(8,128)(2,1)S(1)} %get-tuple-element.33), channel_id=1, source_target_pairs={{0,24},{8,16},{16,8},{24,0},{1,25},{9,17},{17,9},{25,1},{2,26},{10... | collective-permute-start | bytes 393224 | tf_op jit(solution)/shard_map/ppermute | solution.py:35
  (1 other events, 0.7 us)
